TPU v7x, 512 devices: a whole 4x8x8 slice. The times are simulated.
512 devices in a mesh: bl: 64 (over x, z, core), ch: 8 (over y).
Axes of the slice: x: 4, y: 8, z: 8, core: 2. Of those that a mesh axis runs over, the one named last changes fastest.
Arguments:
- model_grid: bfloat16 [8, 8192, 1024], P('ch', 'bl'), may hold values from -6 to 6
- screens: float32 [64, 8, 1024], P('bl'), may hold values from -3 to 3
- observed: float32 [8, 16, 16, 1024], P(None, None, 'ch', 'bl'), may hold values from -6 to 6
- uv_coords: float32 [2, 16, 1024], P(None, None, 'bl'), may hold values from -10 to 10
- station_pairs: int32 [1024, 2], P('bl'), may hold values from 0 to 63, as said below
- tile_owner: int32 [1024, 1], P('bl'), may hold values from 0 to 63; in each aligned block of 16 rows (0 to 15, 16 to 31, ...) at most 2 rows name the same one
- tile_slot: int32 [1024], P('bl'), may hold values from 0 to 127
Outputs:
- residual: float32 [8, 16, 16, 1024], P(None, None, 'ch', 'bl')
- screen_grad: float32 [64, 8, 1024], P('bl')
Inputs may be any that keep to these rules, and one draw needn't show every extreme that they name: `station_pairs`: the two stations of a baseline differ. `tile_owner`: among the rows of one device at most 2 name the same holder, and in some blocks one holder is named by exactly 2.
All inputs are finite; a program needn't handle non-finite values.
Results may differ from a plain program's by a relative error of at most 0.0003.
Values may be sent and summed in bfloat16 or wider, within the bound.
No kernel may reach another device: no remote copies, remote signals or barrier semaphores. Data moves between devices by JAX's collectives and lax.ppermute only.
A program may use at most 64 MiB of HBM per device.

v0:
```python
import math

import jax
import jax.numpy as jnp
from jax import lax
from jax.sharding import PartitionSpec as P

highest = lax.Precision.HIGHEST


def dft_tables(side_cells):
    counter = jnp.arange(side_cells, dtype=jnp.int32)
    product = counter[:, None] * counter[None, :] % side_cells
    angles = product.astype(jnp.float32) * (2.0 * math.pi / side_cells)
    return (jnp.cos(angles), jnp.sin(angles))


def to_image(uv_block):
    side_cells = uv_block.shape[1]
    cosine_table, sine_table = dft_tables(side_cells)
    real_part = uv_block[:4]
    imag_part = uv_block[4:]

    def along_cols(values, lookup):
        return jnp.einsum("pjkb,lk->pjlb", values, lookup, precision=highest)

    def along_rows(values, lookup):
        return jnp.einsum("ij,pjlb->pilb", lookup, values, precision=highest)

    inner_real = along_cols(real_part, cosine_table) - along_cols(imag_part, sine_table)
    inner_imag = along_cols(real_part, sine_table) + along_cols(imag_part, cosine_table)
    outer_real = along_rows(inner_real, cosine_table) - along_rows(inner_imag, sine_table)
    outer_imag = along_rows(inner_imag, cosine_table) + along_rows(inner_real, sine_table)
    return jnp.concatenate([outer_real, outer_imag], axis=0) / side_cells


def complex_mul(left_pair, right_pair):
    return (
        left_pair[0] * right_pair[0] - left_pair[1] * right_pair[1],
        left_pair[0] * right_pair[1] + left_pair[1] * right_pair[0],
    )


def complex_add(left_pair, right_pair):
    return (left_pair[0] + right_pair[0], left_pair[1] + right_pair[1])


def conjugate(pair_value):
    return (pair_value[0], -pair_value[1])


def as_matrix(stacked):
    return [
        [(stacked[0], stacked[4]), (stacked[1], stacked[5])],
        [(stacked[2], stacked[6]), (stacked[3], stacked[7])],
    ]


def jones_product(screen_one, image_block, screen_two):
    jones_one = as_matrix(screen_one)
    sky_image = as_matrix(image_block)
    jones_two = as_matrix(screen_two)
    middle = [
        [
            complex_add(
                complex_mul(jones_one[row_index][0], sky_image[0][col_index]),
                complex_mul(jones_one[row_index][1], sky_image[1][col_index]),
            )
            for col_index in range(2)
        ]
        for row_index in range(2)
    ]
    result = [
        [
            complex_add(
                complex_mul(middle[row_index][0], conjugate(jones_two[col_index][0])),
                complex_mul(middle[row_index][1], conjugate(jones_two[col_index][1])),
            )
            for col_index in range(2)
        ]
        for row_index in range(2)
    ]
    real_parts = [
        result[row_index][col_index][0] for row_index in range(2) for col_index in range(2)
    ]
    imag_parts = [
        result[row_index][col_index][1] for row_index in range(2) for col_index in range(2)
    ]
    return jnp.stack(real_parts + imag_parts, axis=0)


def visibilities(model_block, uv_block, freq_scale):
    side_cells = model_block.shape[1]
    offsets = (jnp.arange(side_cells, dtype=jnp.float32) - side_cells // 2) / side_cells
    factor = 2.0 * math.pi * freq_scale
    angle_rows = (
        factor[None, :, None, None] * uv_block[0][:, None, None, :] * offsets[None, None, :, None]
    )
    angle_cols = (
        factor[None, :, None, None] * uv_block[1][:, None, None, :] * offsets[None, None, :, None]
    )
    cos_rows = jnp.cos(angle_rows)
    sin_rows = jnp.sin(angle_rows)
    cos_cols = jnp.cos(angle_cols)
    sin_cols = jnp.sin(angle_cols)
    real_part = model_block[:4]
    imag_part = model_block[4:]

    def over_cols(lookup, values):
        return jnp.einsum("tcmb,plmb->ptclb", lookup, values, precision=highest)

    sum_real = over_cols(cos_cols, real_part) + over_cols(sin_cols, imag_part)
    sum_imag = over_cols(cos_cols, imag_part) - over_cols(sin_cols, real_part)
    vis_real = jnp.sum(cos_rows[None] * sum_real + sin_rows[None] * sum_imag, axis=3)
    vis_imag = jnp.sum(cos_rows[None] * sum_imag - sin_rows[None] * sum_real, axis=3)
    return jnp.concatenate([vis_real, vis_imag], axis=0) / side_cells


def predict(screen_one, screen_two, image_block, uv_block, freq_scale):
    return visibilities(jones_product(screen_one, image_block, screen_two), uv_block, freq_scale)


def per_device(model_grid, screens, observed, uv_coords, station_pairs, tile_owner, tile_slot):
    owners = lax.axis_size("bl")
    bl_local = tile_slot.shape[0]
    stat_local = screens.shape[0]
    comps = screens.shape[1]
    pixels = model_grid.shape[2]
    side_cells = math.isqrt(pixels)
    capacity = max(2, 3 * bl_local // owners)
    owner_ids = tile_owner[:, 0]
    owner_hits = (owner_ids[:, None] == jnp.arange(owners, dtype=jnp.int32)[None, :]).astype(
        jnp.int32
    )
    earlier = jnp.cumsum(owner_hits, axis=0) - owner_hits
    rank_ids = jnp.sum(earlier * owner_hits, axis=1)
    positions = owner_ids * capacity + rank_ids
    slot_ids = jnp.arange(owners * capacity, dtype=jnp.int32)
    placed = positions[:, None] == slot_ids[None, :]
    requests = jnp.sum(jnp.where(placed, tile_slot[:, None] + 1, 0), axis=0) - 1
    requests = requests.reshape(owners, capacity)
    received = lax.all_to_all(requests, "bl", split_axis=0, concat_axis=0, tiled=True)
    is_valid = received >= 0
    wanted = jnp.maximum(received, 0).reshape(-1)
    tiles_out = jnp.take(model_grid, wanted, axis=1)
    tiles_out = tiles_out.reshape(model_grid.shape[0], received.shape[0], received.shape[1], pixels)
    tiles_out = jnp.where(is_valid[None, :, :, None], tiles_out, jnp.zeros((), model_grid.dtype))
    fetched = lax.all_to_all(tiles_out, "bl", split_axis=1, concat_axis=1, tiled=True)
    fetched = fetched.reshape(fetched.shape[0], owners * capacity, pixels)
    own_tiles = jnp.take(fetched, positions, axis=1)
    all_planes = lax.all_gather(own_tiles, "ch", axis=0, tiled=True)
    planes = all_planes.shape[0]
    uv_tiles = jnp.transpose(all_planes.astype(jnp.float32), (0, 2, 1))
    image_block = to_image(uv_tiles.reshape(planes, side_cells, side_cells, bl_local))
    pair_one = station_pairs[:, 0]
    pair_two = station_pairs[:, 1]
    shard_rows = lax.all_gather(screens, "bl", axis=0, tiled=True)
    rows_here = jnp.arange(shard_rows.shape[0], dtype=jnp.int32)
    pick_one = (rows_here[:, None] == pair_one[None, :]).astype(jnp.float32)
    pick_two = (rows_here[:, None] == pair_two[None, :]).astype(jnp.float32)
    screen_one = jnp.einsum("scx,sb->cxb", shard_rows, pick_one, precision=highest)
    screen_two = jnp.einsum("scx,sb->cxb", shard_rows, pick_two, precision=highest)
    grid_shape = (comps, side_cells, side_cells, bl_local)
    ch_local = observed.shape[2]
    chans_all = ch_local * lax.axis_size("ch")
    channel_ids = lax.axis_index("ch") * ch_local + jnp.arange(ch_local, dtype=jnp.int32)
    freq_scale = 1.0 + channel_ids.astype(jnp.float32) / (2.0 * chans_all)
    times_count = observed.shape[1]
    grad_scale = side_cells / math.sqrt(2.0 * bl_local * chans_all * times_count / stat_local)

    def forward(one_block_screen, two_block_screen):
        return predict(one_block_screen, two_block_screen, image_block, uv_coords, freq_scale)

    predicted, pullback = jax.vjp(
        forward, screen_one.reshape(grid_shape), screen_two.reshape(grid_shape)
    )
    residual = predicted - observed
    grad_one, grad_two = pullback(residual * grad_scale)
    grad_one = grad_one.reshape(comps, pixels, bl_local)
    grad_two = grad_two.reshape(comps, pixels, bl_local)
    rows_here = jnp.arange(stat_local * owners, dtype=jnp.int32)
    pick_one = (rows_here[:, None] == pair_one[None, :]).astype(jnp.float32)
    pick_two = (rows_here[:, None] == pair_two[None, :]).astype(jnp.float32)
    whole_terms = jnp.einsum("sb,cxb->scx", pick_one, grad_one, precision=highest) + jnp.einsum(
        "sb,cxb->scx", pick_two, grad_two, precision=highest
    )
    summed = lax.psum(whole_terms, "ch")
    screen_grad = lax.psum_scatter(summed, "bl", scatter_dimension=0, tiled=True)
    return (residual, screen_grad)


def solution(mesh):
    in_specs = (
        P("ch", "bl", None),
        P("bl", None, None),
        P(None, None, "ch", "bl"),
        P(None, None, "bl"),
        P("bl", None),
        P("bl", None),
        P("bl"),
    )
    out_specs = (P(None, None, "ch", "bl"), P("bl", None, None))
    return jax.shard_map(
        per_device, mesh=mesh, in_specs=in_specs, out_specs=out_specs, check_vma=False
    )
```

profile of v0, /device:TPU:4, one launch (start us, length us, event | category | flops | bytes accessed | tf_op | source)
XLA Modules:
  0.0 383.0 jit_solution(12689524988764223606)
XLA Ops:
  11.0 13.9 %all-to-all-start = ((s32[64,1,2]{2,1,0:T(1,128)}), s32[64,1,2]{2,1,0:T(1,128)S(1)}, u32[]{:S(2)}, u32[]{:S(2)}) async-start(s32[64,1,2]{2,1,0:T(1,128)} %bitcast.10), calls=%async_computation | async-start | bytes 65536 | tf_op jit(solution)/shard_map/all_to_all | solution.py:142
  28.7 3.9 %all-to-all-done = s32[64,1,2]{2,1,0:T(1,128)S(1)} async-done(((s32[64,1,2]{2,1,0:T(1,128)}), s32[64,1,2]{2,1,0:T(1,128)S(1)}, u32[]{:S(2)}, u32[]{:S(2)}) %all-to-all-start) | async-done | bytes 544 | tf_op jit(solution)/shard_map/all_to_all | solution.py:142
  35.3 6.5 %all-to-all-start.1 = ((bf16[1,64,2,1024]{3,2,0,1:T(2,128)(2,1)}), bf16[1,64,2,1024]{3,2,0,1:T(2,128)(2,1)S(1)}, u32[]{:S(2)}, u32[]{:S(2)}) async-start(bf16[1,64,2,1024]{3,2,0,1:T(2,128)(2,1)} %broadcast_select_fusion.1), calls=%async_computation.1 | async-start | bytes 524288 | tf_op jit(solution)/shard_map/all_to_all | solution.py:148
  45.6 7.9 %all-to-all-done.1 = bf16[1,64,2,1024]{3,2,0,1:T(2,128)(2,1)S(1)} async-done(((bf16[1,64,2,1024]{3,2,0,1:T(2,128)(2,1)}), bf16[1,64,2,1024]{3,2,0,1:T(2,128)(2,1)S(1)}, u32[]{:S(2)}, u32[]{:S(2)}) %all-to-all-start.1) | async-done | bytes 262176 | tf_op jit(solution)/shard_map/all_to_all | solution.py:148
  54.3 26.6 %all_gather.7 = bf16[8,16,1024]{2,1,0:T(8,128)(2,1)S(1)} all-gather(bf16[1,16,1024]{2,1,0:T(8,128)(2,1)S(1)} %bitcast_select_fusion), channel_id=1, replica_groups=mesh['bl'=64,'ch'=8] {'ch'}, dimensions={0}, use_global_device_ids=true | all-gather | bytes 294912 | tf_op jit(solution)/shard_map/all_gather | solution.py:151
  81.7 2.5 fusion.74
  84.1 2.5 fusion.78
  86.6 2.5 fusion.9
  90.1 2.5 fusion.8
  96.0 16.7 %all-gather.2.cloned.1.call-done = f32[64,8,1024]{2,1,0:T(8,128)} async-done(((f32[1,8,1024]{2,1,0:T(8,128)}), f32[64,8,1024]{2,1,0:T(8,128)}) %all-gather.2.cloned.1.call-update) | async-done | bytes 2097168 | tf_op jit(solution)/shard_map/all_gather | solution.py:157
  112.8 3.5 fusion.17
  119.0 3.5 fusion.14
  154.9 2.0 fusion.26
  156.9 2.0 fusion.22
  158.9 2.4 fusion.7
  161.4 2.7 add_reduce_fusion
  167.8 1.9 convolution_bitcast_fusion
  169.7 1.9 fusion.11
  171.7 2.1 fusion.13
  180.4 2.9 copy.457
  183.4 2.5 reshape.432
  195.2 2.6 copy.458
  199.5 145.5 %reduce-scatter.2.cloned.1.call-done = f32[1,8,1024]{2,1,0:T(8,128)} async-done(((f32[64,8,1024]{2,1,0:T(8,128)}), f32[1,8,1024]{2,1,0:T(8,128)}) %reduce-scatter.2.cloned.1.call-update) | async-done | bytes 32784 | tf_op jit(solution)/shard_map/reduce_scatter | solution.py:188
  344.9 31.0 %psum.8 = f32[1,8,1024]{2,1,0:T(8,128)} all-reduce(f32[1,8,1024]{2,1,0:T(8,128)} %reduce-scatter.2.cloned.1.call-done), channel_id=1, replica_groups=mesh['bl'=64,'ch'=8] {'ch'}, use_global_device_ids=true, to_apply=%region_5.6 | all-reduce | flops 8192 | bytes 65536 | tf_op jit(solution)/shard_map/psum | solution.py:187
  (162 shorter events, 76.2 us)
Async XLA Ops:
  7.2 26.0 %copy-start = (bf16[1,128,1024]{2,1,0:T(8,128)(2,1)S(1)}, bf16[1,128,1024]{2,1,0:T(8,128)(2,1)}, u32[]{:S(2)}) copy-start(bf16[1,128,1024]{2,1,0:T(8,128)(2,1)} %param.7) | copy-start | bytes 786436
  11.0 21.6 %all-to-all-start = ((s32[64,1,2]{2,1,0:T(1,128)}), s32[64,1,2]{2,1,0:T(1,128)S(1)}, u32[]{:S(2)}, u32[]{:S(2)}) async-start(s32[64,1,2]{2,1,0:T(1,128)} %bitcast.10), calls=%async_computation | async-start | bytes 65536 | tf_op jit(solution)/shard_map/all_to_all | solution.py:142
  24.9 87.8 %all-gather.2.cloned.1.call-start = ((), (), s32[]{:S(2)}) async-start(), calls=%async_computation.3 | async-start | bytes 2129920 | tf_op jit(solution)/shard_map/all_gather | solution.py:157
  27.6 85.2 %copy-start.26 = (s32[16]{0:T(128)}, s32[16]{0:T(128)S(1)}, u32[]{:S(2)}) copy-start(s32[16]{0:T(128)S(1)} %get-tuple-element.104) | copy-start | bytes 196
  28.4 13.4 %copy-start.23 = (f32[8,16,2,16]{3,2,1,0:T(2,128)S(1)}, f32[8,16,2,16]{3,2,1,0:T(2,128)}, u32[]{:S(2)}) copy-start(f32[8,16,2,16]{3,2,1,0:T(2,128)} %param.9) | copy-start | bytes 49156
  35.3 18.2 %all-to-all-start.1 = ((bf16[1,64,2,1024]{3,2,0,1:T(2,128)(2,1)}), bf16[1,64,2,1024]{3,2,0,1:T(2,128)(2,1)S(1)}, u32[]{:S(2)}, u32[]{:S(2)}) async-start(bf16[1,64,2,1024]{3,2,0,1:T(2,128)(2,1)} %broadcast_select_fusion.1), calls=%async_computation.1 | async-start | bytes 524288 | tf_op jit(solution)/shard_map/all_to_all | solution.py:148
  41.8 303.2 %reduce-scatter.2.cloned.1.call-start = ((), (), s32[]{:S(2)}) async-start(), calls=%async_computation.4 | async-start | bytes 2129920 | tf_op jit(solution)/shard_map/reduce_scatter | solution.py:188
  41.9 3.8 copy-start.24
  150.8 1.8 copy-start.11
  150.8 1.8 copy-start.12
  150.8 1.8 copy-start.13
  150.8 1.8 copy-start.14
  158.9 2.5 copy-start.5
  158.9 2.5 copy-start.6
  161.3 3.6 copy-start.9
  161.3 3.6 copy-start.10
  183.4 2.6 copy-start.15
  183.4 2.6 copy-start.16
  183.4 2.6 copy-start.17
  185.9 1.5 copy-start.18
  185.9 1.5 copy-start.19
  185.9 1.5 copy-start.20
  192.0 2.1 copy-start.27
  195.2 180.8 %copy-start.1 = (bf16[1,128,1024]{2,1,0:T(8,128)(2,1)S(1)}, bf16[1,128,1024]{2,1,0:T(8,128)(2,1)}, u32[]{:S(2)}) copy-start(bf16[1,128,1024]{2,1,0:T(8,128)(2,1)} %param.7) | copy-start | bytes 786436
  (9 other events, 9.1 us)
Sparse Core Ops, SparseCore 0:
  29.1 83.5 all-gather.1
  197.9 146.9 reduce-scatter.1
where the time goes:
time: 388 us; the launch traced here: 383 us
  waiting for transfers between devices  175 us (45%)
  blocking collectives  57.6 us (15%)
  local copies, waits for them, and re-layouts  51.1 us (13%)
  matrix products  40.3 us (10%)
  other arithmetic  23.9 us (6%)
  starting transfers between devices  20.5 us (5%)
  between operations  14.9 us (4%)
    reduce_scatter x1, waiting for transfers between devices, per_device(): lax.psum_scatter(summed, 'bl', scatter_dimension=0, tiled=True)  145 us
    psum x1, blocking collectives, per_device(): summed = lax.psum(whole_terms, 'ch')  31 us
    all_gather x1, blocking collectives, per_device(): all_planes = lax.all_gather(own_tiles, 'ch', axis=0, tiled=True)  26.6 us
    dot_general x8, matrix products, over_cols(): return jnp.einsum('tcmb,plmb->ptclb', lookup, values, precision=highest)  17 us
    all_gather x1, waiting for transfers between devices, per_device(): shard_rows = lax.all_gather(screens, 'bl', axis=0, tiled=True)  16.7 us
    all_to_all x1, starting transfers between devices, per_device(): lax.all_to_all(requests, 'bl', split_axis=0, concat_axis=0, tiled=True)  13.9 us
    dot_general x4, matrix products, along_cols(): return jnp.einsum('pjkb,lk->pjlb', values, lookup, precision=highest)  9.86 us
    all_to_all x1, waiting for transfers between devices, per_device(): lax.all_to_all(tiles_out, 'bl', split_axis=1, concat_axis=1, tiled=True)  7.91 us
  transfers between devices with their start and end apart: 4, of which 4 were waited for; matrix products, arithmetic and copies ran while one was open for 7% of the time, Pallas kernels for 0%

commit v1 on v0

v1 whole, which is shorter than its diff:
```python
import math

import jax
import jax.numpy as jnp
import numpy as np
from jax import lax
from jax.experimental import pallas as pl
from jax.experimental.pallas import tpu as pltpu
from jax.sharding import PartitionSpec as P

SUB = 32
PIX = 1024
TIMES = 16
CHANS = 16
NBL = 64
NCH = 8
BLD = 16
TILES = 128
SAMPLES = TIMES * CHANS
MSG1 = 9
MSG3 = 56
MSG5 = 40
f32 = jnp.float32
bf16 = jnp.bfloat16
highest = lax.Precision.HIGHEST
GRAD_SCALE = SUB / math.sqrt(2.0 * BLD * NBL * CHANS * TIMES / NBL)


def vmem(n):
    return [pl.BlockSpec(memory_space=pltpu.VMEM)] * n


def smem(n):
    return [pl.BlockSpec(memory_space=pltpu.SMEM)] * n


params = pltpu.CompilerParams(vmem_limit_bytes=32 * 1024 * 1024)


def row_order():
    q, s = np.divmod(np.arange(SUB), 8)
    return 4 * s + q


def tables():
    j = np.arange(SUB)
    ang = (np.outer(j, j) % SUB) * (2.0 * np.pi / SUB)
    c, s = np.cos(ang), np.sin(ang)
    eye = np.eye(4)
    cc, ss = np.kron(eye, c), np.kron(eye, s)
    cols = np.block([[cc, ss], [-ss, cc]])
    order = row_order()
    cp, sp = c[np.ix_(order, order)], s[np.ix_(order, order)]
    rows = np.block([[cp, -sp], [sp, cp]]) / SUB
    x = (np.arange(SUB) - SUB // 2) / SUB
    xl = np.tile(x[order], 4)
    xm = np.tile(x, 4)
    offs = np.zeros((8, 128))
    offs[0], offs[1] = xl, xm
    offs[2] = np.tile(np.repeat([0.0, 0.25], SUB), 2)
    return cols.astype(np.float32), rows.astype(np.float32), offs.astype(np.float32)


def split2(x):
    hi = x.astype(bf16)
    return hi, (x - hi.astype(f32)).astype(bf16)


def cos_turns(t):
    r = t - jnp.round(t)
    z = 0.25 - jnp.abs(r)
    w = z * z
    c = [(-1.0) ** k * (2.0 * math.pi) ** (2 * k + 1) / math.factorial(2 * k + 1) for k in range(8)]
    acc = jnp.full_like(w, c[7])
    for k in range(6, -1, -1):
        acc = acc * w + c[k]
    return acc * z


def send_requests(owner_ref, slot_ref, screen_ref, out_ref):
    c = lax.axis_index("ch")
    subs = lax.broadcasted_iota(jnp.int32, (8, 128), 0)
    mine = jnp.zeros((8, 128), f32)
    for j in range(8):
        picked = jnp.where(subs == c, screen_ref[0, :, j * 128 : (j + 1) * 128], 0.0)
        mine = jnp.where(subs == j, jnp.sum(picked, axis=0, keepdims=True), mine)
    rows = lax.broadcasted_iota(jnp.int32, (NBL, 128), 0)
    lanes = lax.broadcasted_iota(jnp.int32, (NBL, 128), 1)
    count = jnp.zeros((NBL, 128), jnp.int32)
    req = jnp.zeros((NBL, 128), jnp.int32)
    for i in range(BLD):
        hit = rows == owner_ref[i, 0]
        req = jnp.where(hit & (lanes == count), slot_ref[i] + 1, req)
        count = count + hit.astype(jnp.int32)
    req = req.astype(f32)
    for s in range(NBL):
        out_ref[MSG1 * s : MSG1 * s + 8, :] = mine
        out_ref[MSG1 * s + 8 : MSG1 * s + 9, :] = req[s : s + 1]


def reply_tiles(msg_ref, grid_ref, out_ref, scr_ref):
    req = msg_ref[pl.ds(8, NBL, stride=MSG1), :]
    lanes = lax.broadcasted_iota(jnp.int32, (NBL, 128), 1).astype(f32) + 1.0
    grid = grid_ref[0]
    for k in range(2):
        pick = jnp.where(lanes == req[:, k : k + 1], 1.0, 0.0).astype(bf16)
        got = jnp.dot(pick, grid, preferred_element_type=f32)
        for j in range(8):
            scr_ref[pl.ds(k * 8 + j, NBL, stride=16), :] = got[:, j * 128 : (j + 1) * 128]
    out_ref[...] = scr_ref[...].reshape(NBL, 16, 128).astype(bf16)


def send_baselines(owner_ref, pair_ref, tiles_ref, msg_ref, seen_ref, out_ref):
    for i in range(BLD):
        d, a = divmod(i, 2)
        owner = owner_ref[i, 0]
        rank = jnp.int32(0)
        for e in range(i):
            rank = rank + (owner_ref[e, 0] == owner).astype(jnp.int32)
        both = tiles_ref[owner].astype(f32)
        out_ref[d, a * 8 : a * 8 + 8, :] = jnp.where(rank == 0, both[:8], both[8:])
        for e in range(2):
            at = 16 + (a * 2 + e) * 8
            out_ref[d, at : at + 8, :] = msg_ref[pl.ds(MSG1 * pair_ref[i, e], 8), :]
    out_ref[:, 48:56, :] = seen_ref[...]


def blocks_swap(four):
    lane = lax.broadcasted_iota(jnp.int32, (8, 128), 1) // SUB
    out = []
    for q in range(4):
        acc = None
        for p in range(4):
            turn = (p - q) % 4 * SUB
            moved = four[p] if turn == 0 else pltpu.roll(four[p], turn, 1)
            acc = moved if acc is None else jnp.where(lane == p, moved, acc)
        out.append(acc)
    return out


def to_rows(four):
    return jnp.concatenate(blocks_swap(four), axis=0)


def to_flat(block):
    return blocks_swap([block[8 * q : 8 * q + 8] for q in range(4)])


def cmul(a, b):
    return a[0] * b[0] - a[1] * b[1], a[0] * b[1] + a[1] * b[0]


def cmulc(a, b):
    return a[0] * b[0] + a[1] * b[1], a[1] * b[0] - a[0] * b[1]


def cadd(a, b):
    return a[0] + b[0], a[1] + b[1]


def mat(get):
    return [[get(2 * r + c) for c in range(2)] for r in range(2)]


def prod(a, b):
    return [[cadd(cmul(a[r][0], b[0][c]), cmul(a[r][1], b[1][c])) for c in range(2)] for r in range(2)]


def prod_h(a, b):
    return [[cadd(cmulc(a[r][0], b[c][0]), cmulc(a[r][1], b[c][1])) for c in range(2)] for r in range(2)]


def h_prod(a, b):
    return [[cadd(cmulc(b[0][c], a[0][r]), cmulc(b[1][c], a[1][r])) for c in range(2)] for r in range(2)]


def calibrate(msg_ref, uv_ref, cols_ref, rows_ref, offs_ref, out_ref):
    mine = lax.axis_index("ch") * 2
    lane16 = lax.broadcasted_iota(jnp.int32, (TIMES, BLD), 1)
    lane128 = lax.broadcasted_iota(jnp.int32, (TIMES, 128), 1)

    def column(axis, a):
        picked = jnp.where(lane16 == mine + a, uv_ref[axis], 0.0)
        return jnp.broadcast_to(jnp.sum(picked, axis=1, keepdims=True), (TIMES, 128))

    def phases(base):
        return jnp.concatenate([base * (1.0 + c / (2.0 * CHANS)) for c in range(CHANS)], axis=0)

    u_both = jnp.where(lane128 < 64, column(0, 0), column(0, 1))
    e_row = cos_turns(phases(u_both * offs_ref[0:1, :]) - offs_ref[2:3, :])
    cos_col, sin_col = [], []
    for a in range(2):
        t = phases(column(1, a) * offs_ref[1:2, :])
        cos_col.append(cos_turns(t))
        sin_col.append(cos_turns(t - 0.25))

    planes = [[msg_ref[k, a * 8 : a * 8 + 8, :] for k in range(8)] for a in range(2)]
    grid_re = jnp.concatenate([to_rows(planes[a][:4]) for a in range(2)], axis=0)
    grid_im = jnp.concatenate([to_rows(planes[a][4:]) for a in range(2)], axis=0)
    grid = jnp.concatenate([grid_re, grid_im], axis=1)
    half = jnp.dot(grid, cols_ref[...], precision=highest, preferred_element_type=f32)
    stacked = jnp.concatenate(
        [
            jnp.concatenate([half[:32, :128], half[32:, :128]], axis=1),
            jnp.concatenate([half[:32, 128:], half[32:, 128:]], axis=1),
        ],
        axis=0,
    )
    image = jnp.dot(rows_ref[...], stacked, precision=highest, preferred_element_type=f32)

    lane_re = lax.broadcasted_iota(jnp.int32, (8, 256), 1) // SUB
    sub = lax.broadcasted_iota(jnp.int32, (8, 256), 0)
    ones = jnp.where(lane_re == sub, 1.0, 0.0).astype(bf16)
    zeros = jnp.zeros((64, 256), f32)

    for a in range(2):
        sky_re = to_flat(image[:32, a * 128 : a * 128 + 128])
        sky_im = to_flat(image[32:, a * 128 : a * 128 + 128])
        sky = mat(lambda p: (sky_re[p], sky_im[p]))

        def jones(e):
            at = 16 + (a * 2 + e) * 8
            return mat(lambda p: (msg_ref[p, at : at + 8, :], msg_ref[p + 4, at : at + 8, :]))

        first, second = jones(0), jones(1)
        middle = prod(first, sky)
        model = prod_h(middle, second)
        m_re = to_rows([model[p // 2][p % 2][0] for p in range(4)])
        m_im = to_rows([model[p // 2][p % 2][1] for p in range(4)])
        block = jnp.concatenate(
            [jnp.concatenate([m_re, m_im], axis=1), jnp.concatenate([m_im, -m_re], axis=1)], axis=0
        )
        block = jnp.concatenate([block, zeros] if a == 0 else [zeros, block], axis=0)
        t = jnp.dot(e_row, block, precision=highest, preferred_element_type=f32)
        t_re, t_im = t[:, :128], t[:, 128:]
        w = jnp.concatenate(
            [cos_col[a] * t_re + sin_col[a] * t_im, cos_col[a] * t_im - sin_col[a] * t_re], axis=1
        )
        w_hi, w_lo = split2(w)
        last = (((1,), (1,)), ((), ()))
        vis = lax.dot_general(ones, w_hi, last, preferred_element_type=f32)
        vis = vis + lax.dot_general(ones, w_lo, last, preferred_element_type=f32)
        seen = jnp.concatenate([msg_ref[k, 48:56, a * 32 : a * 32 + 32] for k in range(8)], axis=1)
        resid = vis * (1.0 / SUB) - seen
        for k in range(8):
            out_ref[k, 32:40, a * 32 : a * 32 + 32] = resid[:, k * 32 : k * 32 + 32]
        g = resid * (GRAD_SCALE / SUB)
        g_hi, g_lo = split2(g)
        g_mid = g_lo.astype(f32)
        g_pair = jnp.concatenate([g_hi.astype(f32), g_mid], axis=0).T.astype(bf16)
        wide = jnp.dot(g_pair, jnp.concatenate([ones, ones], axis=0), preferred_element_type=f32)
        g_re, g_im = wide[:, :128], wide[:, 128:]
        d_t = jnp.concatenate(
            [cos_col[a] * g_re - sin_col[a] * g_im, sin_col[a] * g_re + cos_col[a] * g_im], axis=1
        )
        first_dim = (((0,), (0,)), ((), ()))
        d_block = lax.dot_general(e_row, d_t, first_dim, precision=highest, preferred_element_type=f32)
        d_block = d_block[a * 64 : a * 64 + 64]
        d_re = to_flat(d_block[:32, :128] - d_block[32:, 128:])
        d_im = to_flat(d_block[:32, 128:] + d_block[32:, :128])
        down = mat(lambda p: (d_re[p], d_im[p]))
        grads = [prod_h(prod(down, second), sky), h_prod(down, middle)]
        for e in range(2):
            at = (a * 2 + e) * 8
            for p in range(4):
                re, im = grads[e][p // 2][p % 2]
                out_ref[p, at : at + 8, :] = re
                out_ref[p + 4, at : at + 8, :] = im
    out_ref[:, 32:40, 64:] = jnp.zeros((8, 8, 64), f32)


def sum_terms(pair_ref, msg_ref, out_ref):
    out_ref[...] = jnp.zeros_like(out_ref)
    for i in range(BLD):
        d, a = divmod(i, 2)
        for e in range(2):
            s = pair_ref[i, e]
            at = (a * 2 + e) * 8
            out_ref[s] = out_ref[s] + msg_ref[d, at : at + 8, :]


def sum_all(msg_ref, out_ref):
    total = jnp.sum(msg_ref[...], axis=0)
    for k in range(NCH):
        out_ref[k] = total


def per_device(model_grid, screens, observed, uv_coords, station_pairs, tile_owner, tile_slot):
    cols, rows, offs = tables()
    sds = jax.ShapeDtypeStruct

    msg1 = pl.pallas_call(
        send_requests,
        out_shape=sds((NBL * MSG1, 128), f32),
        in_specs=smem(2) + vmem(1),
        out_specs=vmem(1)[0],
        compiler_params=params,
        name="send_requests",
    )(tile_owner, tile_slot, screens)
    got1 = lax.all_to_all(msg1, "bl", 0, 0, tiled=True)

    tiles = pl.pallas_call(
        reply_tiles,
        out_shape=sds((NBL, 16, 128), bf16),
        in_specs=vmem(2),
        out_specs=vmem(1)[0],
        scratch_shapes=[pltpu.VMEM((NBL * 16, 128), f32)],
        compiler_params=params,
        name="reply_tiles",
    )(got1, model_grid)
    got2 = lax.all_to_all(tiles, "bl", 0, 0, tiled=True)

    seen = observed.reshape(8, TIMES, 2, NCH, 2).transpose(3, 0, 4, 2, 1).reshape(NCH, 8, 64)
    seen = jnp.pad(seen, ((0, 0), (0, 0), (0, 64)))
    msg3 = pl.pallas_call(
        send_baselines,
        out_shape=sds((NCH, MSG3, 128), f32),
        in_specs=smem(2) + vmem(3),
        out_specs=vmem(1)[0],
        compiler_params=params,
        name="send_baselines",
    )(tile_owner, station_pairs, got2, got1, seen)
    got3 = lax.all_to_all(msg3, "ch", 0, 0, tiled=True)

    msg5 = pl.pallas_call(
        calibrate,
        out_shape=sds((NCH, MSG5, 128), f32),
        in_specs=vmem(5),
        out_specs=vmem(1)[0],
        compiler_params=params,
        name="calibrate",
    )(got3, uv_coords, cols, rows, offs)
    got5 = lax.all_to_all(msg5, "ch", 0, 0, tiled=True)

    resid = got5[:, 32:40, :64].reshape(NCH, 8, 2, 2, TIMES)
    residual = resid.transpose(1, 4, 3, 0, 2).reshape(8, TIMES, 2, BLD)

    msg6 = pl.pallas_call(
        sum_terms,
        out_shape=sds((NBL, 8, 128), f32),
        in_specs=smem(1) + vmem(1),
        out_specs=vmem(1)[0],
        compiler_params=params,
        name="sum_terms",
    )(station_pairs, got5)
    got6 = lax.all_to_all(msg6, "bl", 0, 0, tiled=True)

    msg7 = pl.pallas_call(
        sum_all,
        out_shape=sds((NCH, 8, 128), f32),
        in_specs=vmem(1),
        out_specs=vmem(1)[0],
        compiler_params=params,
        name="sum_all",
    )(got6)
    got7 = lax.all_to_all(msg7, "ch", 0, 0, tiled=True)
    return residual, got7.reshape(1, 8, PIX)


def solution(mesh):
    in_specs = (
        P("ch", "bl", None),
        P("bl", None, None),
        P(None, None, "ch", "bl"),
        P(None, None, "bl"),
        P("bl", None),
        P("bl", None),
        P("bl"),
    )
    out_specs = (P(None, None, "ch", "bl"), P("bl", None, None))
    return jax.shard_map(
        per_device, mesh=mesh, in_specs=in_specs, out_specs=out_specs, check_vma=False
    )
```

time: 388 us -> 120 us (0.31)
  the two profiles are of different devices: /device:TPU:4 before, /device:TPU:1 now
where the time goes in v1:
time: 120 us
  blocking collectives  79.9 us (67%)
  waiting for transfers between devices  17.3 us (14%)
  starting transfers between devices  9.75 us (8%)
  Pallas kernels  7.43 us (6%)
  local copies, waits for them, and re-layouts  4.54 us (4%)
    all_to_all x1, blocking collectives, per_device(): got1 = lax.all_to_all(msg1, 'bl', 0, 0, tiled=True)  32 us
    all_to_all x1, blocking collectives, per_device(): got6 = lax.all_to_all(msg6, 'bl', 0, 0, tiled=True)  20.4 us
    all_to_all x1, blocking collectives, per_device(): got3 = lax.all_to_all(msg3, 'ch', 0, 0, tiled=True)  16.8 us
    all_to_all x1, waiting for transfers between devices, per_device(): got2 = lax.all_to_all(tiles, 'bl', 0, 0, tiled=True)  11.5 us
    all_to_all x1, blocking collectives, per_device(): got5 = lax.all_to_all(msg5, 'ch', 0, 0, tiled=True)  10.8 us
    all_to_all x1, starting transfers between devices, per_device(): got2 = lax.all_to_all(tiles, 'bl', 0, 0, tiled=True)  6.41 us
    all_to_all x1, waiting for transfers between devices, per_device(): got7 = lax.all_to_all(msg7, 'ch', 0, 0, tiled=True)  5.84 us
    unnamed x22, local copies, waits for them, and re-layouts  3.42 us
  transfers between devices with their start and end apart: 2, of which 2 were waited for; matrix products, arithmetic and copies ran while one was open for 1% of the time, Pallas kernels for 0%

profile of v1, /device:TPU:1, one launch (start us, length us, event | category | flops | bytes accessed | tf_op | source)
XLA Modules:
  0.0 119.8 jit_solution(7419829841008659157)
XLA Ops:
  0.6 0.7 copy.21.owner_ref
  1.4 0.8 copy-done.3
  2.1 0.8 send_requests.1
  3.0 32.0 %all_to_all.36 = f32[64,9,128]{2,1,0:T(8,128)S(1)} all-to-all(f32[64,9,128]{2,1,0:T(8,128)S(1)} %all_to_all.22), channel_id=1, replica_groups=mesh['bl'=64,'ch'=8] {'bl'}, dimensions={0} | all-to-all | bytes 589824 | tf_op jit(solution)/shard_map/all_to_all | solution.py:300
  35.0 0.9 copy-done
  35.9 1.1 reply_tiles.1
  37.0 6.4 %all-to-all-start.1 = ((bf16[64,16,128]{2,1,0:T(8,128)(2,1)}), bf16[64,16,128]{2,1,0:T(8,128)(2,1)S(1)}, u32[]{:S(2)}, u32[]{:S(2)}) async-start(bf16[64,16,128]{2,1,0:T(8,128)(2,1)} %reply_tiles.1), calls=%async_computation.1 | async-start | bytes 524288 | tf_op jit(solution)/shard_map/all_to_all | solution.py:311
  43.4 0.1 copy.22.pair_ref
  43.5 0.1 copy.19
  43.6 0.1 copy.20
  43.7 0.2 reshape.22
  43.9 11.5 %all-to-all-done.1.tiles_ref = bf16[64,16,128]{2,1,0:T(8,128)(2,1)S(1)} async-done(((bf16[64,16,128]{2,1,0:T(8,128)(2,1)}), bf16[64,16,128]{2,1,0:T(8,128)(2,1)S(1)}, u32[]{:S(2)}, u32[]{:S(2)}) %all-to-all-start.1) | async-done | bytes 262176 | tf_op jit(solution)/shard_map/all_to_all | solution.py:311
  55.4 1.0 send_baselines.1
  56.4 16.8 %all_to_all.37.msg_ref = f32[8,56,128]{2,1,0:T(8,128)S(1)} all-to-all(f32[8,56,128]{2,1,0:T(8,128)S(1)} %send_baselines.1), channel_id=1, replica_groups=mesh['bl'=64,'ch'=8] {'ch'}, dimensions={0} | all-to-all | bytes 458752 | tf_op jit(solution)/shard_map/all_to_all | solution.py:323
  73.3 3.1 %calibrate.1 = f32[8,40,128]{2,1,0:T(8,128)S(1)} custom-call(f32[8,56,128]{2,1,0:T(8,128)S(1)} %all_to_all.37.msg_ref, f32[2,16,16]{2,1,0:T(8,128)S(1)} %copy-done.4, f32[256,256]{1,0:T(8,128)S(1)} %copy-done.1, f32[64,64]{1,0:T(8,128)S(1)} %copy-done.2, f32[8,128]{1,0:T(8,128)S(1)} %copy-done.5), custom_call_target="tpu_custom_call" | custom-call | tf_op jit(solution)/shard_map/calibrate/pallas_call | solution.py:325
  76.4 10.8 %all_to_all.38.msg_ref = f32[8,40,128]{2,1,0:T(8,128)S(1)} all-to-all(f32[8,40,128]{2,1,0:T(8,128)S(1)} %calibrate.1), channel_id=1, replica_groups=mesh['bl'=64,'ch'=8] {'ch'}, dimensions={0} | all-to-all | bytes 327680 | tf_op jit(solution)/shard_map/all_to_all | solution.py:333
  87.2 0.8 sum_terms.1
  87.9 20.4 %all_to_all.39.msg_ref = f32[64,8,128]{2,1,0:T(8,128)S(1)} all-to-all(f32[64,8,128]{2,1,0:T(8,128)S(1)} %sum_terms.1), channel_id=1, replica_groups=mesh['bl'=64,'ch'=8] {'bl'}, dimensions={0} | all-to-all | bytes 524288 | tf_op jit(solution)/shard_map/all_to_all | solution.py:346
  108.3 0.7 sum_all.1
  109.0 3.3 %all-to-all-start.5 = ((f32[8,8,128]{2,1,0:T(8,128)}), f32[8,8,128]{2,1,0:T(8,128)S(1)}, u32[]{:S(2)}, u32[]{:S(2)}) async-start(f32[8,8,128]{2,1,0:T(8,128)} %sum_all.1), calls=%async_computation.5 | async-start | bytes 65536 | tf_op jit(solution)/shard_map/all_to_all | solution.py:356
  112.4 0.1 reshape.23
  112.6 0.8 copy.25
  113.3 5.8 %all-to-all-done.5 = f32[8,8,128]{2,1,0:T(8,128)S(1)} async-done(((f32[8,8,128]{2,1,0:T(8,128)}), f32[8,8,128]{2,1,0:T(8,128)S(1)}, u32[]{:S(2)}, u32[]{:S(2)}) %all-to-all-start.5) | async-done | bytes 32800 | tf_op jit(solution)/shard_map/all_to_all | solution.py:356
  119.2 0.6 reshape.25
  (21 shorter events, 0.1 us)
Async XLA Ops:
  0.6 0.8 copy-start.6
  1.4 0.8 copy-start.3
  34.9 1.0 copy-start
  37.0 6.4 %copy-start.8 = (s32[16,2]{0,1:T(2,128)S(1)}, s32[16,2]{0,1:T(2,128)}, u32[]{:S(2)}) copy-start(s32[16,2]{0,1:T(2,128)} %param.14) | copy-start | bytes 388
  37.0 6.5 %copy-start.7 = (f32[8,16,2,16]{3,2,1,0:T(2,128)S(1)}, f32[8,16,2,16]{3,2,1,0:T(2,128)}, u32[]{:S(2)}) copy-start(f32[8,16,2,16]{3,2,1,0:T(2,128)} %param.12) | copy-start | bytes 49156
  37.0 18.4 %all-to-all-start.1 = ((bf16[64,16,128]{2,1,0:T(8,128)(2,1)}), bf16[64,16,128]{2,1,0:T(8,128)(2,1)S(1)}, u32[]{:S(2)}, u32[]{:S(2)}) async-start(bf16[64,16,128]{2,1,0:T(8,128)(2,1)} %reply_tiles.1), calls=%async_computation.1 | async-start | bytes 524288 | tf_op jit(solution)/shard_map/all_to_all | solution.py:311
  56.4 16.8 %copy-start.1 = (f32[256,256]{1,0:T(8,128)S(1)}, f32[256,256]{1,0:T(8,128)}, u32[]{:S(2)}) copy-start(f32[256,256]{1,0:T(8,128)} %constant.9.clone.cols_ref) | copy-start | bytes 786436
  56.4 16.8 %copy-start.2 = (f32[64,64]{1,0:T(8,128)S(1)}, f32[64,64]{1,0:T(8,128)}, u32[]{:S(2)}) copy-start(f32[64,64]{1,0:T(8,128)} %constant.10.clone.rows_ref) | copy-start | bytes 49156
  56.4 16.8 %copy-start.4 = (f32[2,16,16]{2,1,0:T(8,128)S(1)}, f32[2,16,16]{2,1,0:T(8,128)}, u32[]{:S(2)}) copy-start(f32[2,16,16]{2,1,0:T(8,128)} %uv_ref.1) | copy-start | bytes 6148
  56.4 16.8 %copy-start.5 = (f32[8,128]{1,0:T(8,128)S(1)}, f32[8,128]{1,0:T(8,128)}, u32[]{:S(2)}) copy-start(f32[8,128]{1,0:T(8,128)} %constant.11.clone.offs_ref) | copy-start | bytes 12292
  109.0 10.1 %all-to-all-start.5 = ((f32[8,8,128]{2,1,0:T(8,128)}), f32[8,8,128]{2,1,0:T(8,128)S(1)}, u32[]{:S(2)}, u32[]{:S(2)}) async-start(f32[8,8,128]{2,1,0:T(8,128)} %sum_all.1), calls=%async_computation.5 | async-start | bytes 65536 | tf_op jit(solution)/shard_map/all_to_all | solution.py:356

commit v2 on v1

--- a/solution.py
+++ b/solution.py
@@ -17,12 +17,11 @@
 BLD = 16
 TILES = 128
 SAMPLES = TIMES * CHANS
-MSG1 = 9
+MSG1 = PIX + 128
 MSG3 = 56
 MSG5 = 40
 f32 = jnp.float32
 bf16 = jnp.bfloat16
-highest = lax.Precision.HIGHEST
 GRAD_SCALE = SUB / math.sqrt(2.0 * BLD * NBL * CHANS * TIMES / NBL)
 
 
@@ -40,6 +39,11 @@
 def row_order():
     q, s = np.divmod(np.arange(SUB), 8)
     return 4 * s + q
+
+
+def np_split(x):
+    hi = x.astype(jnp.bfloat16)
+    return hi, (x - hi.astype(np.float32)).astype(jnp.bfloat16)
 
 
 def tables():
@@ -58,12 +62,21 @@
     offs = np.zeros((8, 128))
     offs[0], offs[1] = xl, xm
     offs[2] = np.tile(np.repeat([0.0, 0.25], SUB), 2)
-    return cols.astype(np.float32), rows.astype(np.float32), offs.astype(np.float32)
+    cols, rows = cols.astype(np.float32), rows.astype(np.float32)
+    return *np_split(cols), *np_split(rows), offs.astype(np.float32)
 
 
 def split2(x):
     hi = x.astype(bf16)
     return hi, (x - hi.astype(f32)).astype(bf16)
+
+
+def dot(a, b):
+    return jnp.dot(a, b, preferred_element_type=f32)
+
+
+def dot3(a_hi, a_lo, b_hi, b_lo):
+    return dot(a_hi, b_hi) + (dot(a_hi, b_lo) + dot(a_lo, b_hi))
 
 
 def cos_turns(t):
@@ -79,28 +92,23 @@
 
 def send_requests(owner_ref, slot_ref, screen_ref, out_ref):
     c = lax.axis_index("ch")
-    subs = lax.broadcasted_iota(jnp.int32, (8, 128), 0)
-    mine = jnp.zeros((8, 128), f32)
-    for j in range(8):
-        picked = jnp.where(subs == c, screen_ref[0, :, j * 128 : (j + 1) * 128], 0.0)
-        mine = jnp.where(subs == j, jnp.sum(picked, axis=0, keepdims=True), mine)
+    subs = lax.broadcasted_iota(jnp.int32, (8, PIX), 0)
+    mine = jnp.sum(jnp.where(subs == c, screen_ref[0], 0.0), axis=0, keepdims=True)
+    out_ref[:, :, :PIX] = jnp.broadcast_to(mine.reshape(1, 1, PIX), (NBL, 1, PIX))
     rows = lax.broadcasted_iota(jnp.int32, (NBL, 128), 0)
     lanes = lax.broadcasted_iota(jnp.int32, (NBL, 128), 1)
     count = jnp.zeros((NBL, 128), jnp.int32)
     req = jnp.zeros((NBL, 128), jnp.int32)
     for i in range(BLD):
-        hit = rows == owner_ref[i, 0]
+        hit = rows == owner_ref[i]
         req = jnp.where(hit & (lanes == count), slot_ref[i] + 1, req)
         count = count + hit.astype(jnp.int32)
-    req = req.astype(f32)
-    for s in range(NBL):
-        out_ref[MSG1 * s : MSG1 * s + 8, :] = mine
-        out_ref[MSG1 * s + 8 : MSG1 * s + 9, :] = req[s : s + 1]
+    out_ref[:, :, PIX:] = req.astype(f32).reshape(NBL, 1, 128)
 
 
 def reply_tiles(msg_ref, grid_ref, out_ref, scr_ref):
-    req = msg_ref[pl.ds(8, NBL, stride=MSG1), :]
-    lanes = lax.broadcasted_iota(jnp.int32, (NBL, 128), 1).astype(f32) + 1.0
+    req = msg_ref[:, :, PIX:].reshape(NBL, 128).astype(jnp.int32)
+    lanes = lax.broadcasted_iota(jnp.int32, (NBL, 128), 1) + 1
     grid = grid_ref[0]
     for k in range(2):
         pick = jnp.where(lanes == req[:, k : k + 1], 1.0, 0.0).astype(bf16)
@@ -110,18 +118,20 @@
     out_ref[...] = scr_ref[...].reshape(NBL, 16, 128).astype(bf16)
 
 
-def send_baselines(owner_ref, pair_ref, tiles_ref, msg_ref, seen_ref, out_ref):
+def send_baselines(owner_ref, pair_ref, tiles_ref, screens_ref, seen_ref, out_ref):
     for i in range(BLD):
         d, a = divmod(i, 2)
-        owner = owner_ref[i, 0]
+        owner = owner_ref[i]
         rank = jnp.int32(0)
         for e in range(i):
-            rank = rank + (owner_ref[e, 0] == owner).astype(jnp.int32)
+            rank = rank + (owner_ref[e] == owner).astype(jnp.int32)
         both = tiles_ref[owner].astype(f32)
         out_ref[d, a * 8 : a * 8 + 8, :] = jnp.where(rank == 0, both[:8], both[8:])
         for e in range(2):
             at = 16 + (a * 2 + e) * 8
-            out_ref[d, at : at + 8, :] = msg_ref[pl.ds(MSG1 * pair_ref[i, e], 8), :]
+            row = screens_ref[pair_ref[i, e]]
+            for j in range(8):
+                out_ref[d, at + j : at + j + 1, :] = row[:, j * 128 : j * 128 + 128]
     out_ref[:, 48:56, :] = seen_ref[...]
 
 
@@ -174,7 +184,7 @@
     return [[cadd(cmulc(b[0][c], a[0][r]), cmulc(b[1][c], a[1][r])) for c in range(2)] for r in range(2)]
 
 
-def calibrate(msg_ref, uv_ref, cols_ref, rows_ref, offs_ref, out_ref):
+def phases(uv_ref, offs_ref, row_hi_ref, row_lo_ref, cos_ref, sin_ref):
     mine = lax.axis_index("ch") * 2
     lane16 = lax.broadcasted_iota(jnp.int32, (TIMES, BLD), 1)
     lane128 = lax.broadcasted_iota(jnp.int32, (TIMES, 128), 1)
@@ -183,22 +193,37 @@
         picked = jnp.where(lane16 == mine + a, uv_ref[axis], 0.0)
         return jnp.broadcast_to(jnp.sum(picked, axis=1, keepdims=True), (TIMES, 128))
 
-    def phases(base):
+    def turns(base):
         return jnp.concatenate([base * (1.0 + c / (2.0 * CHANS)) for c in range(CHANS)], axis=0)
 
     u_both = jnp.where(lane128 < 64, column(0, 0), column(0, 1))
-    e_row = cos_turns(phases(u_both * offs_ref[0:1, :]) - offs_ref[2:3, :])
-    cos_col, sin_col = [], []
+    e_row = cos_turns(turns(u_both * offs_ref[0:1, :]) - offs_ref[2:3, :])
+    row_hi_ref[...], row_lo_ref[...] = split2(e_row)
     for a in range(2):
-        t = phases(column(1, a) * offs_ref[1:2, :])
-        cos_col.append(cos_turns(t))
-        sin_col.append(cos_turns(t - 0.25))
-
+        t = turns(column(1, a) * offs_ref[1:2, :])
+        cos_ref[a] = cos_turns(t)
+        sin_ref[a] = cos_turns(t - 0.25)
+
+
+def calibrate(
+    msg_ref,
+    row_hi_ref,
+    row_lo_ref,
+    cos_ref,
+    sin_ref,
+    cols_hi_ref,
+    cols_lo_ref,
+    rows_hi_ref,
+    rows_lo_ref,
+    out_ref,
+):
+    row_hi, row_lo = row_hi_ref[...], row_lo_ref[...]
     planes = [[msg_ref[k, a * 8 : a * 8 + 8, :] for k in range(8)] for a in range(2)]
     grid_re = jnp.concatenate([to_rows(planes[a][:4]) for a in range(2)], axis=0)
     grid_im = jnp.concatenate([to_rows(planes[a][4:]) for a in range(2)], axis=0)
     grid = jnp.concatenate([grid_re, grid_im], axis=1)
-    half = jnp.dot(grid, cols_ref[...], precision=highest, preferred_element_type=f32)
+    grid = grid.astype(bf16)
+    half = dot(grid, cols_hi_ref[...]) + dot(grid, cols_lo_ref[...])
     stacked = jnp.concatenate(
         [
             jnp.concatenate([half[:32, :128], half[32:, :128]], axis=1),
@@ -206,7 +231,7 @@
         ],
         axis=0,
     )
-    image = jnp.dot(rows_ref[...], stacked, precision=highest, preferred_element_type=f32)
+    image = dot3(rows_hi_ref[...], rows_lo_ref[...], *split2(stacked))
 
     lane_re = lax.broadcasted_iota(jnp.int32, (8, 256), 1) // SUB
     sub = lax.broadcasted_iota(jnp.int32, (8, 256), 0)
@@ -231,10 +256,11 @@
             [jnp.concatenate([m_re, m_im], axis=1), jnp.concatenate([m_im, -m_re], axis=1)], axis=0
         )
         block = jnp.concatenate([block, zeros] if a == 0 else [zeros, block], axis=0)
-        t = jnp.dot(e_row, block, precision=highest, preferred_element_type=f32)
+        t = dot3(row_hi, row_lo, *split2(block))
         t_re, t_im = t[:, :128], t[:, 128:]
+        cos_col, sin_col = cos_ref[a], sin_ref[a]
         w = jnp.concatenate(
-            [cos_col[a] * t_re + sin_col[a] * t_im, cos_col[a] * t_im - sin_col[a] * t_re], axis=1
+            [cos_col * t_re + sin_col * t_im, cos_col * t_im - sin_col * t_re], axis=1
         )
         w_hi, w_lo = split2(w)
         last = (((1,), (1,)), ((), ()))
@@ -246,15 +272,18 @@
             out_ref[k, 32:40, a * 32 : a * 32 + 32] = resid[:, k * 32 : k * 32 + 32]
         g = resid * (GRAD_SCALE / SUB)
         g_hi, g_lo = split2(g)
-        g_mid = g_lo.astype(f32)
-        g_pair = jnp.concatenate([g_hi.astype(f32), g_mid], axis=0).T.astype(bf16)
-        wide = jnp.dot(g_pair, jnp.concatenate([ones, ones], axis=0), preferred_element_type=f32)
+        g_pair = jnp.concatenate([g_hi.astype(f32), g_lo.astype(f32)], axis=0).T.astype(bf16)
+        wide = dot(g_pair, jnp.concatenate([ones, ones], axis=0))
         g_re, g_im = wide[:, :128], wide[:, 128:]
         d_t = jnp.concatenate(
-            [cos_col[a] * g_re - sin_col[a] * g_im, sin_col[a] * g_re + cos_col[a] * g_im], axis=1
+            [cos_col * g_re - sin_col * g_im, sin_col * g_re + cos_col * g_im], axis=1
         )
-        first_dim = (((0,), (0,)), ((), ()))
-        d_block = lax.dot_general(e_row, d_t, first_dim, precision=highest, preferred_element_type=f32)
+        d_hi, d_lo = split2(d_t)
+
+        def over_samples(e, d):
+            return lax.dot_general(e, d, (((0,), (0,)), ((), ())), preferred_element_type=f32)
+
+        d_block = over_samples(row_hi, d_hi) + (over_samples(row_hi, d_lo) + over_samples(row_lo, d_hi))
         d_block = d_block[a * 64 : a * 64 + 64]
         d_re = to_flat(d_block[:32, :128] - d_block[32:, 128:])
         d_im = to_flat(d_block[:32, 128:] + d_block[32:, :128])
@@ -264,8 +293,8 @@
             at = (a * 2 + e) * 8
             for p in range(4):
                 re, im = grads[e][p // 2][p % 2]
-                out_ref[p, at : at + 8, :] = re
-                out_ref[p + 4, at : at + 8, :] = im
+                out_ref[:, at + p, :] = re
+                out_ref[:, at + p + 4, :] = im
     out_ref[:, 32:40, 64:] = jnp.zeros((8, 8, 64), f32)
 
 
@@ -286,18 +315,29 @@
 
 
 def per_device(model_grid, screens, observed, uv_coords, station_pairs, tile_owner, tile_slot):
-    cols, rows, offs = tables()
+    *dft, offs = tables()
     sds = jax.ShapeDtypeStruct
+    owner = tile_owner.reshape(BLD)
 
     msg1 = pl.pallas_call(
         send_requests,
-        out_shape=sds((NBL * MSG1, 128), f32),
+        out_shape=sds((NBL, 1, MSG1), f32),
         in_specs=smem(2) + vmem(1),
         out_specs=vmem(1)[0],
         compiler_params=params,
         name="send_requests",
-    )(tile_owner, tile_slot, screens)
+    )(owner, tile_slot, screens)
     got1 = lax.all_to_all(msg1, "bl", 0, 0, tiled=True)
+
+    table = sds((SAMPLES, 128), bf16)
+    waves = pl.pallas_call(
+        phases,
+        out_shape=(table, table, sds((2, SAMPLES, 128), f32), sds((2, SAMPLES, 128), f32)),
+        in_specs=vmem(2),
+        out_specs=vmem(4),
+        compiler_params=params,
+        name="phases",
+    )(uv_coords, offs)
 
     tiles = pl.pallas_call(
         reply_tiles,
@@ -319,17 +359,17 @@
         out_specs=vmem(1)[0],
         compiler_params=params,
         name="send_baselines",
-    )(tile_owner, station_pairs, got2, got1, seen)
+    )(owner, station_pairs, got2, got1, seen)
     got3 = lax.all_to_all(msg3, "ch", 0, 0, tiled=True)
 
     msg5 = pl.pallas_call(
         calibrate,
         out_shape=sds((NCH, MSG5, 128), f32),
-        in_specs=vmem(5),
+        in_specs=vmem(9),
         out_specs=vmem(1)[0],
         compiler_params=params,
         name="calibrate",
-    )(got3, uv_coords, cols, rows, offs)
+    )(got3, *waves, *dft)
     got5 = lax.all_to_all(msg5, "ch", 0, 0, tiled=True)
 
     resid = got5[:, 32:40, :64].reshape(NCH, 8, 2, 2, TIMES)
@@ -354,7 +394,7 @@
         name="sum_all",
     )(got6)
     got7 = lax.all_to_all(msg7, "ch", 0, 0, tiled=True)
-    return residual, got7.reshape(1, 8, PIX)
+    return residual, got7.transpose(1, 0, 2).reshape(1, 8, PIX)
 
 
 def solution(mesh):

time: 120 us -> 114 us (0.950)
  blocking collectives: 79.9 us -> 58.6 us
  waiting for transfers between devices: 17.3 us -> 26.8 us
  starting transfers between devices: 9.75 us -> 16.5 us
    all_to_all x1 -> x0, blocking collectives: 16.8 us -> none  [per_device(): got3 = lax.all_to_all(msg3, 'ch', 0, 0, tiled=True)]
    all_to_all x0 -> x1, waiting for transfers between devices: none -> 9.42 us  [per_device(): got3 = lax.all_to_all(msg3, 'ch', 0, 0, tiled=True)]
    all_to_all x0 -> x1, starting transfers between devices: none -> 6.96 us  [per_device(): got3 = lax.all_to_all(msg3, 'ch', 0, 0, tiled=True)]
    all_to_all x1, blocking collectives: 32 us -> 27.4 us  [per_device(): got1 = lax.all_to_all(msg1, 'bl', 0, 0, tiled=True)]
    unnamed x22 -> x28, local copies, waits for them, and re-layouts: 3.42 us -> 3.04 us
  transfers between devices with their start and end apart: 2 -> 3, of which waited for: 2 -> 3; matrix products, arithmetic and copies ran while one was open for 1% -> 1% of each run, Pallas kernels for 0% -> 1%
where the time goes in v2:
time: 114 us
  blocking collectives  58.6 us (51%)
  waiting for transfers between devices  26.8 us (24%)
  starting transfers between devices  16.5 us (14%)
  Pallas kernels  7.75 us (7%)
  local copies, waits for them, and re-layouts  3.47 us (3%)
    all_to_all x1, blocking collectives, per_device(): got1 = lax.all_to_all(msg1, 'bl', 0, 0, tiled=True)  27.4 us
    all_to_all x1, blocking collectives, per_device(): got6 = lax.all_to_all(msg6, 'bl', 0, 0, tiled=True)  20.4 us
    all_to_all x1, waiting for transfers between devices, per_device(): got2 = lax.all_to_all(tiles, 'bl', 0, 0, tiled=True)  11.5 us
    all_to_all x1, blocking collectives, per_device(): got5 = lax.all_to_all(msg5, 'ch', 0, 0, tiled=True)  10.8 us
    all_to_all x1, waiting for transfers between devices, per_device(): got3 = lax.all_to_all(msg3, 'ch', 0, 0, tiled=True)  9.42 us
    all_to_all x1, starting transfers between devices, per_device(): got3 = lax.all_to_all(msg3, 'ch', 0, 0, tiled=True)  6.96 us
    all_to_all x1, starting transfers between devices, per_device(): got2 = lax.all_to_all(tiles, 'bl', 0, 0, tiled=True)  6.2 us
    all_to_all x1, waiting for transfers between devices, per_device(): got7 = lax.all_to_all(msg7, 'ch', 0, 0, tiled=True)  5.84 us
  transfers between devices with their start and end apart: 3, of which 3 were waited for; matrix products, arithmetic and copies ran while one was open for 1% of the time, Pallas kernels for 1%

profile of v2, /device:TPU:1, one launch (start us, length us, event | category | flops | bytes accessed | tf_op | source)
XLA Modules:
  0.0 113.9 jit_solution(5709961303894000503)
XLA Ops:
  0.7 0.6 copy-done.9
  1.3 0.8 copy-done.3
  2.1 0.7 send_requests.1
  2.8 27.4 %all_to_all.30.msg_ref.screens_ref = f32[64,1,1152]{2,1,0:T(1,128)S(1)} all-to-all(f32[64,1,1152]{2,1,0:T(1,128)S(1)} %send_requests.1), channel_id=1, replica_groups=mesh['bl'=64,'ch'=8] {'bl'}, dimensions={0} | all-to-all | bytes 589824 | tf_op jit(solution)/shard_map/all_to_all | solution.py:330
  30.2 1.1 reply_tiles.1
  31.3 6.2 %all-to-all-start.1 = ((bf16[64,16,128]{2,1,0:T(8,128)(2,1)}), bf16[64,16,128]{2,1,0:T(8,128)(2,1)S(1)}, u32[]{:S(2)}, u32[]{:S(2)}) async-start(bf16[64,16,128]{2,1,0:T(8,128)(2,1)} %reply_tiles.1), calls=%async_computation.1 | async-start | bytes 524288 | tf_op jit(solution)/shard_map/all_to_all | solution.py:351
  37.6 0.1 copy.18
  37.8 0.1 copy.19
  37.9 0.2 reshape.24
  38.0 11.5 %all-to-all-done.1.tiles_ref = bf16[64,16,128]{2,1,0:T(8,128)(2,1)S(1)} async-done(((bf16[64,16,128]{2,1,0:T(8,128)(2,1)}), bf16[64,16,128]{2,1,0:T(8,128)(2,1)S(1)}, u32[]{:S(2)}, u32[]{:S(2)}) %all-to-all-start.1) | async-done | bytes 262176 | tf_op jit(solution)/shard_map/all_to_all | solution.py:351
  49.5 1.6 %send_baselines.1 = f32[8,56,128]{2,1,0:T(8,128)} custom-call(s32[16]{0:T(128)S(1)} %bitcast.11, s32[16,2]{1,0:T(8,128)S(1)} %copy.20.pair_ref, bf16[64,16,128]{2,1,0:T(8,128)(2,1)S(1)} %all-to-all-done.1.tiles_ref, f32[64,1,1152]{2,1,0:T(1,128)S(1)} %all_to_all.30.msg_ref.screens_ref, f32[8,8,128]{2,1,0:T(8,128)S(1)} %pad.4.seen_ref), custom_call_target="tpu_custom_call" | custom-call | tf_op jit(solution)/shard_map/send_baselines/pallas_call | solution.py:355
  51.1 7.0 %all-to-all-start.2 = ((f32[8,56,128]{2,1,0:T(8,128)}), f32[8,56,128]{2,1,0:T(8,128)S(1)}, u32[]{:S(2)}, u32[]{:S(2)}) async-start(f32[8,56,128]{2,1,0:T(8,128)} %send_baselines.1), calls=%async_computation.2 | async-start | bytes 458752 | tf_op jit(solution)/shard_map/all_to_all | solution.py:363
  58.1 0.6 phases.1
  58.7 9.4 %all-to-all-done.2.msg_ref = f32[8,56,128]{2,1,0:T(8,128)S(1)} async-done(((f32[8,56,128]{2,1,0:T(8,128)}), f32[8,56,128]{2,1,0:T(8,128)S(1)}, u32[]{:S(2)}, u32[]{:S(2)}) %all-to-all-start.2) | async-done | bytes 229408 | tf_op jit(solution)/shard_map/all_to_all | solution.py:363
  68.1 2.4 %calibrate.1 = f32[8,40,128]{2,1,0:T(8,128)S(1)} custom-call(f32[8,56,128]{2,1,0:T(8,128)S(1)} %all-to-all-done.2.msg_ref, bf16[256,128]{1,0:T(8,128)(2,1)S(1)} %get-tuple-element.6.row_hi_ref, bf16[256,128]{1,0:T(8,128)(2,1)S(1)} %get-tuple-element.7.row_lo_ref, f32[2,256,128]{2,1,0:T(8,128)S(1)} %get-tuple-element.8.cos_ref, ...), custom_call_target="tpu_custom_call" | custom-call | tf_op jit(solution)/shard_map/calibrate/pallas_call | solution.py:365
  70.5 10.8 %all_to_all.31.msg_ref = f32[8,40,128]{2,1,0:T(8,128)S(1)} all-to-all(f32[8,40,128]{2,1,0:T(8,128)S(1)} %calibrate.1), channel_id=1, replica_groups=mesh['bl'=64,'ch'=8] {'ch'}, dimensions={0} | all-to-all | bytes 327680 | tf_op jit(solution)/shard_map/all_to_all | solution.py:373
  81.3 0.8 sum_terms.1
  82.0 20.4 %all_to_all.32.msg_ref = f32[64,8,128]{2,1,0:T(8,128)S(1)} all-to-all(f32[64,8,128]{2,1,0:T(8,128)S(1)} %sum_terms.1), channel_id=1, replica_groups=mesh['bl'=64,'ch'=8] {'bl'}, dimensions={0} | all-to-all | bytes 524288 | tf_op jit(solution)/shard_map/all_to_all | solution.py:386
  102.4 0.7 sum_all.1
  103.1 3.3 %all-to-all-start.5 = ((f32[8,8,128]{2,1,0:T(8,128)}), f32[8,8,128]{2,1,0:T(8,128)S(1)}, u32[]{:S(2)}, u32[]{:S(2)}) async-start(f32[8,8,128]{2,1,0:T(8,128)} %sum_all.1), calls=%async_computation.5 | async-start | bytes 65536 | tf_op jit(solution)/shard_map/all_to_all | solution.py:396
  106.5 0.1 reshape.25
  106.7 0.8 copy.23
  107.4 5.8 %all-to-all-done.5 = f32[8,8,128]{2,1,0:T(8,128)S(1)} async-done(((f32[8,8,128]{2,1,0:T(8,128)}), f32[8,8,128]{2,1,0:T(8,128)S(1)}, u32[]{:S(2)}, u32[]{:S(2)}) %all-to-all-start.5) | async-done | bytes 32800 | tf_op jit(solution)/shard_map/all_to_all | solution.py:396
  113.3 0.6 copy.25
  (26 shorter events, 0.2 us)
Async XLA Ops:
  0.6 0.7 copy-start.9
  0.6 0.7 copy-start.8
  1.3 0.8 copy-start.3
  2.8 27.4 %copy-start = (bf16[1,128,1024]{2,1,0:T(8,128)(2,1)S(1)}, bf16[1,128,1024]{2,1,0:T(8,128)(2,1)}, u32[]{:S(2)}) copy-start(bf16[1,128,1024]{2,1,0:T(8,128)(2,1)} %grid_ref.1) | copy-start | bytes 786436
  31.3 6.2 %copy-start.11 = (s32[16,2]{0,1:T(2,128)S(1)}, s32[16,2]{0,1:T(2,128)}, u32[]{:S(2)}) copy-start(s32[16,2]{0,1:T(2,128)} %param.16) | copy-start | bytes 388
  31.3 6.3 %copy-start.10 = (f32[8,16,2,16]{3,2,1,0:T(2,128)S(1)}, f32[8,16,2,16]{3,2,1,0:T(2,128)}, u32[]{:S(2)}) copy-start(f32[8,16,2,16]{3,2,1,0:T(2,128)} %param.14) | copy-start | bytes 49156
  31.3 18.2 %all-to-all-start.1 = ((bf16[64,16,128]{2,1,0:T(8,128)(2,1)}), bf16[64,16,128]{2,1,0:T(8,128)(2,1)S(1)}, u32[]{:S(2)}, u32[]{:S(2)}) async-start(bf16[64,16,128]{2,1,0:T(8,128)(2,1)} %reply_tiles.1), calls=%async_computation.1 | async-start | bytes 524288 | tf_op jit(solution)/shard_map/all_to_all | solution.py:351
  51.1 7.0 %copy-start.6 = (f32[2,16,16]{2,1,0:T(8,128)S(1)}, f32[2,16,16]{2,1,0:T(8,128)}, u32[]{:S(2)}) copy-start(f32[2,16,16]{2,1,0:T(8,128)} %uv_ref.1) | copy-start | bytes 6148
  51.1 7.0 %copy-start.7 = (f32[8,128]{1,0:T(8,128)S(1)}, f32[8,128]{1,0:T(8,128)}, u32[]{:S(2)}) copy-start(f32[8,128]{1,0:T(8,128)} %constant.13.clone.offs_ref) | copy-start | bytes 12292
  51.1 17.0 %copy-start.1 = (bf16[256,256]{1,0:T(8,128)(2,1)S(1)}, bf16[256,256]{1,0:T(8,128)(2,1)}, u32[]{:S(2)}) copy-start(bf16[256,256]{1,0:T(8,128)(2,1)} %constant.15.clone.cols_lo_ref) | copy-start | bytes 393220
  51.1 17.0 %copy-start.2 = (bf16[256,256]{1,0:T(8,128)(2,1)S(1)}, bf16[256,256]{1,0:T(8,128)(2,1)}, u32[]{:S(2)}) copy-start(bf16[256,256]{1,0:T(8,128)(2,1)} %constant.14.clone.cols_hi_ref) | copy-start | bytes 393220
  51.1 17.0 %copy-start.5 = (bf16[64,64]{1,0:T(8,128)(2,1)S(1)}, bf16[64,64]{1,0:T(8,128)(2,1)}, u32[]{:S(2)}) copy-start(bf16[64,64]{1,0:T(8,128)(2,1)} %constant.16.clone.rows_hi_ref) | copy-start | bytes 24580
  51.1 17.0 %all-to-all-start.2 = ((f32[8,56,128]{2,1,0:T(8,128)}), f32[8,56,128]{2,1,0:T(8,128)S(1)}, u32[]{:S(2)}, u32[]{:S(2)}) async-start(f32[8,56,128]{2,1,0:T(8,128)} %send_baselines.1), calls=%async_computation.2 | async-start | bytes 458752 | tf_op jit(solution)/shard_map/all_to_all | solution.py:363
  58.1 10.0 %copy-start.4 = (bf16[64,64]{1,0:T(8,128)(2,1)S(1)}, bf16[64,64]{1,0:T(8,128)(2,1)}, u32[]{:S(2)}) copy-start(bf16[64,64]{1,0:T(8,128)(2,1)} %constant.17.clone.rows_lo_ref) | copy-start | bytes 24580
  103.1 10.1 %all-to-all-start.5 = ((f32[8,8,128]{2,1,0:T(8,128)}), f32[8,8,128]{2,1,0:T(8,128)S(1)}, u32[]{:S(2)}, u32[]{:S(2)}) async-start(f32[8,8,128]{2,1,0:T(8,128)} %sum_all.1), calls=%async_computation.5 | async-start | bytes 65536 | tf_op jit(solution)/shard_map/all_to_all | solution.py:396

commit v3 on v2

--- a/solution.py
+++ b/solution.py
@@ -6,6 +6,7 @@
 from jax import lax
 from jax.experimental import pallas as pl
 from jax.experimental.pallas import tpu as pltpu
+from jax.sharding import Mesh
 from jax.sharding import PartitionSpec as P
 
 SUB = 32
@@ -13,13 +14,14 @@
 TIMES = 16
 CHANS = 16
 NBL = 64
+CHIPS = 32
 NCH = 8
 BLD = 16
 TILES = 128
 SAMPLES = TIMES * CHANS
 MSG1 = PIX + 128
 MSG3 = 56
-MSG5 = 40
+MSG5 = 24
 f32 = jnp.float32
 bf16 = jnp.bfloat16
 GRAD_SCALE = SUB / math.sqrt(2.0 * BLD * NBL * CHANS * TIMES / NBL)
@@ -94,31 +96,40 @@
     c = lax.axis_index("ch")
     subs = lax.broadcasted_iota(jnp.int32, (8, PIX), 0)
     mine = jnp.sum(jnp.where(subs == c, screen_ref[0], 0.0), axis=0, keepdims=True)
-    out_ref[:, :, :PIX] = jnp.broadcast_to(mine.reshape(1, 1, PIX), (NBL, 1, PIX))
-    rows = lax.broadcasted_iota(jnp.int32, (NBL, 128), 0)
-    lanes = lax.broadcasted_iota(jnp.int32, (NBL, 128), 1)
-    count = jnp.zeros((NBL, 128), jnp.int32)
-    req = jnp.zeros((NBL, 128), jnp.int32)
+    out_ref[:, :, :PIX] = jnp.broadcast_to(mine.reshape(1, 1, PIX), (CHIPS, 1, PIX))
+    rows = lax.broadcasted_iota(jnp.int32, (CHIPS, 128), 0)
+    lanes = lax.broadcasted_iota(jnp.int32, (CHIPS, 128), 1)
+    holder = rows * 2 + lanes // 2
+    count = lanes % 2
+    req = jnp.zeros((CHIPS, 128), jnp.int32)
     for i in range(BLD):
-        hit = rows == owner_ref[i]
-        req = jnp.where(hit & (lanes == count), slot_ref[i] + 1, req)
-        count = count + hit.astype(jnp.int32)
-    out_ref[:, :, PIX:] = req.astype(f32).reshape(NBL, 1, 128)
-
-
-def reply_tiles(msg_ref, grid_ref, out_ref, scr_ref):
-    req = msg_ref[:, :, PIX:].reshape(NBL, 128).astype(jnp.int32)
-    lanes = lax.broadcasted_iota(jnp.int32, (NBL, 128), 1) + 1
-    grid = grid_ref[0]
-    for k in range(2):
-        pick = jnp.where(lanes == req[:, k : k + 1], 1.0, 0.0).astype(bf16)
-        got = jnp.dot(pick, grid, preferred_element_type=f32)
+        hit = (holder == owner_ref[i]) & (lanes < 4)
+        req = jnp.where(hit & (count == 0), slot_ref[i] + 1, req)
+        count = count - hit.astype(jnp.int32)
+    out_ref[:, :, PIX:] = req.astype(f32).reshape(CHIPS, 1, 128)
+
+
+def reply_tiles(msg_ref, grid_ref, other_ref, out_ref, scr_ref):
+    core = lax.axis_index("core")
+    req = msg_ref[:, :, PIX:].reshape(CHIPS, 128).astype(jnp.int32)
+    lanes = lax.broadcasted_iota(jnp.int32, (CHIPS, 2 * TILES), 1) + 1
+    picks = []
+    for k in range(4):
+        wanted = req[:, k : k + 1]
+        shift = jnp.where(core == k // 2, 0, TILES)
+        hit = (lanes == wanted + shift) & (wanted > 0)
+        picks.append(jnp.where(hit, 1.0, 0.0).astype(bf16))
+    both = jnp.concatenate([grid_ref[0], other_ref[0]], axis=0)
+    got = dot(jnp.concatenate(picks, axis=0), both)
+    for k in range(4):
         for j in range(8):
-            scr_ref[pl.ds(k * 8 + j, NBL, stride=16), :] = got[:, j * 128 : (j + 1) * 128]
-    out_ref[...] = scr_ref[...].reshape(NBL, 16, 128).astype(bf16)
-
-
-def send_baselines(owner_ref, pair_ref, tiles_ref, screens_ref, seen_ref, out_ref):
+            part = got[k * CHIPS : (k + 1) * CHIPS, j * 128 : (j + 1) * 128]
+            scr_ref[pl.ds(k * 8 + j, CHIPS, stride=32), :] = part
+    out_ref[...] = scr_ref[...].reshape(CHIPS, 32, 128).astype(bf16)
+
+
+def send_baselines(owner_ref, pair_ref, tiles_ref, mine_ref, other_ref, seen_ref, out_ref):
+    core = lax.axis_index("core")
     for i in range(BLD):
         d, a = divmod(i, 2)
         owner = owner_ref[i]
@@ -129,7 +140,8 @@
         out_ref[d, a * 8 : a * 8 + 8, :] = jnp.where(rank == 0, both[:8], both[8:])
         for e in range(2):
             at = 16 + (a * 2 + e) * 8
-            row = screens_ref[pair_ref[i, e]]
+            s = pair_ref[i, e]
+            row = jnp.where(s % 2 == core, mine_ref[s // 2], other_ref[s // 2])
             for j in range(8):
                 out_ref[d, at + j : at + j + 1, :] = row[:, j * 128 : j * 128 + 128]
     out_ref[:, 48:56, :] = seen_ref[...]
@@ -269,7 +281,9 @@
         seen = jnp.concatenate([msg_ref[k, 48:56, a * 32 : a * 32 + 32] for k in range(8)], axis=1)
         resid = vis * (1.0 / SUB) - seen
         for k in range(8):
-            out_ref[k, 32:40, a * 32 : a * 32 + 32] = resid[:, k * 32 : k * 32 + 32]
+            part = resid[:, k * 32 : k * 32 + 32]
+            out_ref[k, 0, 16:24, a * 32 : a * 32 + 32] = part
+            out_ref[k, 1, 16:24, a * 32 : a * 32 + 32] = part
         g = resid * (GRAD_SCALE / SUB)
         g_hi, g_lo = split2(g)
         g_pair = jnp.concatenate([g_hi.astype(f32), g_lo.astype(f32)], axis=0).T.astype(bf16)
@@ -290,22 +304,27 @@
         down = mat(lambda p: (d_re[p], d_im[p]))
         grads = [prod_h(prod(down, second), sky), h_prod(down, middle)]
         for e in range(2):
-            at = (a * 2 + e) * 8
+            at = (a * 2 + e) * 4
             for p in range(4):
                 re, im = grads[e][p // 2][p % 2]
-                out_ref[:, at + p, :] = re
-                out_ref[:, at + p + 4, :] = im
-    out_ref[:, 32:40, 64:] = jnp.zeros((8, 8, 64), f32)
-
-
-def sum_terms(pair_ref, msg_ref, out_ref):
+                out_ref[:, 0, at + p, :] = re
+                out_ref[:, 1, at + p, :] = im
+    out_ref[:, :, 16:24, 64:] = jnp.zeros((8, 2, 8, 64), f32)
+
+
+def sum_terms(pair_ref, other_ref, msg_ref, out_ref):
+    core = lax.axis_index("core")
+    half = lax.broadcasted_iota(jnp.int32, (8, 128), 0) // 4
     out_ref[...] = jnp.zeros_like(out_ref)
     for i in range(BLD):
         d, a = divmod(i, 2)
-        for e in range(2):
-            s = pair_ref[i, e]
-            at = (a * 2 + e) * 8
-            out_ref[s] = out_ref[s] + msg_ref[d, at : at + 8, :]
+        for k in range(2):
+            both = msg_ref[d, k, a * 8 : a * 8 + 8, :]
+            turned = pltpu.roll(both, 4, 0)
+            for e in range(2):
+                s = jnp.where(core == k, pair_ref[i, e], other_ref[i, e])
+                term = jnp.where(s % 2 == e, both, turned)
+                out_ref[s // 2] = out_ref[s // 2] + jnp.where(half == s % 2, term, 0.0)
 
 
 def sum_all(msg_ref, out_ref):
@@ -319,15 +338,22 @@
     sds = jax.ShapeDtypeStruct
     owner = tile_owner.reshape(BLD)
 
+    def from_other_core(x):
+        return lax.ppermute(x, "core", [(0, 1), (1, 0)])
+
+    other_grid = from_other_core(model_grid)
+    other_pairs = from_other_core(station_pairs)
+
     msg1 = pl.pallas_call(
         send_requests,
-        out_shape=sds((NBL, 1, MSG1), f32),
+        out_shape=sds((CHIPS, 1, MSG1), f32),
         in_specs=smem(2) + vmem(1),
         out_specs=vmem(1)[0],
         compiler_params=params,
         name="send_requests",
     )(owner, tile_slot, screens)
-    got1 = lax.all_to_all(msg1, "bl", 0, 0, tiled=True)
+    got1 = lax.all_to_all(msg1, "xz", 0, 0, tiled=True)
+    other1 = from_other_core(got1)
 
     table = sds((SAMPLES, 128), bf16)
     waves = pl.pallas_call(
@@ -341,49 +367,52 @@
 
     tiles = pl.pallas_call(
         reply_tiles,
-        out_shape=sds((NBL, 16, 128), bf16),
-        in_specs=vmem(2),
-        out_specs=vmem(1)[0],
-        scratch_shapes=[pltpu.VMEM((NBL * 16, 128), f32)],
+        out_shape=sds((CHIPS, 32, 128), bf16),
+        in_specs=vmem(3),
+        out_specs=vmem(1)[0],
+        scratch_shapes=[pltpu.VMEM((CHIPS * 32, 128), f32)],
         compiler_params=params,
         name="reply_tiles",
-    )(got1, model_grid)
-    got2 = lax.all_to_all(tiles, "bl", 0, 0, tiled=True)
+    )(got1, model_grid, other_grid)
+    got2 = lax.all_to_all(tiles, "xz", 0, 0, tiled=True).reshape(NBL, 16, 128)
 
     seen = observed.reshape(8, TIMES, 2, NCH, 2).transpose(3, 0, 4, 2, 1).reshape(NCH, 8, 64)
     seen = jnp.pad(seen, ((0, 0), (0, 0), (0, 64)))
     msg3 = pl.pallas_call(
         send_baselines,
         out_shape=sds((NCH, MSG3, 128), f32),
-        in_specs=smem(2) + vmem(3),
+        in_specs=smem(2) + vmem(4),
         out_specs=vmem(1)[0],
         compiler_params=params,
         name="send_baselines",
-    )(owner, station_pairs, got2, got1, seen)
+    )(owner, station_pairs, got2, got1, other1, seen)
     got3 = lax.all_to_all(msg3, "ch", 0, 0, tiled=True)
 
     msg5 = pl.pallas_call(
         calibrate,
-        out_shape=sds((NCH, MSG5, 128), f32),
+        out_shape=sds((NCH, 2, MSG5, 128), f32),
         in_specs=vmem(9),
         out_specs=vmem(1)[0],
         compiler_params=params,
         name="calibrate",
     )(got3, *waves, *dft)
-    got5 = lax.all_to_all(msg5, "ch", 0, 0, tiled=True)
-
-    resid = got5[:, 32:40, :64].reshape(NCH, 8, 2, 2, TIMES)
+    got5 = lax.all_to_all(msg5.reshape(2 * NCH, MSG5, 128), ("ch", "core"), 0, 0, tiled=True)
+    got5 = got5.reshape(NCH, 2, MSG5, 128)
+
+    core = lax.axis_index("core")
+    resid = jnp.where(core == 0, got5[:, 0, 16:24, :64], got5[:, 1, 16:24, :64])
+    resid = resid.reshape(NCH, 8, 2, 2, TIMES)
     residual = resid.transpose(1, 4, 3, 0, 2).reshape(8, TIMES, 2, BLD)
 
     msg6 = pl.pallas_call(
         sum_terms,
-        out_shape=sds((NBL, 8, 128), f32),
-        in_specs=smem(1) + vmem(1),
+        out_shape=sds((CHIPS, 8, 128), f32),
+        in_specs=smem(2) + vmem(1),
         out_specs=vmem(1)[0],
         compiler_params=params,
         name="sum_terms",
-    )(station_pairs, got5)
-    got6 = lax.all_to_all(msg6, "bl", 0, 0, tiled=True)
+    )(station_pairs, other_pairs, got5)
+    got6 = lax.all_to_all(msg6, "xz", 0, 0, tiled=True)
 
     msg7 = pl.pallas_call(
         sum_all,
@@ -393,21 +422,23 @@
         compiler_params=params,
         name="sum_all",
     )(got6)
-    got7 = lax.all_to_all(msg7, "ch", 0, 0, tiled=True)
-    return residual, got7.transpose(1, 0, 2).reshape(1, 8, PIX)
+    got7 = lax.all_to_all(msg7.reshape(2 * NCH, 4, 128), ("ch", "core"), 0, 0, tiled=True)
+    return residual, got7.reshape(NCH, 8, 128).transpose(1, 0, 2).reshape(1, 8, PIX)
 
 
 def solution(mesh):
+    mesh = Mesh(mesh.devices.reshape(CHIPS, 2, NCH), ("xz", "core", "ch"))
+    bl = ("xz", "core")
     in_specs = (
-        P("ch", "bl", None),
-        P("bl", None, None),
-        P(None, None, "ch", "bl"),
-        P(None, None, "bl"),
-        P("bl", None),
-        P("bl", None),
-        P("bl"),
+        P("ch", bl, None),
+        P(bl, None, None),
+        P(None, None, "ch", bl),
+        P(None, None, bl),
+        P(bl, None),
+        P(bl, None),
+        P(bl),
     )
-    out_specs = (P(None, None, "ch", "bl"), P("bl", None, None))
+    out_specs = (P(None, None, "ch", bl), P(bl, None, None))
     return jax.shard_map(
         per_device, mesh=mesh, in_specs=in_specs, out_specs=out_specs, check_vma=False
     )

time: 114 us -> 112 us (0.982)
  blocking collectives: 58.6 us -> 0 us
  starting transfers between devices: 16.5 us -> 51.3 us
  waiting for transfers between devices: 26.8 us -> 44.4 us
  Pallas kernels: 7.75 us -> 10.7 us
    all_to_all x3 -> x0, blocking collectives: 58.6 us -> none  [the longest x1 27.4 us: per_device(): got1 = lax.all_to_all(msg1, 'bl', 0, 0, tiled=True)]
    all_to_all x2 -> x5, starting transfers between devices: 9.54 us -> 35.7 us  [the longest x1 13.7 us: per_device(): got1 = lax.all_to_all(msg1, 'xz', 0, 0, tiled=True)]
    all_to_all x2 -> x5, waiting for transfers between devices: 17.3 us -> 33.5 us  [the longest x1 9.37 us: per_device(): got6 = lax.all_to_all(msg6, 'xz', 0, 0, tiled=True)]
    ppermute x0 -> x3, starting transfers between devices: none -> 8.68 us  [from_other_core(): return lax.ppermute(x, 'core', [(0, 1), (1, 0)])]
    pallas_call x4, Pallas kernels: 4.93 us -> 7.69 us  [the longest x1 3.06 us: per_device(): pl.pallas_call(calibrate, out_shape=sds((NCH, 2, MSG5, 128), f32), in_spe...]
    ppermute x0 -> x3, waiting for transfers between devices: none -> 2.55 us  [from_other_core(): return lax.ppermute(x, 'core', [(0, 1), (1, 0)])]
    unnamed x28 -> x30, local copies, waits for them, and re-layouts: 3.04 us -> 3.73 us
  transfers between devices with their start and end apart: 3 -> 9, of which waited for: 3 -> 9; matrix products, arithmetic and copies ran while one was open for 1% -> 1% of each run, Pallas kernels for 1% -> 1%
where the time goes in v3:
time: 112 us; the launch traced here: 111 us
  starting transfers between devices  51.3 us (46%)
  waiting for transfers between devices  44.4 us (40%)
  Pallas kernels  10.7 us (10%)
  local copies, waits for them, and re-layouts  4.15 us (4%)
    all_to_all x1, starting transfers between devices, per_device(): got1 = lax.all_to_all(msg1, 'xz', 0, 0, tiled=True)  13.7 us
    all_to_all x1, waiting for transfers between devices, per_device(): got6 = lax.all_to_all(msg6, 'xz', 0, 0, tiled=True)  9.37 us
    ppermute x3, starting transfers between devices, from_other_core(): return lax.ppermute(x, 'core', [(0, 1), (1, 0)])  8.68 us
    all_to_all x1, starting transfers between devices, per_device(): lax.all_to_all(msg5.reshape(2 * NCH, MSG5, 128), ('ch', 'core'), 0, 0, ti...  8.36 us
    all_to_all x1, waiting for transfers between devices, per_device(): got3 = lax.all_to_all(msg3, 'ch', 0, 0, tiled=True)  8.36 us
    all_to_all x1, waiting for transfers between devices, per_device(): lax.all_to_all(msg5.reshape(2 * NCH, MSG5, 128), ('ch', 'core'), 0, 0, ti...  7.32 us
    all_to_all x1, starting transfers between devices, per_device(): got3 = lax.all_to_all(msg3, 'ch', 0, 0, tiled=True)  6.96 us
    all_to_all x1, waiting for transfers between devices, per_device(): lax.all_to_all(msg7.reshape(2 * NCH, 4, 128), ('ch', 'core'), 0, 0, tiled...  6.53 us
  transfers between devices with their start and end apart: 9, of which 9 were waited for; matrix products, arithmetic and copies ran while one was open for 1% of the time, Pallas kernels for 1%

profile of v3, /device:TPU:1, one launch (start us, length us, event | category | flops | bytes accessed | tf_op | source)
XLA Modules:
  0.0 111.4 jit_solution(2745220528895873587)
XLA Ops:
  0.6 0.8 copy-done.3
  2.8 1.3 %send_requests.1 = f32[32,1,1152]{2,1,0:T(1,128)} custom-call(s32[16]{0:T(128)S(1)} %bitcast.21, s32[16]{0:T(128)S(1)} %copy-done.10, f32[1,8,1024]{2,1,0:T(8,128)S(1)} %copy-done.3), custom_call_target="tpu_custom_call" | custom-call | tf_op jit(solution)/shard_map/send_requests/pallas_call | solution.py:347
  4.1 13.7 %all-to-all-start = ((f32[32,1,1152]{2,1,0:T(1,128)}), f32[32,1,1152]{2,1,0:T(1,128)S(1)}, u32[]{:S(2)}, u32[]{:S(2)}) async-start(f32[32,1,1152]{2,1,0:T(1,128)} %send_requests.1), calls=%async_computation | async-start | bytes 294912 | tf_op jit(solution)/shard_map/all_to_all | solution.py:355
  17.8 2.9 %collective-permute-start = (bf16[1,128,1024]{2,1,0:T(8,128)(2,1)S(1)}, bf16[1,128,1024]{2,1,0:T(8,128)(2,1)S(1)}, u32[]{:S(2)}, u32[]{:S(2)}) collective-permute-start(bf16[1,128,1024]{2,1,0:T(8,128)(2,1)S(1)} %copy-done), channel_id=1, source_target_pairs={{0,8},{8,0},{1,9},{9,1},{2,10},{10,2},{3,11},{11,3},{4,12},{12,4},... | collective-permute-start | bytes 786440 | tf_op jit(solution)/shard_map/ppermute | solution.py:342
  20.7 1.1 %collective-permute-done.other_ref = bf16[1,128,1024]{2,1,0:T(8,128)(2,1)S(1)} collective-permute-done((bf16[1,128,1024]{2,1,0:T(8,128)(2,1)S(1)}, bf16[1,128,1024]{2,1,0:T(8,128)(2,1)S(1)}, u32[]{:S(2)}, u32[]{:S(2)}) %collective-permute-start) | collective-permute-done | bytes 262176 | tf_op jit(solution)/shard_map/ppermute | solution.py:342
  21.8 5.3 %all-to-all-done.msg_ref.mine_ref = f32[32,1,1152]{2,1,0:T(1,128)S(1)} async-done(((f32[32,1,1152]{2,1,0:T(1,128)}), f32[32,1,1152]{2,1,0:T(1,128)S(1)}, u32[]{:S(2)}, u32[]{:S(2)}) %all-to-all-start) | async-done | bytes 147488 | tf_op jit(solution)/shard_map/all_to_all | solution.py:355
  27.1 1.4 %reply_tiles.1 = bf16[32,32,128]{2,1,0:T(8,128)(2,1)} custom-call(f32[32,1,1152]{2,1,0:T(1,128)S(1)} %all-to-all-done.msg_ref.mine_ref, bf16[1,128,1024]{2,1,0:T(8,128)(2,1)S(1)} %copy-done, bf16[1,128,1024]{2,1,0:T(8,128)(2,1)S(1)} %collective-permute-done.other_ref), custom_call_target="tpu_custom_call" | custom-call | tf_op jit(solution)/shard_map/reply_tiles/pallas_call | solution.py:368
  28.5 4.4 %all-to-all-start.1 = ((bf16[32,32,128]{2,1,0:T(8,128)(2,1)}), bf16[32,32,128]{2,1,0:T(8,128)(2,1)S(1)}, u32[]{:S(2)}, u32[]{:S(2)}) async-start(bf16[32,32,128]{2,1,0:T(8,128)(2,1)} %reply_tiles.1), calls=%async_computation.1 | async-start | bytes 524288 | tf_op jit(solution)/shard_map/all_to_all | solution.py:377
  32.9 3.7 %collective-permute-start.1 = (f32[32,1,1152]{2,1,0:T(1,128)S(1)}, f32[32,1,1152]{2,1,0:T(1,128)S(1)}, u32[]{:S(2)}, u32[]{:S(2)}) collective-permute-start(f32[32,1,1152]{2,1,0:T(1,128)S(1)} %all-to-all-done.msg_ref.mine_ref), channel_id=1, source_target_pairs={{0,8},{8,0},{1,9},{9,1},{2,10},{10,2},{3,11},{11,3},{4,12},{12,4},... | collective-permute-start | bytes 442376 | tf_op jit(solution)/shard_map/ppermute | solution.py:342
  37.6 5.0 %all-to-all-done.1 = bf16[32,32,128]{2,1,0:T(8,128)(2,1)S(1)} async-done(((bf16[32,32,128]{2,1,0:T(8,128)(2,1)}), bf16[32,32,128]{2,1,0:T(8,128)(2,1)S(1)}, u32[]{:S(2)}, u32[]{:S(2)}) %all-to-all-start.1) | async-done | bytes 262176 | tf_op jit(solution)/shard_map/all_to_all | solution.py:377
  42.6 1.8 %send_baselines.1 = f32[8,56,128]{2,1,0:T(8,128)} custom-call(s32[16]{0:T(128)S(1)} %bitcast.22, s32[16,2]{1,0:T(8,128)S(1)} %copy.21.pair_ref, bf16[64,16,128]{2,1,0:T(8,128)(2,1)S(1)} %bitcast.20, f32[32,1,1152]{2,1,0:T(1,128)S(1)} %all-to-all-done.msg_ref.mine_ref, f32[32,1,1152]{2,1,0:T(1,128)S(1)} %collective-permute-done.1.other_ref, ...), custom_call_target="tpu_custom_call" | custom-call | tf_op jit(solution)/shard_map/send_baselines/pallas_call | solution.py:381
  44.4 7.0 %all-to-all-start.2 = ((f32[8,56,128]{2,1,0:T(8,128)}), f32[8,56,128]{2,1,0:T(8,128)S(1)}, u32[]{:S(2)}, u32[]{:S(2)}) async-start(f32[8,56,128]{2,1,0:T(8,128)} %send_baselines.1), calls=%async_computation.2 | async-start | bytes 458752 | tf_op jit(solution)/shard_map/all_to_all | solution.py:389
  51.9 8.4 %all-to-all-done.2.msg_ref = f32[8,56,128]{2,1,0:T(8,128)S(1)} async-done(((f32[8,56,128]{2,1,0:T(8,128)}), f32[8,56,128]{2,1,0:T(8,128)S(1)}, u32[]{:S(2)}, u32[]{:S(2)}) %all-to-all-start.2) | async-done | bytes 229408 | tf_op jit(solution)/shard_map/all_to_all | solution.py:389
  60.3 3.1 %calibrate.1 = f32[8,2,24,128]{3,2,1,0:T(8,128)} custom-call(f32[8,56,128]{2,1,0:T(8,128)S(1)} %all-to-all-done.2.msg_ref, bf16[256,128]{1,0:T(8,128)(2,1)S(1)} %get-tuple-element.6.row_hi_ref, bf16[256,128]{1,0:T(8,128)(2,1)S(1)} %get-tuple-element.7.row_lo_ref, f32[2,256,128]{2,1,0:T(8,128)S(1)} %get-tuple-element.8.cos_ref, ...), custom_call_target="tpu_custom_call" | custom-call | tf_op jit(solution)/shard_map/calibrate/pallas_call | solution.py:391
  63.4 8.4 %all-to-all-start.3 = ((f32[16,24,128]{2,1,0:T(8,128)}), f32[16,24,128]{2,1,0:T(8,128)S(1)}, u32[]{:S(2)}, u32[]{:S(2)}) async-start(f32[16,24,128]{2,1,0:T(8,128)} %bitcast.4), calls=%async_computation.3 | async-start | bytes 393216 | tf_op jit(solution)/shard_map/all_to_all | solution.py:399
  71.7 2.1 %collective-permute-start.2 = (s32[16,2]{1,0:T(8,128)S(1)}, s32[16,2]{1,0:T(8,128)S(1)}, u32[]{:S(2)}, u32[]{:S(2)}) collective-permute-start(s32[16,2]{1,0:T(8,128)S(1)} %copy.21.pair_ref), channel_id=1, source_target_pairs={{0,8},{8,0},{1,9},{9,1},{2,10},{10,2},{3,11},{11,3},{4,12},{12,4},... | collective-permute-start | bytes 392 | tf_op jit(solution)/shard_map/ppermute | solution.py:342
  73.9 0.9 collective-permute-done.2.other_ref
  74.8 7.3 %all-to-all-done.3 = f32[16,24,128]{2,1,0:T(8,128)S(1)} async-done(((f32[16,24,128]{2,1,0:T(8,128)}), f32[16,24,128]{2,1,0:T(8,128)S(1)}, u32[]{:S(2)}, u32[]{:S(2)}) %all-to-all-start.3) | async-done | bytes 196640 | tf_op jit(solution)/shard_map/all_to_all | solution.py:399
  82.1 1.9 %sum_terms.1 = f32[32,8,128]{2,1,0:T(8,128)} custom-call(s32[16,2]{1,0:T(8,128)S(1)} %copy.21.pair_ref, s32[16,2]{1,0:T(8,128)S(1)} %collective-permute-done.2.other_ref, f32[8,2,24,128]{3,2,1,0:T(8,128)S(1)} %bitcast.18), custom_call_target="tpu_custom_call" | custom-call | tf_op jit(solution)/shard_map/sum_terms/pallas_call | solution.py:407
  84.0 4.2 %all-to-all-start.4 = ((f32[32,8,128]{2,1,0:T(8,128)}), f32[32,8,128]{2,1,0:T(8,128)S(1)}, u32[]{:S(2)}, u32[]{:S(2)}) async-start(f32[32,8,128]{2,1,0:T(8,128)} %sum_terms.1), calls=%async_computation.4 | async-start | bytes 262144 | tf_op jit(solution)/shard_map/all_to_all | solution.py:415
  88.3 9.4 %all-to-all-done.4.msg_ref = f32[32,8,128]{2,1,0:T(8,128)S(1)} async-done(((f32[32,8,128]{2,1,0:T(8,128)}), f32[32,8,128]{2,1,0:T(8,128)S(1)}, u32[]{:S(2)}, u32[]{:S(2)}) %all-to-all-start.4) | async-done | bytes 131104 | tf_op jit(solution)/shard_map/all_to_all | solution.py:415
  98.3 5.0 %all-to-all-start.5 = ((f32[16,4,128]{2,1,0:T(4,128)}), f32[16,4,128]{2,1,0:T(4,128)S(1)}, u32[]{:S(2)}, u32[]{:S(2)}) async-start(f32[16,4,128]{2,1,0:T(4,128)} %bitcast.8), calls=%async_computation.5 | async-start | bytes 65536 | tf_op jit(solution)/shard_map/all_to_all | solution.py:425
  103.4 0.8 copy.25
  104.2 6.5 %all-to-all-done.5 = f32[16,4,128]{2,1,0:T(4,128)S(1)} async-done(((f32[16,4,128]{2,1,0:T(4,128)}), f32[16,4,128]{2,1,0:T(4,128)S(1)}, u32[]{:S(2)}, u32[]{:S(2)}) %all-to-all-start.5) | async-done | bytes 32800 | tf_op jit(solution)/shard_map/all_to_all | solution.py:425
  (37 shorter events, 4.3 us)
Async XLA Ops:
  0.6 17.1 %copy-start = (bf16[1,128,1024]{2,1,0:T(8,128)(2,1)S(1)}, bf16[1,128,1024]{2,1,0:T(8,128)(2,1)}, u32[]{:S(2)}) copy-start(bf16[1,128,1024]{2,1,0:T(8,128)(2,1)} %grid_ref.1) | copy-start | bytes 786436
  0.6 0.8 copy-start.3
  1.4 0.7 copy-start.8
  2.1 0.7 copy-start.10
  4.1 23.0 %all-to-all-start = ((f32[32,1,1152]{2,1,0:T(1,128)}), f32[32,1,1152]{2,1,0:T(1,128)S(1)}, u32[]{:S(2)}, u32[]{:S(2)}) async-start(f32[32,1,1152]{2,1,0:T(1,128)} %send_requests.1), calls=%async_computation | async-start | bytes 294912 | tf_op jit(solution)/shard_map/all_to_all | solution.py:355
  17.8 4.0 %collective-permute-start = (bf16[1,128,1024]{2,1,0:T(8,128)(2,1)S(1)}, bf16[1,128,1024]{2,1,0:T(8,128)(2,1)S(1)}, u32[]{:S(2)}, u32[]{:S(2)}) collective-permute-start(bf16[1,128,1024]{2,1,0:T(8,128)(2,1)S(1)} %copy-done), channel_id=1, source_target_pairs={{0,8},{8,0},{1,9},{9,1},{2,10},{10,2},{3,11},{11,3},{4,12},{12,4},... | collective-permute-start | bytes 786440 | tf_op jit(solution)/shard_map/ppermute | solution.py:342
  28.5 8.1 %copy-start.12 = (s32[16,2]{0,1:T(2,128)S(1)}, s32[16,2]{0,1:T(2,128)}, u32[]{:S(2)}) copy-start(s32[16,2]{0,1:T(2,128)} %param.16) | copy-start | bytes 388
  28.5 8.2 %copy-start.11 = (f32[8,16,2,16]{3,2,1,0:T(2,128)S(1)}, f32[8,16,2,16]{3,2,1,0:T(2,128)}, u32[]{:S(2)}) copy-start(f32[8,16,2,16]{3,2,1,0:T(2,128)} %param.14) | copy-start | bytes 49156
  28.5 14.1 %all-to-all-start.1 = ((bf16[32,32,128]{2,1,0:T(8,128)(2,1)}), bf16[32,32,128]{2,1,0:T(8,128)(2,1)S(1)}, u32[]{:S(2)}, u32[]{:S(2)}) async-start(bf16[32,32,128]{2,1,0:T(8,128)(2,1)} %reply_tiles.1), calls=%async_computation.1 | async-start | bytes 524288 | tf_op jit(solution)/shard_map/all_to_all | solution.py:377
  32.9 4.7 %collective-permute-start.1 = (f32[32,1,1152]{2,1,0:T(1,128)S(1)}, f32[32,1,1152]{2,1,0:T(1,128)S(1)}, u32[]{:S(2)}, u32[]{:S(2)}) collective-permute-start(f32[32,1,1152]{2,1,0:T(1,128)S(1)} %all-to-all-done.msg_ref.mine_ref), channel_id=1, source_target_pairs={{0,8},{8,0},{1,9},{9,1},{2,10},{10,2},{3,11},{11,3},{4,12},{12,4},... | collective-permute-start | bytes 442376 | tf_op jit(solution)/shard_map/ppermute | solution.py:342
  37.1 5.5 %copy-start.9 = (s32[16,1]{0,1:T(1,128)S(1)}, s32[16,1]{0,1:T(1,128)}, u32[]{:S(2)}) copy-start(s32[16,1]{0,1:T(1,128)} %param.17) | copy-start | bytes 196
  44.3 7.0 %copy-start.6 = (f32[2,16,16]{2,1,0:T(8,128)S(1)}, f32[2,16,16]{2,1,0:T(8,128)}, u32[]{:S(2)}) copy-start(f32[2,16,16]{2,1,0:T(8,128)} %uv_ref.1) | copy-start | bytes 6148
  44.3 7.0 %copy-start.7 = (f32[8,128]{1,0:T(8,128)S(1)}, f32[8,128]{1,0:T(8,128)}, u32[]{:S(2)}) copy-start(f32[8,128]{1,0:T(8,128)} %constant.20.clone.offs_ref) | copy-start | bytes 12292
  44.3 16.0 %copy-start.1 = (bf16[256,256]{1,0:T(8,128)(2,1)S(1)}, bf16[256,256]{1,0:T(8,128)(2,1)}, u32[]{:S(2)}) copy-start(bf16[256,256]{1,0:T(8,128)(2,1)} %constant.21.clone.cols_hi_ref) | copy-start | bytes 393220
  44.3 16.0 %copy-start.2 = (bf16[256,256]{1,0:T(8,128)(2,1)S(1)}, bf16[256,256]{1,0:T(8,128)(2,1)}, u32[]{:S(2)}) copy-start(bf16[256,256]{1,0:T(8,128)(2,1)} %constant.22.clone.cols_lo_ref) | copy-start | bytes 393220
  44.3 16.0 %copy-start.5 = (bf16[64,64]{1,0:T(8,128)(2,1)S(1)}, bf16[64,64]{1,0:T(8,128)(2,1)}, u32[]{:S(2)}) copy-start(bf16[64,64]{1,0:T(8,128)(2,1)} %constant.24.clone.rows_lo_ref) | copy-start | bytes 24580
  44.4 15.9 %all-to-all-start.2 = ((f32[8,56,128]{2,1,0:T(8,128)}), f32[8,56,128]{2,1,0:T(8,128)S(1)}, u32[]{:S(2)}, u32[]{:S(2)}) async-start(f32[8,56,128]{2,1,0:T(8,128)} %send_baselines.1), calls=%async_computation.2 | async-start | bytes 458752 | tf_op jit(solution)/shard_map/all_to_all | solution.py:389
  51.3 9.0 %copy-start.4 = (bf16[64,64]{1,0:T(8,128)(2,1)S(1)}, bf16[64,64]{1,0:T(8,128)(2,1)}, u32[]{:S(2)}) copy-start(bf16[64,64]{1,0:T(8,128)(2,1)} %constant.23.clone.rows_hi_ref) | copy-start | bytes 24580
  63.4 18.7 %all-to-all-start.3 = ((f32[16,24,128]{2,1,0:T(8,128)}), f32[16,24,128]{2,1,0:T(8,128)S(1)}, u32[]{:S(2)}, u32[]{:S(2)}) async-start(f32[16,24,128]{2,1,0:T(8,128)} %bitcast.4), calls=%async_computation.3 | async-start | bytes 393216 | tf_op jit(solution)/shard_map/all_to_all | solution.py:399
  71.7 3.1 %collective-permute-start.2 = (s32[16,2]{1,0:T(8,128)S(1)}, s32[16,2]{1,0:T(8,128)S(1)}, u32[]{:S(2)}, u32[]{:S(2)}) collective-permute-start(s32[16,2]{1,0:T(8,128)S(1)} %copy.21.pair_ref), channel_id=1, source_target_pairs={{0,8},{8,0},{1,9},{9,1},{2,10},{10,2},{3,11},{11,3},{4,12},{12,4},... | collective-permute-start | bytes 392 | tf_op jit(solution)/shard_map/ppermute | solution.py:342
  84.0 13.6 %all-to-all-start.4 = ((f32[32,8,128]{2,1,0:T(8,128)}), f32[32,8,128]{2,1,0:T(8,128)S(1)}, u32[]{:S(2)}, u32[]{:S(2)}) async-start(f32[32,8,128]{2,1,0:T(8,128)} %sum_terms.1), calls=%async_computation.4 | async-start | bytes 262144 | tf_op jit(solution)/shard_map/all_to_all | solution.py:415
  98.3 12.4 %all-to-all-start.5 = ((f32[16,4,128]{2,1,0:T(4,128)}), f32[16,4,128]{2,1,0:T(4,128)S(1)}, u32[]{:S(2)}, u32[]{:S(2)}) async-start(f32[16,4,128]{2,1,0:T(4,128)} %bitcast.8), calls=%async_computation.5 | async-start | bytes 65536 | tf_op jit(solution)/shard_map/all_to_all | solution.py:425

commit v4 on v3

--- a/solution.py
+++ b/solution.py
@@ -19,9 +19,9 @@
 BLD = 16
 TILES = 128
 SAMPLES = TIMES * CHANS
-MSG1 = PIX + 128
+MSG1 = 9
 MSG3 = 56
-MSG5 = 24
+MSG5 = 40
 f32 = jnp.float32
 bf16 = jnp.bfloat16
 GRAD_SCALE = SUB / math.sqrt(2.0 * BLD * NBL * CHANS * TIMES / NBL)
@@ -92,26 +92,40 @@
     return acc * z
 
 
-def send_requests(owner_ref, slot_ref, screen_ref, out_ref):
+def send_requests(owner_hbm, slot_hbm, screen_hbm, out_ref, owner_ref, slot_ref, screen_ref, sems):
+    copies = [
+        pltpu.make_async_copy(owner_hbm, owner_ref, sems.at[0]),
+        pltpu.make_async_copy(slot_hbm, slot_ref, sems.at[1]),
+        pltpu.make_async_copy(screen_hbm, screen_ref, sems.at[2]),
+    ]
+    for copy in copies:
+        copy.start()
+    for copy in copies:
+        copy.wait()
     c = lax.axis_index("ch")
-    subs = lax.broadcasted_iota(jnp.int32, (8, PIX), 0)
-    mine = jnp.sum(jnp.where(subs == c, screen_ref[0], 0.0), axis=0, keepdims=True)
-    out_ref[:, :, :PIX] = jnp.broadcast_to(mine.reshape(1, 1, PIX), (CHIPS, 1, PIX))
+    subs = lax.broadcasted_iota(jnp.int32, (8, 128), 0)
+    mine = jnp.zeros((8, 128), f32)
+    for j in range(8):
+        picked = jnp.where(subs == c, screen_ref[0, :, j * 128 : (j + 1) * 128], 0.0)
+        mine = jnp.where(subs == j, jnp.sum(picked, axis=0, keepdims=True), mine)
     rows = lax.broadcasted_iota(jnp.int32, (CHIPS, 128), 0)
     lanes = lax.broadcasted_iota(jnp.int32, (CHIPS, 128), 1)
-    holder = rows * 2 + lanes // 2
+    holder = jnp.where(lanes < 4, rows * 2 + lanes // 2, -1)
     count = lanes % 2
     req = jnp.zeros((CHIPS, 128), jnp.int32)
     for i in range(BLD):
-        hit = (holder == owner_ref[i]) & (lanes < 4)
+        hit = holder == owner_ref[i]
         req = jnp.where(hit & (count == 0), slot_ref[i] + 1, req)
-        count = count - hit.astype(jnp.int32)
-    out_ref[:, :, PIX:] = req.astype(f32).reshape(CHIPS, 1, 128)
+        count = jnp.where(hit, count - 1, count)
+    req = req.astype(f32)
+    for s in range(CHIPS):
+        out_ref[MSG1 * s : MSG1 * s + 8, :] = mine
+        out_ref[MSG1 * s + 8 : MSG1 * s + 9, :] = req[s : s + 1]
 
 
 def reply_tiles(msg_ref, grid_ref, other_ref, out_ref, scr_ref):
     core = lax.axis_index("core")
-    req = msg_ref[:, :, PIX:].reshape(CHIPS, 128).astype(jnp.int32)
+    req = msg_ref[pl.ds(8, CHIPS, stride=MSG1), :].astype(jnp.int32)
     lanes = lax.broadcasted_iota(jnp.int32, (CHIPS, 2 * TILES), 1) + 1
     picks = []
     for k in range(4):
@@ -141,9 +155,8 @@
         for e in range(2):
             at = 16 + (a * 2 + e) * 8
             s = pair_ref[i, e]
-            row = jnp.where(s % 2 == core, mine_ref[s // 2], other_ref[s // 2])
-            for j in range(8):
-                out_ref[d, at + j : at + j + 1, :] = row[:, j * 128 : j * 128 + 128]
+            rows = pl.ds(MSG1 * (s // 2), 8)
+            out_ref[d, at : at + 8, :] = jnp.where(s % 2 == core, mine_ref[rows, :], other_ref[rows, :])
     out_ref[:, 48:56, :] = seen_ref[...]
 
 
@@ -281,9 +294,7 @@
         seen = jnp.concatenate([msg_ref[k, 48:56, a * 32 : a * 32 + 32] for k in range(8)], axis=1)
         resid = vis * (1.0 / SUB) - seen
         for k in range(8):
-            part = resid[:, k * 32 : k * 32 + 32]
-            out_ref[k, 0, 16:24, a * 32 : a * 32 + 32] = part
-            out_ref[k, 1, 16:24, a * 32 : a * 32 + 32] = part
+            out_ref[k, 32:40, a * 32 : a * 32 + 32] = resid[:, k * 32 : k * 32 + 32]
         g = resid * (GRAD_SCALE / SUB)
         g_hi, g_lo = split2(g)
         g_pair = jnp.concatenate([g_hi.astype(f32), g_lo.astype(f32)], axis=0).T.astype(bf16)
@@ -304,30 +315,25 @@
         down = mat(lambda p: (d_re[p], d_im[p]))
         grads = [prod_h(prod(down, second), sky), h_prod(down, middle)]
         for e in range(2):
-            at = (a * 2 + e) * 4
+            at = (a * 2 + e) * 8
             for p in range(4):
                 re, im = grads[e][p // 2][p % 2]
-                out_ref[:, 0, at + p, :] = re
-                out_ref[:, 1, at + p, :] = im
-    out_ref[:, :, 16:24, 64:] = jnp.zeros((8, 2, 8, 64), f32)
-
-
-def sum_terms(pair_ref, other_ref, msg_ref, out_ref):
-    core = lax.axis_index("core")
-    half = lax.broadcasted_iota(jnp.int32, (8, 128), 0) // 4
+                out_ref[:, at + p, :] = re
+                out_ref[:, at + p + 4, :] = im
+    out_ref[:, 32:40, 64:] = jnp.zeros((8, 8, 64), f32)
+
+
+def sum_terms(pair_ref, msg_ref, out_ref):
     out_ref[...] = jnp.zeros_like(out_ref)
     for i in range(BLD):
         d, a = divmod(i, 2)
-        for k in range(2):
-            both = msg_ref[d, k, a * 8 : a * 8 + 8, :]
-            turned = pltpu.roll(both, 4, 0)
-            for e in range(2):
-                s = jnp.where(core == k, pair_ref[i, e], other_ref[i, e])
-                term = jnp.where(s % 2 == e, both, turned)
-                out_ref[s // 2] = out_ref[s // 2] + jnp.where(half == s % 2, term, 0.0)
-
-
-def sum_all(msg_ref, out_ref):
+        for e in range(2):
+            s = pair_ref[i, e]
+            at = (a * 2 + e) * 8
+            out_ref[s] = out_ref[s] + msg_ref[d, at : at + 8, :]
+
+
+def sum_chips(msg_ref, out_ref):
     total = jnp.sum(msg_ref[...], axis=0)
     for k in range(NCH):
         out_ref[k] = total
@@ -342,17 +348,23 @@
         return lax.ppermute(x, "core", [(0, 1), (1, 0)])
 
     other_grid = from_other_core(model_grid)
-    other_pairs = from_other_core(station_pairs)
-
+    outside = [pl.BlockSpec(memory_space=pltpu.HBM)] * 3
     msg1 = pl.pallas_call(
         send_requests,
-        out_shape=sds((CHIPS, 1, MSG1), f32),
-        in_specs=smem(2) + vmem(1),
-        out_specs=vmem(1)[0],
+        out_shape=sds((CHIPS * MSG1, 128), f32),
+        in_specs=outside,
+        out_specs=vmem(1)[0],
+        scratch_shapes=[
+            pltpu.SMEM((BLD,), jnp.int32),
+            pltpu.SMEM((BLD,), jnp.int32),
+            pltpu.VMEM((1, 8, PIX), f32),
+            pltpu.SemaphoreType.DMA((3,)),
+        ],
         compiler_params=params,
         name="send_requests",
-    )(owner, tile_slot, screens)
-    got1 = lax.all_to_all(msg1, "xz", 0, 0, tiled=True)
+    )(*[pltpu.with_memory_space_constraint(x, pltpu.HBM) for x in (owner, tile_slot, screens)])
+    got1 = lax.all_to_all(msg1.reshape(CHIPS, 1, MSG1 * 128), "xz", 0, 0, tiled=True)
+    got1 = got1.reshape(CHIPS * MSG1, 128)
     other1 = from_other_core(got1)
 
     table = sds((SAMPLES, 128), bf16)
@@ -390,40 +402,39 @@
 
     msg5 = pl.pallas_call(
         calibrate,
-        out_shape=sds((NCH, 2, MSG5, 128), f32),
+        out_shape=sds((NCH, MSG5, 128), f32),
         in_specs=vmem(9),
         out_specs=vmem(1)[0],
         compiler_params=params,
         name="calibrate",
     )(got3, *waves, *dft)
-    got5 = lax.all_to_all(msg5.reshape(2 * NCH, MSG5, 128), ("ch", "core"), 0, 0, tiled=True)
-    got5 = got5.reshape(NCH, 2, MSG5, 128)
-
-    core = lax.axis_index("core")
-    resid = jnp.where(core == 0, got5[:, 0, 16:24, :64], got5[:, 1, 16:24, :64])
-    resid = resid.reshape(NCH, 8, 2, 2, TIMES)
+    got5 = lax.all_to_all(msg5, "ch", 0, 0, tiled=True)
+
+    resid = got5[:, 32:40, :64].reshape(NCH, 8, 2, 2, TIMES)
     residual = resid.transpose(1, 4, 3, 0, 2).reshape(8, TIMES, 2, BLD)
 
     msg6 = pl.pallas_call(
         sum_terms,
-        out_shape=sds((CHIPS, 8, 128), f32),
-        in_specs=smem(2) + vmem(1),
+        out_shape=sds((NBL, 8, 128), f32),
+        in_specs=smem(1) + vmem(1),
         out_specs=vmem(1)[0],
         compiler_params=params,
         name="sum_terms",
-    )(station_pairs, other_pairs, got5)
-    got6 = lax.all_to_all(msg6, "xz", 0, 0, tiled=True)
+    )(station_pairs, got5)
+    got6 = lax.all_to_all(msg6.reshape(CHIPS, 16, 128), "xz", 0, 0, tiled=True)
 
     msg7 = pl.pallas_call(
-        sum_all,
-        out_shape=sds((NCH, 8, 128), f32),
+        sum_chips,
+        out_shape=sds((NCH, 16, 128), f32),
         in_specs=vmem(1),
         out_specs=vmem(1)[0],
         compiler_params=params,
-        name="sum_all",
+        name="sum_chips",
     )(got6)
-    got7 = lax.all_to_all(msg7.reshape(2 * NCH, 4, 128), ("ch", "core"), 0, 0, tiled=True)
-    return residual, got7.reshape(NCH, 8, 128).transpose(1, 0, 2).reshape(1, 8, PIX)
+    got7 = lax.all_to_all(msg7.reshape(2 * NCH, 8, 128), ("ch", "core"), 0, 0, tiled=True)
+    got7 = got7.reshape(NCH, 2, 8, 128)
+    screen_grad = (got7[:, 0] + got7[:, 1]).transpose(1, 0, 2).reshape(1, 8, PIX)
+    return residual, screen_grad
 
 
 def solution(mesh):

time: 112 us -> 106 us (0.946)
  blocking collectives: 0 us -> 26 us
  waiting for transfers between devices: 44.4 us -> 27.1 us
  starting transfers between devices: 51.3 us -> 40.9 us
  local copies, waits for them, and re-layouts: 4.15 us -> 1.44 us
  Pallas kernels: 10.7 us -> 8.89 us
    all_to_all x0 -> x2, blocking collectives: none -> 26 us  [the longest x1 15.4 us: per_device(): got6 = lax.all_to_all(msg6.reshape(CHIPS, 16, 128), 'xz', 0, 0, tiled=True)]
    all_to_all x4 -> x2, waiting for transfers between devices: 28.5 us -> 12.2 us  [the longest x1 6.89 us: per_device(): lax.all_to_all(msg7.reshape(2 * NCH, 8, 128), ('ch', 'core'), 0, 0, tiled...]
    all_to_all x4 -> x2, starting transfers between devices: 31.3 us -> 23 us  [the longest x1 13.7 us: per_device(): lax.all_to_all(msg1.reshape(CHIPS, 1, MSG1 * 128), 'xz', 0, 0, tiled=True)]
    unnamed x30 -> x23, local copies, waits for them, and re-layouts: 3.73 us -> 1.01 us
    ppermute x3 -> x2, starting transfers between devices: 8.68 us -> 6.56 us  [from_other_core(): return lax.ppermute(x, 'core', [(0, 1), (1, 0)])]
    pallas_call x4, Pallas kernels: 6.92 us -> 5.33 us  [the longest x1 2.36 us: per_device(): pl.pallas_call(calibrate, out_shape=sds((NCH, MSG5, 128), f32), in_specs=...]
    ppermute x3 -> x2, waiting for transfers between devices: 2.55 us -> 1.63 us  [from_other_core(): return lax.ppermute(x, 'core', [(0, 1), (1, 0)])]
  transfers between devices with their start and end apart: 9 -> 6, of which waited for: 9 -> 6; matrix products, arithmetic and copies ran while one was open for 1% -> 1% of each run, Pallas kernels for 1% -> 1%
where the time goes in v4:
time: 106 us
  starting transfers between devices  40.9 us (39%)
  waiting for transfers between devices  27.1 us (26%)
  blocking collectives  26 us (25%)
  Pallas kernels  8.89 us (8%)
  local copies, waits for them, and re-layouts  1.44 us (1%)
    all_to_all x1, blocking collectives, per_device(): got6 = lax.all_to_all(msg6.reshape(CHIPS, 16, 128), 'xz', 0, 0, tiled=True)  15.4 us
    all_to_all x1, starting transfers between devices, per_device(): lax.all_to_all(msg1.reshape(CHIPS, 1, MSG1 * 128), 'xz', 0, 0, tiled=True)  13.7 us
    all_to_all x1, blocking collectives, per_device(): got5 = lax.all_to_all(msg5, 'ch', 0, 0, tiled=True)  10.7 us
    all_to_all x1, starting transfers between devices, per_device(): lax.all_to_all(msg7.reshape(2 * NCH, 8, 128), ('ch', 'core'), 0, 0, tiled...  9.25 us
    all_to_all x1, waiting for transfers between devices, per_device(): got3 = lax.all_to_all(msg3, 'ch', 0, 0, tiled=True)  8.36 us
    all_to_all x1, starting transfers between devices, per_device(): got3 = lax.all_to_all(msg3, 'ch', 0, 0, tiled=True)  6.96 us
    all_to_all x1, waiting for transfers between devices, per_device(): lax.all_to_all(msg7.reshape(2 * NCH, 8, 128), ('ch', 'core'), 0, 0, tiled...  6.89 us
    ppermute x2, starting transfers between devices, from_other_core(): return lax.ppermute(x, 'core', [(0, 1), (1, 0)])  6.56 us
  transfers between devices with their start and end apart: 6, of which 6 were waited for; matrix products, arithmetic and copies ran while one was open for 1% of the time, Pallas kernels for 1%

profile of v4, /device:TPU:1, one launch (start us, length us, event | category | flops | bytes accessed | tf_op | source)
XLA Modules:
  0.0 105.8 jit_solution(9275365115049812215)
XLA Ops:
  0.6 1.6 %send_requests.1 = f32[288,128]{1,0:T(8,128)} custom-call(s32[16]{0:T(128)} %bitcast.34, s32[16]{0:T(128)} %slot_hbm.1, f32[1,8,1024]{2,1,0:T(8,128)} %screen_hbm.1), custom_call_target="tpu_custom_call" | custom-call | tf_op jit(solution)/shard_map/send_requests/pallas_call | solution.py:352
  2.2 13.7 %all-to-all-start = ((f32[32,1,1152]{2,1,0:T(1,128)}), f32[32,1,1152]{2,1,0:T(1,128)S(1)}, u32[]{:S(2)}, u32[]{:S(2)}) async-start(f32[32,1,1152]{2,1,0:T(1,128)} %bitcast.1), calls=%async_computation | async-start | bytes 294912 | tf_op jit(solution)/shard_map/all_to_all | solution.py:366
  16.0 2.9 %collective-permute-start = (bf16[1,128,1024]{2,1,0:T(8,128)(2,1)S(1)}, bf16[1,128,1024]{2,1,0:T(8,128)(2,1)S(1)}, u32[]{:S(2)}, u32[]{:S(2)}) collective-permute-start(bf16[1,128,1024]{2,1,0:T(8,128)(2,1)S(1)} %copy-done), channel_id=1, source_target_pairs={{0,8},{8,0},{1,9},{9,1},{2,10},{10,2},{3,11},{11,3},{4,12},{12,4},... | collective-permute-start | bytes 786440 | tf_op jit(solution)/shard_map/ppermute | solution.py:348
  18.8 1.1 %collective-permute-done.other_ref = bf16[1,128,1024]{2,1,0:T(8,128)(2,1)S(1)} collective-permute-done((bf16[1,128,1024]{2,1,0:T(8,128)(2,1)S(1)}, bf16[1,128,1024]{2,1,0:T(8,128)(2,1)S(1)}, u32[]{:S(2)}, u32[]{:S(2)}) %collective-permute-start) | collective-permute-done | bytes 262176 | tf_op jit(solution)/shard_map/ppermute | solution.py:348
  20.0 5.3 %all-to-all-done = f32[32,1,1152]{2,1,0:T(1,128)S(1)} async-done(((f32[32,1,1152]{2,1,0:T(1,128)}), f32[32,1,1152]{2,1,0:T(1,128)S(1)}, u32[]{:S(2)}, u32[]{:S(2)}) %all-to-all-start) | async-done | bytes 147488 | tf_op jit(solution)/shard_map/all_to_all | solution.py:366
  25.2 1.2 %reply_tiles.1 = bf16[32,32,128]{2,1,0:T(8,128)(2,1)} custom-call(f32[288,128]{1,0:T(8,128)S(1)} %bitcast.29, bf16[1,128,1024]{2,1,0:T(8,128)(2,1)S(1)} %copy-done, bf16[1,128,1024]{2,1,0:T(8,128)(2,1)S(1)} %collective-permute-done.other_ref), custom_call_target="tpu_custom_call" | custom-call | tf_op jit(solution)/shard_map/reply_tiles/pallas_call | solution.py:380
  26.5 4.4 %all-to-all-start.1 = ((bf16[32,32,128]{2,1,0:T(8,128)(2,1)}), bf16[32,32,128]{2,1,0:T(8,128)(2,1)S(1)}, u32[]{:S(2)}, u32[]{:S(2)}) async-start(bf16[32,32,128]{2,1,0:T(8,128)(2,1)} %reply_tiles.1), calls=%async_computation.1 | async-start | bytes 524288 | tf_op jit(solution)/shard_map/all_to_all | solution.py:389
  30.9 3.7 %collective-permute-start.1 = (f32[288,128]{1,0:T(8,128)S(1)}, f32[288,128]{1,0:T(8,128)S(1)}, u32[]{:S(2)}, u32[]{:S(2)}) collective-permute-start(f32[288,128]{1,0:T(8,128)S(1)} %bitcast.30), channel_id=1, source_target_pairs={{0,8},{8,0},{1,9},{9,1},{2,10},{10,2},{3,11},{11,3},{4,12},{12,4},... | collective-permute-start | bytes 442376 | tf_op jit(solution)/shard_map/ppermute | solution.py:348
  34.9 0.2 reshape.46
  35.1 0.5 collective-permute-done.1.other_ref
  35.6 5.0 %all-to-all-done.1 = bf16[32,32,128]{2,1,0:T(8,128)(2,1)S(1)} async-done(((bf16[32,32,128]{2,1,0:T(8,128)(2,1)}), bf16[32,32,128]{2,1,0:T(8,128)(2,1)S(1)}, u32[]{:S(2)}, u32[]{:S(2)}) %all-to-all-start.1) | async-done | bytes 262176 | tf_op jit(solution)/shard_map/all_to_all | solution.py:389
  40.5 1.7 %send_baselines.1 = f32[8,56,128]{2,1,0:T(8,128)} custom-call(s32[16]{0:T(128)S(1)} %bitcast.35, s32[16,2]{1,0:T(8,128)S(1)} %copy.31.pair_ref, bf16[64,16,128]{2,1,0:T(8,128)(2,1)S(1)} %bitcast.33, f32[288,128]{1,0:T(8,128)S(1)} %bitcast.31, f32[288,128]{1,0:T(8,128)S(1)} %collective-permute-done.1.other_ref, f32[8,8,128]{2,1,0:T(8,128)S(1)} %pad.4.seen_ref), custom_call_target="tpu_custom_call" | custom-call | tf_op jit(solution)/shard_map/send_baselines/pallas_call | solution.py:393
  42.3 7.0 %all-to-all-start.2 = ((f32[8,56,128]{2,1,0:T(8,128)}), f32[8,56,128]{2,1,0:T(8,128)S(1)}, u32[]{:S(2)}, u32[]{:S(2)}) async-start(f32[8,56,128]{2,1,0:T(8,128)} %send_baselines.1), calls=%async_computation.2 | async-start | bytes 458752 | tf_op jit(solution)/shard_map/all_to_all | solution.py:401
  49.3 0.6 phases.1
  49.9 8.4 %all-to-all-done.2.msg_ref = f32[8,56,128]{2,1,0:T(8,128)S(1)} async-done(((f32[8,56,128]{2,1,0:T(8,128)}), f32[8,56,128]{2,1,0:T(8,128)S(1)}, u32[]{:S(2)}, u32[]{:S(2)}) %all-to-all-start.2) | async-done | bytes 229408 | tf_op jit(solution)/shard_map/all_to_all | solution.py:401
  58.3 2.4 %calibrate.1 = f32[8,40,128]{2,1,0:T(8,128)S(1)} custom-call(f32[8,56,128]{2,1,0:T(8,128)S(1)} %all-to-all-done.2.msg_ref, bf16[256,128]{1,0:T(8,128)(2,1)S(1)} %get-tuple-element.6.row_hi_ref, bf16[256,128]{1,0:T(8,128)(2,1)S(1)} %get-tuple-element.7.row_lo_ref, f32[2,256,128]{2,1,0:T(8,128)S(1)} %get-tuple-element.8.cos_ref, ...), custom_call_target="tpu_custom_call" | custom-call | tf_op jit(solution)/shard_map/calibrate/pallas_call | solution.py:403
  60.6 10.7 %all_to_all.30.msg_ref = f32[8,40,128]{2,1,0:T(8,128)S(1)} all-to-all(f32[8,40,128]{2,1,0:T(8,128)S(1)} %calibrate.1), channel_id=1, replica_groups=mesh['xz'=32,'core'=2,'ch'=8] {'ch'}, dimensions={0} | all-to-all | bytes 327680 | tf_op jit(solution)/shard_map/all_to_all | solution.py:411
  71.3 0.8 sum_terms.1
  72.1 15.4 %all_to_all.31.msg_ref = f32[32,16,128]{2,1,0:T(8,128)S(1)} all-to-all(f32[32,16,128]{2,1,0:T(8,128)S(1)} %bitcast.32), channel_id=1, replica_groups=mesh['xz'=32,'core'=2,'ch'=8] {'xz'}, dimensions={0} | all-to-all | bytes 524288 | tf_op jit(solution)/shard_map/all_to_all | solution.py:424
  87.4 0.7 sum_chips.1
  88.1 9.3 %all-to-all-start.5 = ((f32[16,8,128]{2,1,0:T(8,128)}), f32[16,8,128]{2,1,0:T(8,128)S(1)}, u32[]{:S(2)}, u32[]{:S(2)}) async-start(f32[16,8,128]{2,1,0:T(8,128)} %bitcast.9), calls=%async_computation.5 | async-start | bytes 131072 | tf_op jit(solution)/shard_map/all_to_all | solution.py:434
  97.5 0.8 copy.36
  98.3 6.9 %all-to-all-done.5 = f32[16,8,128]{2,1,0:T(8,128)S(1)} async-done(((f32[16,8,128]{2,1,0:T(8,128)}), f32[16,8,128]{2,1,0:T(8,128)S(1)}, u32[]{:S(2)}, u32[]{:S(2)}) %all-to-all-start.5) | async-done | bytes 65568 | tf_op jit(solution)/shard_map/all_to_all | solution.py:434
  105.2 0.6 fusion.1
  (27 shorter events, 0.5 us)
Async XLA Ops:
  0.6 15.3 %copy-start = (bf16[1,128,1024]{2,1,0:T(8,128)(2,1)S(1)}, bf16[1,128,1024]{2,1,0:T(8,128)(2,1)}, u32[]{:S(2)}) copy-start(bf16[1,128,1024]{2,1,0:T(8,128)(2,1)} %grid_ref.1) | copy-start | bytes 786436
  2.2 23.0 %all-to-all-start = ((f32[32,1,1152]{2,1,0:T(1,128)}), f32[32,1,1152]{2,1,0:T(1,128)S(1)}, u32[]{:S(2)}, u32[]{:S(2)}) async-start(f32[32,1,1152]{2,1,0:T(1,128)} %bitcast.1), calls=%async_computation | async-start | bytes 294912 | tf_op jit(solution)/shard_map/all_to_all | solution.py:366
  16.0 4.0 %collective-permute-start = (bf16[1,128,1024]{2,1,0:T(8,128)(2,1)S(1)}, bf16[1,128,1024]{2,1,0:T(8,128)(2,1)S(1)}, u32[]{:S(2)}, u32[]{:S(2)}) collective-permute-start(bf16[1,128,1024]{2,1,0:T(8,128)(2,1)S(1)} %copy-done), channel_id=1, source_target_pairs={{0,8},{8,0},{1,9},{9,1},{2,10},{10,2},{3,11},{11,3},{4,12},{12,4},... | collective-permute-start | bytes 786440 | tf_op jit(solution)/shard_map/ppermute | solution.py:348
  26.5 8.1 %copy-start.9 = (s32[16,2]{0,1:T(2,128)S(1)}, s32[16,2]{0,1:T(2,128)}, u32[]{:S(2)}) copy-start(s32[16,2]{0,1:T(2,128)} %param.16) | copy-start | bytes 388
  26.5 8.2 %copy-start.8 = (f32[8,16,2,16]{3,2,1,0:T(2,128)S(1)}, f32[8,16,2,16]{3,2,1,0:T(2,128)}, u32[]{:S(2)}) copy-start(f32[8,16,2,16]{3,2,1,0:T(2,128)} %param.14) | copy-start | bytes 49156
  26.5 14.1 %all-to-all-start.1 = ((bf16[32,32,128]{2,1,0:T(8,128)(2,1)}), bf16[32,32,128]{2,1,0:T(8,128)(2,1)S(1)}, u32[]{:S(2)}, u32[]{:S(2)}) async-start(bf16[32,32,128]{2,1,0:T(8,128)(2,1)} %reply_tiles.1), calls=%async_computation.1 | async-start | bytes 524288 | tf_op jit(solution)/shard_map/all_to_all | solution.py:389
  30.9 4.7 %collective-permute-start.1 = (f32[288,128]{1,0:T(8,128)S(1)}, f32[288,128]{1,0:T(8,128)S(1)}, u32[]{:S(2)}, u32[]{:S(2)}) collective-permute-start(f32[288,128]{1,0:T(8,128)S(1)} %bitcast.30), channel_id=1, source_target_pairs={{0,8},{8,0},{1,9},{9,1},{2,10},{10,2},{3,11},{11,3},{4,12},{12,4},... | collective-permute-start | bytes 442376 | tf_op jit(solution)/shard_map/ppermute | solution.py:348
  35.1 5.5 %copy-start.7 = (s32[16,1]{0,1:T(1,128)S(1)}, s32[16,1]{0,1:T(1,128)}, u32[]{:S(2)}) copy-start(s32[16,1]{0,1:T(1,128)} %param.17) | copy-start | bytes 196
  42.3 7.0 %copy-start.5 = (f32[2,16,16]{2,1,0:T(8,128)S(1)}, f32[2,16,16]{2,1,0:T(8,128)}, u32[]{:S(2)}) copy-start(f32[2,16,16]{2,1,0:T(8,128)} %uv_ref.1) | copy-start | bytes 6148
  42.3 7.0 %copy-start.6 = (f32[8,128]{1,0:T(8,128)S(1)}, f32[8,128]{1,0:T(8,128)}, u32[]{:S(2)}) copy-start(f32[8,128]{1,0:T(8,128)} %constant.13.clone.offs_ref) | copy-start | bytes 12292
  42.3 16.0 %copy-start.1 = (bf16[256,256]{1,0:T(8,128)(2,1)S(1)}, bf16[256,256]{1,0:T(8,128)(2,1)}, u32[]{:S(2)}) copy-start(bf16[256,256]{1,0:T(8,128)(2,1)} %constant.15.clone.cols_lo_ref) | copy-start | bytes 393220
  42.3 16.0 %copy-start.2 = (bf16[256,256]{1,0:T(8,128)(2,1)S(1)}, bf16[256,256]{1,0:T(8,128)(2,1)}, u32[]{:S(2)}) copy-start(bf16[256,256]{1,0:T(8,128)(2,1)} %constant.14.clone.cols_hi_ref) | copy-start | bytes 393220
  42.3 16.0 %copy-start.4 = (bf16[64,64]{1,0:T(8,128)(2,1)S(1)}, bf16[64,64]{1,0:T(8,128)(2,1)}, u32[]{:S(2)}) copy-start(bf16[64,64]{1,0:T(8,128)(2,1)} %constant.16.clone.rows_hi_ref) | copy-start | bytes 24580
  42.3 15.9 %all-to-all-start.2 = ((f32[8,56,128]{2,1,0:T(8,128)}), f32[8,56,128]{2,1,0:T(8,128)S(1)}, u32[]{:S(2)}, u32[]{:S(2)}) async-start(f32[8,56,128]{2,1,0:T(8,128)} %send_baselines.1), calls=%async_computation.2 | async-start | bytes 458752 | tf_op jit(solution)/shard_map/all_to_all | solution.py:401
  49.3 9.0 %copy-start.3 = (bf16[64,64]{1,0:T(8,128)(2,1)S(1)}, bf16[64,64]{1,0:T(8,128)(2,1)}, u32[]{:S(2)}) copy-start(bf16[64,64]{1,0:T(8,128)(2,1)} %constant.17.clone.rows_lo_ref) | copy-start | bytes 24580
  88.1 17.1 %all-to-all-start.5 = ((f32[16,8,128]{2,1,0:T(8,128)}), f32[16,8,128]{2,1,0:T(8,128)S(1)}, u32[]{:S(2)}, u32[]{:S(2)}) async-start(f32[16,8,128]{2,1,0:T(8,128)} %bitcast.9), calls=%async_computation.5 | async-start | bytes 131072 | tf_op jit(solution)/shard_map/all_to_all | solution.py:434

commit v5 on v4

--- a/solution.py
+++ b/solution.py
@@ -59,13 +59,10 @@
     cp, sp = c[np.ix_(order, order)], s[np.ix_(order, order)]
     rows = np.block([[cp, -sp], [sp, cp]]) / SUB
     x = (np.arange(SUB) - SUB // 2) / SUB
-    xl = np.tile(x[order], 4)
-    xm = np.tile(x, 4)
-    offs = np.zeros((8, 128))
-    offs[0], offs[1] = xl, xm
-    offs[2] = np.tile(np.repeat([0.0, 0.25], SUB), 2)
+    places = np.zeros((2, SUB, 128))
+    places[0], places[1] = x[order][:, None], x[:, None]
     cols, rows = cols.astype(np.float32), rows.astype(np.float32)
-    return *np_split(cols), *np_split(rows), offs.astype(np.float32)
+    return *np_split(cols), *np_split(rows), places.astype(np.float32)
 
 
 def split2(x):
@@ -123,7 +120,7 @@
         out_ref[MSG1 * s + 8 : MSG1 * s + 9, :] = req[s : s + 1]
 
 
-def reply_tiles(msg_ref, grid_ref, other_ref, out_ref, scr_ref):
+def reply_tiles(msg_ref, grid_ref, other_ref, _, out_ref, scr_ref):
     core = lax.axis_index("core")
     req = msg_ref[pl.ds(8, CHIPS, stride=MSG1), :].astype(jnp.int32)
     lanes = lax.broadcasted_iota(jnp.int32, (CHIPS, 2 * TILES), 1) + 1
@@ -142,21 +139,18 @@
     out_ref[...] = scr_ref[...].reshape(CHIPS, 32, 128).astype(bf16)
 
 
-def send_baselines(owner_ref, pair_ref, tiles_ref, mine_ref, other_ref, seen_ref, out_ref):
+def send_baselines(place_ref, pair_ref, tiles_ref, mine_ref, other_ref, seen_ref, out_ref, rows_ref):
     core = lax.axis_index("core")
+    rows_ref[: CHIPS * MSG1, :] = mine_ref[...]
+    rows_ref[CHIPS * MSG1 :, :] = other_ref[...]
     for i in range(BLD):
         d, a = divmod(i, 2)
-        owner = owner_ref[i]
-        rank = jnp.int32(0)
-        for e in range(i):
-            rank = rank + (owner_ref[e] == owner).astype(jnp.int32)
-        both = tiles_ref[owner].astype(f32)
-        out_ref[d, a * 8 : a * 8 + 8, :] = jnp.where(rank == 0, both[:8], both[8:])
+        out_ref[d, a * 8 : a * 8 + 8, :] = tiles_ref[place_ref[i]].astype(f32)
         for e in range(2):
             at = 16 + (a * 2 + e) * 8
             s = pair_ref[i, e]
-            rows = pl.ds(MSG1 * (s // 2), 8)
-            out_ref[d, at : at + 8, :] = jnp.where(s % 2 == core, mine_ref[rows, :], other_ref[rows, :])
+            row = MSG1 * (s // 2 + CHIPS * lax.rem(s + core, 2))
+            out_ref[d, at : at + 8, :] = rows_ref[pl.ds(row, 8), :]
     out_ref[:, 48:56, :] = seen_ref[...]
 
 
@@ -209,31 +203,42 @@
     return [[cadd(cmulc(b[0][c], a[0][r]), cmulc(b[1][c], a[1][r])) for c in range(2)] for r in range(2)]
 
 
-def phases(uv_ref, offs_ref, row_hi_ref, row_lo_ref, cos_ref, sin_ref):
+def phases(owner_ref, uv_ref, places_ref, factor_ref, hi_ref, lo_ref, cos_ref, sin_ref, at_ref):
+    owners = [owner_ref[i] for i in range(BLD)]
+    for i in range(BLD):
+        rank = jnp.int32(0)
+        for e in range(i):
+            rank = jnp.where(owners[e] == owners[i], 1, rank)
+        at_ref[i] = owners[i] * 2 + rank
+
     mine = lax.axis_index("ch") * 2
-    lane16 = lax.broadcasted_iota(jnp.int32, (TIMES, BLD), 1)
-    lane128 = lax.broadcasted_iota(jnp.int32, (TIMES, 128), 1)
-
-    def column(axis, a):
-        picked = jnp.where(lane16 == mine + a, uv_ref[axis], 0.0)
-        return jnp.broadcast_to(jnp.sum(picked, axis=1, keepdims=True), (TIMES, 128))
-
-    def turns(base):
-        return jnp.concatenate([base * (1.0 + c / (2.0 * CHANS)) for c in range(CHANS)], axis=0)
-
-    u_both = jnp.where(lane128 < 64, column(0, 0), column(0, 1))
-    e_row = cos_turns(turns(u_both * offs_ref[0:1, :]) - offs_ref[2:3, :])
-    row_hi_ref[...], row_lo_ref[...] = split2(e_row)
+    sub = lax.broadcasted_iota(jnp.int32, (BLD, TIMES), 0)
+
+    def turns(axis, a):
+        rows = uv_ref[axis].T
+        picked = jnp.sum(jnp.where(sub == mine + a, rows, 0.0), axis=0, keepdims=True)
+        times = jnp.concatenate([picked] * CHANS, axis=1) * factor_ref[0:1, :]
+        place = jnp.concatenate([places_ref[axis], places_ref[axis]], axis=1)
+        return times * place
+
     for a in range(2):
-        t = turns(column(1, a) * offs_ref[1:2, :])
+        t = turns(0, a)
         cos_ref[a] = cos_turns(t)
         sin_ref[a] = cos_turns(t - 0.25)
+        t = turns(1, a)
+        wave = jnp.concatenate([cos_turns(t), cos_turns(t - 0.25)], axis=0)
+        hi_ref[64 * a : 64 * a + 64, :], lo_ref[64 * a : 64 * a + 64, :] = split2(wave)
+
+
+def turn_lanes(x, amount):
+    amount = amount % 128
+    return x if amount == 0 else pltpu.roll(x, amount, 1)
 
 
 def calibrate(
     msg_ref,
-    row_hi_ref,
-    row_lo_ref,
+    wave_hi_ref,
+    wave_lo_ref,
     cos_ref,
     sin_ref,
     cols_hi_ref,
@@ -242,7 +247,6 @@
     rows_lo_ref,
     out_ref,
 ):
-    row_hi, row_lo = row_hi_ref[...], row_lo_ref[...]
     planes = [[msg_ref[k, a * 8 : a * 8 + 8, :] for k in range(8)] for a in range(2)]
     grid_re = jnp.concatenate([to_rows(planes[a][:4]) for a in range(2)], axis=0)
     grid_im = jnp.concatenate([to_rows(planes[a][4:]) for a in range(2)], axis=0)
@@ -258,10 +262,8 @@
     )
     image = dot3(rows_hi_ref[...], rows_lo_ref[...], *split2(stacked))
 
-    lane_re = lax.broadcasted_iota(jnp.int32, (8, 256), 1) // SUB
-    sub = lax.broadcasted_iota(jnp.int32, (8, 256), 0)
-    ones = jnp.where(lane_re == sub, 1.0, 0.0).astype(bf16)
-    zeros = jnp.zeros((64, 256), f32)
+    lane = lax.broadcasted_iota(jnp.int32, (8, 128), 1)
+    low = lane < SUB
 
     for a in range(2):
         sky_re = to_flat(image[:32, a * 128 : a * 128 + 128])
@@ -275,44 +277,55 @@
         first, second = jones(0), jones(1)
         middle = prod(first, sky)
         model = prod_h(middle, second)
-        m_re = to_rows([model[p // 2][p % 2][0] for p in range(4)])
-        m_im = to_rows([model[p // 2][p % 2][1] for p in range(4)])
-        block = jnp.concatenate(
-            [jnp.concatenate([m_re, m_im], axis=1), jnp.concatenate([m_im, -m_re], axis=1)], axis=0
-        )
-        block = jnp.concatenate([block, zeros] if a == 0 else [zeros, block], axis=0)
-        t = dot3(row_hi, row_lo, *split2(block))
-        t_re, t_im = t[:, :128], t[:, 128:]
-        cos_col, sin_col = cos_ref[a], sin_ref[a]
-        w = jnp.concatenate(
-            [cos_col * t_re + sin_col * t_im, cos_col * t_im - sin_col * t_re], axis=1
-        )
-        w_hi, w_lo = split2(w)
-        last = (((1,), (1,)), ((), ()))
-        vis = lax.dot_general(ones, w_hi, last, preferred_element_type=f32)
-        vis = vis + lax.dot_general(ones, w_lo, last, preferred_element_type=f32)
+        left_re, left_im = [], []
+        for p in range(4):
+            re, im = model[p // 2][p % 2]
+            for q in range(4):
+                at = -SUB * q
+                left_re.append(jnp.where(low, turn_lanes(re, at), turn_lanes(im, at + SUB)))
+                left_im.append(jnp.where(low, turn_lanes(im, at), -turn_lanes(re, at + SUB)))
+        left = jnp.concatenate(left_re + left_im, axis=0)[:, :64]
+        left_hi, left_lo = split2(left)
+        wave = slice(64 * a, 64 * a + 64)
+        t = dot3(left_hi, left_lo, wave_hi_ref[wave, :], wave_lo_ref[wave, :])
+        cos_row, sin_row = cos_ref[a], sin_ref[a]
+        vis_re, vis_im = [], []
+        for p in range(4):
+            t_re, t_im = t[p * 32 : p * 32 + 32], t[128 + p * 32 : 160 + p * 32]
+            vis_re.append(jnp.sum(cos_row * t_re + sin_row * t_im, axis=0, keepdims=True))
+            vis_im.append(jnp.sum(cos_row * t_im - sin_row * t_re, axis=0, keepdims=True))
+        vis = jnp.concatenate(vis_re + vis_im, axis=0)
         seen = jnp.concatenate([msg_ref[k, 48:56, a * 32 : a * 32 + 32] for k in range(8)], axis=1)
         resid = vis * (1.0 / SUB) - seen
         for k in range(8):
             out_ref[k, 32:40, a * 32 : a * 32 + 32] = resid[:, k * 32 : k * 32 + 32]
         g = resid * (GRAD_SCALE / SUB)
-        g_hi, g_lo = split2(g)
-        g_pair = jnp.concatenate([g_hi.astype(f32), g_lo.astype(f32)], axis=0).T.astype(bf16)
-        wide = dot(g_pair, jnp.concatenate([ones, ones], axis=0))
-        g_re, g_im = wide[:, :128], wide[:, 128:]
-        d_t = jnp.concatenate(
-            [cos_col * g_re - sin_col * g_im, sin_col * g_re + cos_col * g_im], axis=1
-        )
-        d_hi, d_lo = split2(d_t)
-
-        def over_samples(e, d):
-            return lax.dot_general(e, d, (((0,), (0,)), ((), ())), preferred_element_type=f32)
-
-        d_block = over_samples(row_hi, d_hi) + (over_samples(row_hi, d_lo) + over_samples(row_lo, d_hi))
-        d_block = d_block[a * 64 : a * 64 + 64]
-        d_re = to_flat(d_block[:32, :128] - d_block[32:, 128:])
-        d_im = to_flat(d_block[:32, 128:] + d_block[32:, :128])
-        down = mat(lambda p: (d_re[p], d_im[p]))
+        d_re, d_im = [], []
+        for p in range(4):
+            g_re, g_im = g[p : p + 1], g[p + 4 : p + 5]
+            d_re.append(cos_row * g_re - sin_row * g_im)
+            d_im.append(sin_row * g_re + cos_row * g_im)
+        d_hi, d_lo = split2(jnp.concatenate(d_re + d_im, axis=0))
+
+        def over_samples(d, e):
+            return lax.dot_general(d, e, (((1,), (1,)), ((), ())), preferred_element_type=f32)
+
+        wave_hi = wave_hi_ref[...]
+        back = over_samples(d_hi, wave_hi) + (over_samples(d_hi, wave_lo_ref[...]) + over_samples(d_lo, wave_hi))
+        down = []
+        for p in range(4):
+            re, im = None, None
+            for q in range(4):
+                at = p * 32 + q * 8
+                b_re, b_im = back[at : at + 8], back[128 + at : 136 + at]
+                to = SUB * q - 64 * a
+                part_re = turn_lanes(b_re, to) - turn_lanes(b_im, to - SUB)
+                part_im = turn_lanes(b_re, to - SUB) + turn_lanes(b_im, to)
+                here = lane // SUB == q
+                re = part_re if q == 0 else jnp.where(here, part_re, re)
+                im = part_im if q == 0 else jnp.where(here, part_im, im)
+            down.append((re, im))
+        down = [down[:2], down[2:]]
         grads = [prod_h(prod(down, second), sky), h_prod(down, middle)]
         for e in range(2):
             at = (a * 2 + e) * 8
@@ -340,7 +353,7 @@
 
 
 def per_device(model_grid, screens, observed, uv_coords, station_pairs, tile_owner, tile_slot):
-    *dft, offs = tables()
+    *dft, places = tables()
     sds = jax.ShapeDtypeStruct
     owner = tile_owner.reshape(BLD)
 
@@ -367,27 +380,27 @@
     got1 = got1.reshape(CHIPS * MSG1, 128)
     other1 = from_other_core(got1)
 
-    table = sds((SAMPLES, 128), bf16)
-    waves = pl.pallas_call(
+    factor = np.tile(np.repeat(1.0 + np.arange(CHANS) / (2.0 * CHANS), TIMES), (8, 1))
+    table, wave = sds((128, SAMPLES), bf16), sds((2, SUB, SAMPLES), f32)
+    *waves, place = pl.pallas_call(
         phases,
-        out_shape=(table, table, sds((2, SAMPLES, 128), f32), sds((2, SAMPLES, 128), f32)),
-        in_specs=vmem(2),
-        out_specs=vmem(4),
+        out_shape=(table, table, wave, wave, sds((BLD,), jnp.int32)),
+        in_specs=smem(1) + vmem(3),
+        out_specs=vmem(4) + smem(1),
         compiler_params=params,
         name="phases",
-    )(uv_coords, offs)
+    )(owner, uv_coords, places, factor.astype(np.float32))
 
     tiles = pl.pallas_call(
         reply_tiles,
         out_shape=sds((CHIPS, 32, 128), bf16),
-        in_specs=vmem(3),
+        in_specs=vmem(3) + [pl.BlockSpec(memory_space=pl.ANY)],
         out_specs=vmem(1)[0],
         scratch_shapes=[pltpu.VMEM((CHIPS * 32, 128), f32)],
         compiler_params=params,
         name="reply_tiles",
-    )(got1, model_grid, other_grid)
-    got2 = lax.all_to_all(tiles, "xz", 0, 0, tiled=True).reshape(NBL, 16, 128)
-
+    )(got1, model_grid, other_grid, waves[0])
+    got2 = lax.all_to_all(tiles, "xz", 0, 0, tiled=True).reshape(2 * NBL, 8, 128)
     seen = observed.reshape(8, TIMES, 2, NCH, 2).transpose(3, 0, 4, 2, 1).reshape(NCH, 8, 64)
     seen = jnp.pad(seen, ((0, 0), (0, 0), (0, 64)))
     msg3 = pl.pallas_call(
@@ -395,9 +408,10 @@
         out_shape=sds((NCH, MSG3, 128), f32),
         in_specs=smem(2) + vmem(4),
         out_specs=vmem(1)[0],
+        scratch_shapes=[pltpu.VMEM((2 * CHIPS * MSG1, 128), f32)],
         compiler_params=params,
         name="send_baselines",
-    )(owner, station_pairs, got2, got1, other1, seen)
+    )(place, station_pairs, got2, got1, other1, seen)
     got3 = lax.all_to_all(msg3, "ch", 0, 0, tiled=True)
 
     msg5 = pl.pallas_call(

time: 106 us -> 105 us (level)
  blocking collectives: 26 us -> 42 us
  waiting for transfers between devices: 27.1 us -> 17.6 us
  starting transfers between devices: 40.9 us -> 33.9 us
    all_to_all x0 -> x1, blocking collectives: none -> 15.7 us  [per_device(): got3 = lax.all_to_all(msg3, 'ch', 0, 0, tiled=True)]
    all_to_all x2 -> x1, waiting for transfers between devices: 13.3 us -> 5.38 us  [per_device(): lax.all_to_all(tiles, 'xz', 0, 0, tiled=True).reshape(2 * NBL, 8, 128)]
    all_to_all x2 -> x1, starting transfers between devices: 11.4 us -> 4.8 us  [per_device(): lax.all_to_all(tiles, 'xz', 0, 0, tiled=True).reshape(2 * NBL, 8, 128)]
    ppermute x2, waiting for transfers between devices: 1.63 us -> 0.5 us  [from_other_core(): return lax.ppermute(x, 'core', [(0, 1), (1, 0)])]
  transfers between devices with their start and end apart: 6 -> 5, of which waited for: 6 -> 4; matrix products, arithmetic and copies ran while one was open for 1% -> 1% of each run, Pallas kernels for 1% -> 1%
where the time goes in v5:
time: 105 us
  blocking collectives  42 us (40%)
  starting transfers between devices  33.9 us (32%)
  waiting for transfers between devices  17.6 us (17%)
  Pallas kernels  8.47 us (8%)
  local copies, waits for them, and re-layouts  1.46 us (1%)
    all_to_all x1, blocking collectives, per_device(): got3 = lax.all_to_all(msg3, 'ch', 0, 0, tiled=True)  15.7 us
    all_to_all x1, blocking collectives, per_device(): got6 = lax.all_to_all(msg6.reshape(CHIPS, 16, 128), 'xz', 0, 0, tiled=True)  15.6 us
    all_to_all x1, starting transfers between devices, per_device(): lax.all_to_all(msg1.reshape(CHIPS, 1, MSG1 * 128), 'xz', 0, 0, tiled=True)  13.9 us
    all_to_all x1, blocking collectives, per_device(): got5 = lax.all_to_all(msg5, 'ch', 0, 0, tiled=True)  10.7 us
    all_to_all x1, starting transfers between devices, per_device(): lax.all_to_all(msg7.reshape(2 * NCH, 8, 128), ('ch', 'core'), 0, 0, tiled...  9.05 us
    all_to_all x1, waiting for transfers between devices, per_device(): lax.all_to_all(msg7.reshape(2 * NCH, 8, 128), ('ch', 'core'), 0, 0, tiled...  6.89 us
    ppermute x2, starting transfers between devices, from_other_core(): return lax.ppermute(x, 'core', [(0, 1), (1, 0)])  6.15 us
    all_to_all x1, waiting for transfers between devices, per_device(): lax.all_to_all(tiles, 'xz', 0, 0, tiled=True).reshape(2 * NBL, 8, 128)  5.38 us
  transfers between devices with their start and end apart: 5, of which 4 were waited for; matrix products, arithmetic and copies ran while one was open for 1% of the time, Pallas kernels for 1%

profile of v5, /device:TPU:1, one launch (start us, length us, event | category | flops | bytes accessed | tf_op | source)
XLA Modules:
  0.0 104.9 jit_solution(3827422831425251856)
XLA Ops:
  0.6 1.6 %send_requests.1 = f32[288,128]{1,0:T(8,128)} custom-call(s32[16]{0:T(128)} %bitcast.34, s32[16]{0:T(128)} %slot_hbm.1, f32[1,8,1024]{2,1,0:T(8,128)} %screen_hbm.1), custom_call_target="tpu_custom_call" | custom-call | tf_op jit(solution)/shard_map/send_requests/pallas_call | solution.py:365
  2.3 13.9 %all-to-all-start = ((f32[32,1,1152]{2,1,0:T(1,128)}), f32[32,1,1152]{2,1,0:T(1,128)S(1)}, u32[]{:S(2)}, u32[]{:S(2)}) async-start(f32[32,1,1152]{2,1,0:T(1,128)} %bitcast.1), calls=%async_computation | async-start | bytes 294912 | tf_op jit(solution)/shard_map/all_to_all | solution.py:379
  16.1 2.9 %collective-permute-start = (bf16[1,128,1024]{2,1,0:T(8,128)(2,1)S(1)}, bf16[1,128,1024]{2,1,0:T(8,128)(2,1)S(1)}, u32[]{:S(2)}, u32[]{:S(2)}) collective-permute-start(bf16[1,128,1024]{2,1,0:T(8,128)(2,1)S(1)} %copy-done), channel_id=1, source_target_pairs={{0,8},{8,0},{1,9},{9,1},{2,10},{10,2},{3,11},{11,3},{4,12},{12,4},... | collective-permute-start | bytes 786440 | tf_op jit(solution)/shard_map/ppermute | solution.py:361
  19.1 1.5 %phases.1 = (bf16[128,256]{1,0:T(8,128)(2,1)S(1)}, bf16[128,256]{1,0:T(8,128)(2,1)S(1)}, f32[2,32,256]{2,1,0:T(8,128)S(1)}, f32[2,32,256]{2,1,0:T(8,128)S(1)}, s32[16]{0:T(128)S(1)}) custom-call(s32[16]{0:T(128)S(1)} %bitcast.35, f32[2,16,16]{2,1,0:T(8,128)S(1)} %copy-done.4, f32[2,32,128]{2,1,0:T(8,128)S(1)} %copy-done.3, f32[8,256]{1,0:T(8,128)S(1)} %copy-done.7), custom_call_target="tpu_custom_call" | custom-call | tf_op jit(solution)/shard_map/phases/pallas_call | solution.py:385
  20.6 4.8 %all-to-all-done = f32[32,1,1152]{2,1,0:T(1,128)S(1)} async-done(((f32[32,1,1152]{2,1,0:T(1,128)}), f32[32,1,1152]{2,1,0:T(1,128)S(1)}, u32[]{:S(2)}, u32[]{:S(2)}) %all-to-all-start) | async-done | bytes 147488 | tf_op jit(solution)/shard_map/all_to_all | solution.py:379
  25.4 1.2 %reply_tiles.1 = bf16[32,32,128]{2,1,0:T(8,128)(2,1)} custom-call(f32[288,128]{1,0:T(8,128)S(1)} %bitcast.29, bf16[1,128,1024]{2,1,0:T(8,128)(2,1)S(1)} %copy-done, bf16[1,128,1024]{2,1,0:T(8,128)(2,1)S(1)} %collective-permute-done.other_ref, bf16[128,256]{1,0:T(8,128)(2,1)S(1)} %get-tuple-element.8._.wave_hi_ref), custom_call_target="tpu_custom_call" | custom-call | tf_op jit(solution)/shard_map/reply_tiles/pallas_call | solution.py:394
  26.7 4.8 %all-to-all-start.1 = ((bf16[32,32,128]{2,1,0:T(8,128)(2,1)}), bf16[32,32,128]{2,1,0:T(8,128)(2,1)S(1)}, u32[]{:S(2)}, u32[]{:S(2)}) async-start(bf16[32,32,128]{2,1,0:T(8,128)(2,1)} %reply_tiles.1), calls=%async_computation.1 | async-start | bytes 524288 | tf_op jit(solution)/shard_map/all_to_all | solution.py:403
  31.5 3.3 %collective-permute-start.1 = (f32[288,128]{1,0:T(8,128)S(1)}, f32[288,128]{1,0:T(8,128)S(1)}, u32[]{:S(2)}, u32[]{:S(2)}) collective-permute-start(f32[288,128]{1,0:T(8,128)S(1)} %bitcast.30), channel_id=1, source_target_pairs={{0,8},{8,0},{1,9},{9,1},{2,10},{10,2},{3,11},{11,3},{4,12},{12,4},... | collective-permute-start | bytes 442376 | tf_op jit(solution)/shard_map/ppermute | solution.py:361
  34.9 0.1 copy.30
  35.1 0.2 reshape.46
  35.3 0.5 collective-permute-done.1.other_ref
  35.7 5.4 %all-to-all-done.1 = bf16[32,32,128]{2,1,0:T(8,128)(2,1)S(1)} async-done(((bf16[32,32,128]{2,1,0:T(8,128)(2,1)}), bf16[32,32,128]{2,1,0:T(8,128)(2,1)S(1)}, u32[]{:S(2)}, u32[]{:S(2)}) %all-to-all-start.1) | async-done | bytes 262176 | tf_op jit(solution)/shard_map/all_to_all | solution.py:403
  41.1 0.9 send_baselines.1
  42.1 15.7 %all_to_all.30.msg_ref = f32[8,56,128]{2,1,0:T(8,128)S(1)} all-to-all(f32[8,56,128]{2,1,0:T(8,128)S(1)} %send_baselines.1), channel_id=1, replica_groups=mesh['xz'=32,'core'=2,'ch'=8] {'ch'}, dimensions={0} | all-to-all | bytes 458752 | tf_op jit(solution)/shard_map/all_to_all | solution.py:415
  57.9 1.8 %calibrate.1 = f32[8,40,128]{2,1,0:T(8,128)S(1)} custom-call(f32[8,56,128]{2,1,0:T(8,128)S(1)} %all_to_all.30.msg_ref, bf16[128,256]{1,0:T(8,128)(2,1)S(1)} %get-tuple-element.8._.wave_hi_ref, bf16[128,256]{1,0:T(8,128)(2,1)S(1)} %get-tuple-element.9.wave_lo_ref, f32[2,32,256]{2,1,0:T(8,128)S(1)} %get-tuple-element.10.cos_ref, ...), custom_call_target="tpu_custom_call" | custom-call | tf_op jit(solution)/shard_map/calibrate/pallas_call | solution.py:417
  59.7 10.7 %all_to_all.31.msg_ref = f32[8,40,128]{2,1,0:T(8,128)S(1)} all-to-all(f32[8,40,128]{2,1,0:T(8,128)S(1)} %calibrate.1), channel_id=1, replica_groups=mesh['xz'=32,'core'=2,'ch'=8] {'ch'}, dimensions={0} | all-to-all | bytes 327680 | tf_op jit(solution)/shard_map/all_to_all | solution.py:425
  70.4 0.8 sum_terms.1
  71.1 15.6 %all_to_all.32.msg_ref = f32[32,16,128]{2,1,0:T(8,128)S(1)} all-to-all(f32[32,16,128]{2,1,0:T(8,128)S(1)} %bitcast.32), channel_id=1, replica_groups=mesh['xz'=32,'core'=2,'ch'=8] {'xz'}, dimensions={0} | all-to-all | bytes 524288 | tf_op jit(solution)/shard_map/all_to_all | solution.py:438
  86.7 0.7 sum_chips.1
  87.4 9.1 %all-to-all-start.5 = ((f32[16,8,128]{2,1,0:T(8,128)}), f32[16,8,128]{2,1,0:T(8,128)S(1)}, u32[]{:S(2)}, u32[]{:S(2)}) async-start(f32[16,8,128]{2,1,0:T(8,128)} %bitcast.9), calls=%async_computation.5 | async-start | bytes 131072 | tf_op jit(solution)/shard_map/all_to_all | solution.py:448
  96.4 0.1 reshape.47
  96.6 0.8 copy.37
  97.4 6.9 %all-to-all-done.5 = f32[16,8,128]{2,1,0:T(8,128)S(1)} async-done(((f32[16,8,128]{2,1,0:T(8,128)}), f32[16,8,128]{2,1,0:T(8,128)S(1)}, u32[]{:S(2)}, u32[]{:S(2)}) %all-to-all-start.5) | async-done | bytes 65568 | tf_op jit(solution)/shard_map/all_to_all | solution.py:448
  104.3 0.6 fusion.1
  (28 shorter events, 0.3 us)
Async XLA Ops:
  0.6 15.5 %copy-start = (bf16[1,128,1024]{2,1,0:T(8,128)(2,1)S(1)}, bf16[1,128,1024]{2,1,0:T(8,128)(2,1)}, u32[]{:S(2)}) copy-start(bf16[1,128,1024]{2,1,0:T(8,128)(2,1)} %grid_ref.1) | copy-start | bytes 786436
  2.2 16.8 %copy-start.3 = (f32[2,32,128]{2,1,0:T(8,128)S(1)}, f32[2,32,128]{2,1,0:T(8,128)}, u32[]{:S(2)}) copy-start(f32[2,32,128]{2,1,0:T(8,128)} %constant.15.clone.places_ref) | copy-start | bytes 98308
  2.2 16.8 %copy-start.4 = (f32[2,16,16]{2,1,0:T(8,128)S(1)}, f32[2,16,16]{2,1,0:T(8,128)}, u32[]{:S(2)}) copy-start(f32[2,16,16]{2,1,0:T(8,128)} %uv_ref.1) | copy-start | bytes 6148
  2.2 16.8 %copy-start.7 = (f32[8,256]{1,0:T(8,128)S(1)}, f32[8,256]{1,0:T(8,128)}, u32[]{:S(2)}) copy-start(f32[8,256]{1,0:T(8,128)} %constant.16.clone.factor_ref) | copy-start | bytes 24580
  2.2 16.8 %copy-start.8 = (s32[16,1]{0,1:T(1,128)S(1)}, s32[16,1]{0,1:T(1,128)}, u32[]{:S(2)}) copy-start(s32[16,1]{0,1:T(1,128)} %param.18) | copy-start | bytes 196
  2.3 23.2 %all-to-all-start = ((f32[32,1,1152]{2,1,0:T(1,128)}), f32[32,1,1152]{2,1,0:T(1,128)S(1)}, u32[]{:S(2)}, u32[]{:S(2)}) async-start(f32[32,1,1152]{2,1,0:T(1,128)} %bitcast.1), calls=%async_computation | async-start | bytes 294912 | tf_op jit(solution)/shard_map/all_to_all | solution.py:379
  16.1 4.4 %collective-permute-start = (bf16[1,128,1024]{2,1,0:T(8,128)(2,1)S(1)}, bf16[1,128,1024]{2,1,0:T(8,128)(2,1)S(1)}, u32[]{:S(2)}, u32[]{:S(2)}) collective-permute-start(bf16[1,128,1024]{2,1,0:T(8,128)(2,1)S(1)} %copy-done), channel_id=1, source_target_pairs={{0,8},{8,0},{1,9},{9,1},{2,10},{10,2},{3,11},{11,3},{4,12},{12,4},... | collective-permute-start | bytes 786440 | tf_op jit(solution)/shard_map/ppermute | solution.py:361
  26.7 8.1 %copy-start.10 = (s32[16,2]{0,1:T(2,128)S(1)}, s32[16,2]{0,1:T(2,128)}, u32[]{:S(2)}) copy-start(s32[16,2]{0,1:T(2,128)} %param.17) | copy-start | bytes 388
  26.7 8.2 %copy-start.9 = (f32[8,16,2,16]{3,2,1,0:T(2,128)S(1)}, f32[8,16,2,16]{3,2,1,0:T(2,128)}, u32[]{:S(2)}) copy-start(f32[8,16,2,16]{3,2,1,0:T(2,128)} %param.15) | copy-start | bytes 49156
  26.7 14.5 %all-to-all-start.1 = ((bf16[32,32,128]{2,1,0:T(8,128)(2,1)}), bf16[32,32,128]{2,1,0:T(8,128)(2,1)S(1)}, u32[]{:S(2)}, u32[]{:S(2)}) async-start(bf16[32,32,128]{2,1,0:T(8,128)(2,1)} %reply_tiles.1), calls=%async_computation.1 | async-start | bytes 524288 | tf_op jit(solution)/shard_map/all_to_all | solution.py:403
  31.5 4.3 %collective-permute-start.1 = (f32[288,128]{1,0:T(8,128)S(1)}, f32[288,128]{1,0:T(8,128)S(1)}, u32[]{:S(2)}, u32[]{:S(2)}) collective-permute-start(f32[288,128]{1,0:T(8,128)S(1)} %bitcast.30), channel_id=1, source_target_pairs={{0,8},{8,0},{1,9},{9,1},{2,10},{10,2},{3,11},{11,3},{4,12},{12,4},... | collective-permute-start | bytes 442376 | tf_op jit(solution)/shard_map/ppermute | solution.py:361
  42.1 15.8 %copy-start.1 = (bf16[256,256]{1,0:T(8,128)(2,1)S(1)}, bf16[256,256]{1,0:T(8,128)(2,1)}, u32[]{:S(2)}) copy-start(bf16[256,256]{1,0:T(8,128)(2,1)} %constant.17.clone.cols_hi_ref) | copy-start | bytes 393220
  42.1 15.8 %copy-start.2 = (bf16[256,256]{1,0:T(8,128)(2,1)S(1)}, bf16[256,256]{1,0:T(8,128)(2,1)}, u32[]{:S(2)}) copy-start(bf16[256,256]{1,0:T(8,128)(2,1)} %constant.18.clone.cols_lo_ref) | copy-start | bytes 393220
  42.1 15.8 %copy-start.5 = (bf16[64,64]{1,0:T(8,128)(2,1)S(1)}, bf16[64,64]{1,0:T(8,128)(2,1)}, u32[]{:S(2)}) copy-start(bf16[64,64]{1,0:T(8,128)(2,1)} %constant.19.clone.rows_hi_ref) | copy-start | bytes 24580
  42.1 15.8 %copy-start.6 = (bf16[64,64]{1,0:T(8,128)(2,1)S(1)}, bf16[64,64]{1,0:T(8,128)(2,1)}, u32[]{:S(2)}) copy-start(bf16[64,64]{1,0:T(8,128)(2,1)} %constant.20.clone.rows_lo_ref) | copy-start | bytes 24580
  87.4 16.9 %all-to-all-start.5 = ((f32[16,8,128]{2,1,0:T(8,128)}), f32[16,8,128]{2,1,0:T(8,128)S(1)}, u32[]{:S(2)}, u32[]{:S(2)}) async-start(f32[16,8,128]{2,1,0:T(8,128)} %bitcast.9), calls=%async_computation.5 | async-start | bytes 131072 | tf_op jit(solution)/shard_map/all_to_all | solution.py:448

commit v6 on v5

--- a/solution.py
+++ b/solution.py
@@ -19,6 +19,8 @@
 BLD = 16
 TILES = 128
 SAMPLES = TIMES * CHANS
+RING = (0, 4, 1, 5, 2, 6, 3, 7)
+TURN = (0, 2, 4, 6, 1, 3, 5, 7)
 MSG1 = 9
 MSG3 = 56
 MSG5 = 40
@@ -144,14 +146,15 @@
     rows_ref[: CHIPS * MSG1, :] = mine_ref[...]
     rows_ref[CHIPS * MSG1 :, :] = other_ref[...]
     for i in range(BLD):
-        d, a = divmod(i, 2)
+        d, a = TURN[i // 2], i % 2
         out_ref[d, a * 8 : a * 8 + 8, :] = tiles_ref[place_ref[i]].astype(f32)
         for e in range(2):
             at = 16 + (a * 2 + e) * 8
             s = pair_ref[i, e]
             row = MSG1 * (s // 2 + CHIPS * lax.rem(s + core, 2))
             out_ref[d, at : at + 8, :] = rows_ref[pl.ds(row, 8), :]
-    out_ref[:, 48:56, :] = seen_ref[...]
+    for c in range(NCH):
+        out_ref[TURN[c], 48:56, :] = seen_ref[c]
 
 
 def blocks_swap(four):
@@ -247,7 +250,7 @@
     rows_lo_ref,
     out_ref,
 ):
-    planes = [[msg_ref[k, a * 8 : a * 8 + 8, :] for k in range(8)] for a in range(2)]
+    planes = [[msg_ref[TURN[k], a * 8 : a * 8 + 8, :] for k in range(8)] for a in range(2)]
     grid_re = jnp.concatenate([to_rows(planes[a][:4]) for a in range(2)], axis=0)
     grid_im = jnp.concatenate([to_rows(planes[a][4:]) for a in range(2)], axis=0)
     grid = jnp.concatenate([grid_re, grid_im], axis=1)
@@ -272,7 +275,7 @@
 
         def jones(e):
             at = 16 + (a * 2 + e) * 8
-            return mat(lambda p: (msg_ref[p, at : at + 8, :], msg_ref[p + 4, at : at + 8, :]))
+            return mat(lambda p: (msg_ref[TURN[p], at : at + 8, :], msg_ref[TURN[p + 4], at : at + 8, :]))
 
         first, second = jones(0), jones(1)
         middle = prod(first, sky)
@@ -295,10 +298,11 @@
             vis_re.append(jnp.sum(cos_row * t_re + sin_row * t_im, axis=0, keepdims=True))
             vis_im.append(jnp.sum(cos_row * t_im - sin_row * t_re, axis=0, keepdims=True))
         vis = jnp.concatenate(vis_re + vis_im, axis=0)
-        seen = jnp.concatenate([msg_ref[k, 48:56, a * 32 : a * 32 + 32] for k in range(8)], axis=1)
+        seen = jnp.concatenate([msg_ref[c, 48:56, a * 32 : a * 32 + 32] for c in TURN], axis=1)
         resid = vis * (1.0 / SUB) - seen
         for k in range(8):
-            out_ref[k, 32:40, a * 32 : a * 32 + 32] = resid[:, k * 32 : k * 32 + 32]
+            h, l = divmod(TURN[k], 2)
+            out_ref[h, l, 32:40, a * 32 : a * 32 + 32] = resid[:, k * 32 : k * 32 + 32]
         g = resid * (GRAD_SCALE / SUB)
         d_re, d_im = [], []
         for p in range(4):
@@ -331,15 +335,16 @@
             at = (a * 2 + e) * 8
             for p in range(4):
                 re, im = grads[e][p // 2][p % 2]
-                out_ref[:, at + p, :] = re
-                out_ref[:, at + p + 4, :] = im
-    out_ref[:, 32:40, 64:] = jnp.zeros((8, 8, 64), f32)
+                for l in range(2):
+                    out_ref[:, l, at + p, :] = re[4 * l : 4 * l + 4]
+                    out_ref[:, l, at + p + 4, :] = im[4 * l : 4 * l + 4]
+    out_ref[:, :, 32:40, 64:] = jnp.zeros((4, 2, 8, 64), f32)
 
 
 def sum_terms(pair_ref, msg_ref, out_ref):
     out_ref[...] = jnp.zeros_like(out_ref)
     for i in range(BLD):
-        d, a = divmod(i, 2)
+        d, a = TURN[i // 2], i % 2
         for e in range(2):
             s = pair_ref[i, e]
             at = (a * 2 + e) * 8
@@ -412,20 +417,21 @@
         compiler_params=params,
         name="send_baselines",
     )(place, station_pairs, got2, got1, other1, seen)
-    got3 = lax.all_to_all(msg3, "ch", 0, 0, tiled=True)
+    got3 = lax.all_to_all(msg3, "ch", 0, 0, tiled=True, axis_index_groups=[RING])
 
     msg5 = pl.pallas_call(
         calibrate,
-        out_shape=sds((NCH, MSG5, 128), f32),
+        out_shape=sds((NCH // 2, 2, MSG5, 128), f32),
         in_specs=vmem(9),
         out_specs=vmem(1)[0],
         compiler_params=params,
         name="calibrate",
     )(got3, *waves, *dft)
-    got5 = lax.all_to_all(msg5, "ch", 0, 0, tiled=True)
-
-    resid = got5[:, 32:40, :64].reshape(NCH, 8, 2, 2, TIMES)
-    residual = resid.transpose(1, 4, 3, 0, 2).reshape(8, TIMES, 2, BLD)
+    msg5 = msg5.reshape(NCH, MSG5, 128)
+    got5 = lax.all_to_all(msg5, "ch", 0, 0, tiled=True, axis_index_groups=[RING])
+
+    resid = got5[:, 32:40, :64].reshape(NCH // 2, 2, 8, 2, 2, TIMES)
+    residual = resid.transpose(2, 5, 4, 1, 0, 3).reshape(8, TIMES, 2, BLD)
 
     msg6 = pl.pallas_call(
         sum_terms,

time: 105 us -> 103 us (0.981)
  blocking collectives: 42 us -> 39.7 us
    all_to_all x2, blocking collectives: 26.4 us -> 23.9 us  [the longest x1 13.7 us: per_device(): lax.all_to_all(msg3, 'ch', 0, 0, tiled=True, axis_index_groups=[RING])]
where the time goes in v6:
time: 103 us
  blocking collectives  39.7 us (39%)
  starting transfers between devices  34.1 us (33%)
  waiting for transfers between devices  17.6 us (17%)
  Pallas kernels  8.45 us (8%)
  local copies, waits for them, and re-layouts  1.46 us (1%)
    all_to_all x1, blocking collectives, per_device(): got6 = lax.all_to_all(msg6.reshape(CHIPS, 16, 128), 'xz', 0, 0, tiled=True)  15.8 us
    all_to_all x1, starting transfers between devices, per_device(): lax.all_to_all(msg1.reshape(CHIPS, 1, MSG1 * 128), 'xz', 0, 0, tiled=True)  13.9 us
    all_to_all x1, blocking collectives, per_device(): lax.all_to_all(msg3, 'ch', 0, 0, tiled=True, axis_index_groups=[RING])  13.7 us
    all_to_all x1, blocking collectives, per_device(): lax.all_to_all(msg5, 'ch', 0, 0, tiled=True, axis_index_groups=[RING])  10.2 us
    all_to_all x1, starting transfers between devices, per_device(): lax.all_to_all(msg7.reshape(2 * NCH, 8, 128), ('ch', 'core'), 0, 0, tiled...  9.31 us
    all_to_all x1, waiting for transfers between devices, per_device(): lax.all_to_all(msg7.reshape(2 * NCH, 8, 128), ('ch', 'core'), 0, 0, tiled...  6.89 us
    ppermute x2, starting transfers between devices, from_other_core(): return lax.ppermute(x, 'core', [(0, 1), (1, 0)])  6.15 us
    all_to_all x1, waiting for transfers between devices, per_device(): lax.all_to_all(tiles, 'xz', 0, 0, tiled=True).reshape(2 * NBL, 8, 128)  5.38 us
  transfers between devices with their start and end apart: 5, of which 4 were waited for; matrix products, arithmetic and copies ran while one was open for 1% of the time, Pallas kernels for 1%

profile of v6, /device:TPU:1, one launch (start us, length us, event | category | flops | bytes accessed | tf_op | source)
XLA Modules:
  0.0 102.8 jit_solution(18191152187713694974)
XLA Ops:
  0.6 1.6 %send_requests.1 = f32[288,128]{1,0:T(8,128)} custom-call(s32[16]{0:T(128)} %bitcast.36, s32[16]{0:T(128)} %slot_hbm.1, f32[1,8,1024]{2,1,0:T(8,128)} %screen_hbm.1), custom_call_target="tpu_custom_call" | custom-call | tf_op jit(solution)/shard_map/send_requests/pallas_call | solution.py:370
  2.3 13.9 %all-to-all-start = ((f32[32,1,1152]{2,1,0:T(1,128)}), f32[32,1,1152]{2,1,0:T(1,128)S(1)}, u32[]{:S(2)}, u32[]{:S(2)}) async-start(f32[32,1,1152]{2,1,0:T(1,128)} %bitcast.1), calls=%async_computation | async-start | bytes 294912 | tf_op jit(solution)/shard_map/all_to_all | solution.py:384
  16.1 2.9 %collective-permute-start = (bf16[1,128,1024]{2,1,0:T(8,128)(2,1)S(1)}, bf16[1,128,1024]{2,1,0:T(8,128)(2,1)S(1)}, u32[]{:S(2)}, u32[]{:S(2)}) collective-permute-start(bf16[1,128,1024]{2,1,0:T(8,128)(2,1)S(1)} %copy-done), channel_id=1, source_target_pairs={{0,8},{8,0},{1,9},{9,1},{2,10},{10,2},{3,11},{11,3},{4,12},{12,4},... | collective-permute-start | bytes 786440 | tf_op jit(solution)/shard_map/ppermute | solution.py:366
  19.1 1.5 %phases.1 = (bf16[128,256]{1,0:T(8,128)(2,1)S(1)}, bf16[128,256]{1,0:T(8,128)(2,1)S(1)}, f32[2,32,256]{2,1,0:T(8,128)S(1)}, f32[2,32,256]{2,1,0:T(8,128)S(1)}, s32[16]{0:T(128)S(1)}) custom-call(s32[16]{0:T(128)S(1)} %bitcast.37, f32[2,16,16]{2,1,0:T(8,128)S(1)} %copy-done.4, f32[2,32,128]{2,1,0:T(8,128)S(1)} %copy-done.3, f32[8,256]{1,0:T(8,128)S(1)} %copy-done.7), custom_call_target="tpu_custom_call" | custom-call | tf_op jit(solution)/shard_map/phases/pallas_call | solution.py:390
  20.6 4.8 %all-to-all-done = f32[32,1,1152]{2,1,0:T(1,128)S(1)} async-done(((f32[32,1,1152]{2,1,0:T(1,128)}), f32[32,1,1152]{2,1,0:T(1,128)S(1)}, u32[]{:S(2)}, u32[]{:S(2)}) %all-to-all-start) | async-done | bytes 147488 | tf_op jit(solution)/shard_map/all_to_all | solution.py:384
  25.4 1.2 %reply_tiles.1 = bf16[32,32,128]{2,1,0:T(8,128)(2,1)} custom-call(f32[288,128]{1,0:T(8,128)S(1)} %bitcast.30, bf16[1,128,1024]{2,1,0:T(8,128)(2,1)S(1)} %copy-done, bf16[1,128,1024]{2,1,0:T(8,128)(2,1)S(1)} %collective-permute-done.other_ref, bf16[128,256]{1,0:T(8,128)(2,1)S(1)} %get-tuple-element.8._.wave_hi_ref), custom_call_target="tpu_custom_call" | custom-call | tf_op jit(solution)/shard_map/reply_tiles/pallas_call | solution.py:399
  26.7 4.8 %all-to-all-start.1 = ((bf16[32,32,128]{2,1,0:T(8,128)(2,1)}), bf16[32,32,128]{2,1,0:T(8,128)(2,1)S(1)}, u32[]{:S(2)}, u32[]{:S(2)}) async-start(bf16[32,32,128]{2,1,0:T(8,128)(2,1)} %reply_tiles.1), calls=%async_computation.1 | async-start | bytes 524288 | tf_op jit(solution)/shard_map/all_to_all | solution.py:408
  31.5 3.3 %collective-permute-start.1 = (f32[288,128]{1,0:T(8,128)S(1)}, f32[288,128]{1,0:T(8,128)S(1)}, u32[]{:S(2)}, u32[]{:S(2)}) collective-permute-start(f32[288,128]{1,0:T(8,128)S(1)} %bitcast.31), channel_id=1, source_target_pairs={{0,8},{8,0},{1,9},{9,1},{2,10},{10,2},{3,11},{11,3},{4,12},{12,4},... | collective-permute-start | bytes 442376 | tf_op jit(solution)/shard_map/ppermute | solution.py:366
  34.9 0.1 copy.30
  35.1 0.2 reshape.49
  35.3 0.5 collective-permute-done.1.other_ref
  35.7 5.4 %all-to-all-done.1 = bf16[32,32,128]{2,1,0:T(8,128)(2,1)S(1)} async-done(((bf16[32,32,128]{2,1,0:T(8,128)(2,1)}), bf16[32,32,128]{2,1,0:T(8,128)(2,1)S(1)}, u32[]{:S(2)}, u32[]{:S(2)}) %all-to-all-start.1) | async-done | bytes 262176 | tf_op jit(solution)/shard_map/all_to_all | solution.py:408
  41.1 0.9 send_baselines.1
  42.1 13.7 %all_to_all.30.msg_ref = f32[8,56,128]{2,1,0:T(8,128)S(1)} all-to-all(f32[8,56,128]{2,1,0:T(8,128)S(1)} %send_baselines.1), channel_id=1, replica_groups={{0,4,1,5,2,6,3,7},{8,12,9,13,10,14,11,15},{16,20,17,21,18,22,19,23},{24..., dimensions={0} | all-to-all | bytes 458752 | tf_op jit(solution)/shard_map/all_to_all | solution.py:420
  55.9 1.8 %calibrate.1 = f32[4,2,40,128]{3,2,1,0:T(8,128)S(1)} custom-call(f32[8,56,128]{2,1,0:T(8,128)S(1)} %all_to_all.30.msg_ref, bf16[128,256]{1,0:T(8,128)(2,1)S(1)} %get-tuple-element.8._.wave_hi_ref, bf16[128,256]{1,0:T(8,128)(2,1)S(1)} %get-tuple-element.9.wave_lo_ref, f32[2,32,256]{2,1,0:T(8,128)S(1)} %get-tuple-element.10.cos_ref, ...), custom_call_target="tpu_custom_call" | custom-call | tf_op jit(solution)/shard_map/calibrate/pallas_call | solution.py:422
  57.7 10.2 %all_to_all.31.msg_ref = f32[8,40,128]{2,1,0:T(8,128)S(1)} all-to-all(f32[8,40,128]{2,1,0:T(8,128)S(1)} %bitcast.35), channel_id=1, replica_groups={{0,4,1,5,2,6,3,7},{8,12,9,13,10,14,11,15},{16,20,17,21,18,22,19,23},{24..., dimensions={0} | all-to-all | bytes 327680 | tf_op jit(solution)/shard_map/all_to_all | solution.py:431
  67.8 0.8 sum_terms.1
  68.6 15.8 %all_to_all.32.msg_ref = f32[32,16,128]{2,1,0:T(8,128)S(1)} all-to-all(f32[32,16,128]{2,1,0:T(8,128)S(1)} %bitcast.33), channel_id=1, replica_groups=mesh['xz'=32,'core'=2,'ch'=8] {'xz'}, dimensions={0} | all-to-all | bytes 524288 | tf_op jit(solution)/shard_map/all_to_all | solution.py:444
  84.4 0.7 sum_chips.1
  85.0 9.3 %all-to-all-start.5 = ((f32[16,8,128]{2,1,0:T(8,128)}), f32[16,8,128]{2,1,0:T(8,128)S(1)}, u32[]{:S(2)}, u32[]{:S(2)}) async-start(f32[16,8,128]{2,1,0:T(8,128)} %bitcast.10), calls=%async_computation.5 | async-start | bytes 131072 | tf_op jit(solution)/shard_map/all_to_all | solution.py:454
  94.4 0.1 reshape.51
  94.5 0.8 copy.37
  95.3 6.9 %all-to-all-done.5 = f32[16,8,128]{2,1,0:T(8,128)S(1)} async-done(((f32[16,8,128]{2,1,0:T(8,128)}), f32[16,8,128]{2,1,0:T(8,128)S(1)}, u32[]{:S(2)}, u32[]{:S(2)}) %all-to-all-start.5) | async-done | bytes 65568 | tf_op jit(solution)/shard_map/all_to_all | solution.py:454
  102.2 0.6 fusion.1
  (28 shorter events, 0.3 us)
Async XLA Ops:
  0.6 15.5 %copy-start = (bf16[1,128,1024]{2,1,0:T(8,128)(2,1)S(1)}, bf16[1,128,1024]{2,1,0:T(8,128)(2,1)}, u32[]{:S(2)}) copy-start(bf16[1,128,1024]{2,1,0:T(8,128)(2,1)} %grid_ref.1) | copy-start | bytes 786436
  2.2 16.8 %copy-start.3 = (f32[2,32,128]{2,1,0:T(8,128)S(1)}, f32[2,32,128]{2,1,0:T(8,128)}, u32[]{:S(2)}) copy-start(f32[2,32,128]{2,1,0:T(8,128)} %constant.15.clone.places_ref) | copy-start | bytes 98308
  2.2 16.8 %copy-start.4 = (f32[2,16,16]{2,1,0:T(8,128)S(1)}, f32[2,16,16]{2,1,0:T(8,128)}, u32[]{:S(2)}) copy-start(f32[2,16,16]{2,1,0:T(8,128)} %uv_ref.1) | copy-start | bytes 6148
  2.2 16.8 %copy-start.7 = (f32[8,256]{1,0:T(8,128)S(1)}, f32[8,256]{1,0:T(8,128)}, u32[]{:S(2)}) copy-start(f32[8,256]{1,0:T(8,128)} %constant.16.clone.factor_ref) | copy-start | bytes 24580
  2.2 16.8 %copy-start.8 = (s32[16,1]{0,1:T(1,128)S(1)}, s32[16,1]{0,1:T(1,128)}, u32[]{:S(2)}) copy-start(s32[16,1]{0,1:T(1,128)} %param.18) | copy-start | bytes 196
  2.3 23.2 %all-to-all-start = ((f32[32,1,1152]{2,1,0:T(1,128)}), f32[32,1,1152]{2,1,0:T(1,128)S(1)}, u32[]{:S(2)}, u32[]{:S(2)}) async-start(f32[32,1,1152]{2,1,0:T(1,128)} %bitcast.1), calls=%async_computation | async-start | bytes 294912 | tf_op jit(solution)/shard_map/all_to_all | solution.py:384
  16.1 4.4 %collective-permute-start = (bf16[1,128,1024]{2,1,0:T(8,128)(2,1)S(1)}, bf16[1,128,1024]{2,1,0:T(8,128)(2,1)S(1)}, u32[]{:S(2)}, u32[]{:S(2)}) collective-permute-start(bf16[1,128,1024]{2,1,0:T(8,128)(2,1)S(1)} %copy-done), channel_id=1, source_target_pairs={{0,8},{8,0},{1,9},{9,1},{2,10},{10,2},{3,11},{11,3},{4,12},{12,4},... | collective-permute-start | bytes 786440 | tf_op jit(solution)/shard_map/ppermute | solution.py:366
  26.7 8.1 %copy-start.10 = (s32[16,2]{0,1:T(2,128)S(1)}, s32[16,2]{0,1:T(2,128)}, u32[]{:S(2)}) copy-start(s32[16,2]{0,1:T(2,128)} %param.17) | copy-start | bytes 388
  26.7 8.2 %copy-start.9 = (f32[8,16,2,16]{3,2,1,0:T(2,128)S(1)}, f32[8,16,2,16]{3,2,1,0:T(2,128)}, u32[]{:S(2)}) copy-start(f32[8,16,2,16]{3,2,1,0:T(2,128)} %param.15) | copy-start | bytes 49156
  26.7 14.5 %all-to-all-start.1 = ((bf16[32,32,128]{2,1,0:T(8,128)(2,1)}), bf16[32,32,128]{2,1,0:T(8,128)(2,1)S(1)}, u32[]{:S(2)}, u32[]{:S(2)}) async-start(bf16[32,32,128]{2,1,0:T(8,128)(2,1)} %reply_tiles.1), calls=%async_computation.1 | async-start | bytes 524288 | tf_op jit(solution)/shard_map/all_to_all | solution.py:408
  31.5 4.3 %collective-permute-start.1 = (f32[288,128]{1,0:T(8,128)S(1)}, f32[288,128]{1,0:T(8,128)S(1)}, u32[]{:S(2)}, u32[]{:S(2)}) collective-permute-start(f32[288,128]{1,0:T(8,128)S(1)} %bitcast.31), channel_id=1, source_target_pairs={{0,8},{8,0},{1,9},{9,1},{2,10},{10,2},{3,11},{11,3},{4,12},{12,4},... | collective-permute-start | bytes 442376 | tf_op jit(solution)/shard_map/ppermute | solution.py:366
  42.1 13.8 %copy-start.1 = (bf16[256,256]{1,0:T(8,128)(2,1)S(1)}, bf16[256,256]{1,0:T(8,128)(2,1)}, u32[]{:S(2)}) copy-start(bf16[256,256]{1,0:T(8,128)(2,1)} %constant.17.clone.cols_hi_ref) | copy-start | bytes 393220
  42.1 13.8 %copy-start.2 = (bf16[256,256]{1,0:T(8,128)(2,1)S(1)}, bf16[256,256]{1,0:T(8,128)(2,1)}, u32[]{:S(2)}) copy-start(bf16[256,256]{1,0:T(8,128)(2,1)} %constant.18.clone.cols_lo_ref) | copy-start | bytes 393220
  42.1 13.8 %copy-start.5 = (bf16[64,64]{1,0:T(8,128)(2,1)S(1)}, bf16[64,64]{1,0:T(8,128)(2,1)}, u32[]{:S(2)}) copy-start(bf16[64,64]{1,0:T(8,128)(2,1)} %constant.19.clone.rows_hi_ref) | copy-start | bytes 24580
  42.1 13.8 %copy-start.6 = (bf16[64,64]{1,0:T(8,128)(2,1)S(1)}, bf16[64,64]{1,0:T(8,128)(2,1)}, u32[]{:S(2)}) copy-start(bf16[64,64]{1,0:T(8,128)(2,1)} %constant.20.clone.rows_lo_ref) | copy-start | bytes 24580
  85.0 17.1 %all-to-all-start.5 = ((f32[16,8,128]{2,1,0:T(8,128)}), f32[16,8,128]{2,1,0:T(8,128)S(1)}, u32[]{:S(2)}, u32[]{:S(2)}) async-start(f32[16,8,128]{2,1,0:T(8,128)} %bitcast.10), calls=%async_computation.5 | async-start | bytes 131072 | tf_op jit(solution)/shard_map/all_to_all | solution.py:454

commit v7 on v6

--- a/solution.py
+++ b/solution.py
@@ -19,8 +19,12 @@
 BLD = 16
 TILES = 128
 SAMPLES = TIMES * CHANS
-RING = (0, 4, 1, 5, 2, 6, 3, 7)
-TURN = (0, 2, 4, 6, 1, 3, 5, 7)
+RING3 = (4, 0, 5, 1, 6, 2, 7, 3)
+TURN3 = (1, 3, 5, 7, 0, 2, 4, 6)
+RING5 = (0, 4, 1, 5, 2, 6, 3, 7)
+TURN5 = (0, 2, 4, 6, 1, 3, 5, 7)
+CHIPS1 = tuple(x * 8 + (z + 7) % 8 for x in range(4) for z in range(8))
+RING7 = tuple(2 * c + 1 - k for c in range(NCH) for k in range(2))
 MSG1 = 9
 MSG3 = 56
 MSG5 = 40
@@ -117,14 +121,15 @@
         req = jnp.where(hit & (count == 0), slot_ref[i] + 1, req)
         count = jnp.where(hit, count - 1, count)
     req = req.astype(f32)
-    for s in range(CHIPS):
-        out_ref[MSG1 * s : MSG1 * s + 8, :] = mine
-        out_ref[MSG1 * s + 8 : MSG1 * s + 9, :] = req[s : s + 1]
+    for at, s in enumerate(CHIPS1):
+        out_ref[MSG1 * at : MSG1 * at + 8, :] = mine
+        out_ref[MSG1 * at + 8 : MSG1 * at + 9, :] = req[s : s + 1]
 
 
 def reply_tiles(msg_ref, grid_ref, other_ref, _, out_ref, scr_ref):
     core = lax.axis_index("core")
     req = msg_ref[pl.ds(8, CHIPS, stride=MSG1), :].astype(jnp.int32)
+    req = jnp.concatenate([pltpu.roll(req[x : x + 8], 7, 0) for x in range(0, CHIPS, 8)], axis=0)
     lanes = lax.broadcasted_iota(jnp.int32, (CHIPS, 2 * TILES), 1) + 1
     picks = []
     for k in range(4):
@@ -146,15 +151,17 @@
     rows_ref[: CHIPS * MSG1, :] = mine_ref[...]
     rows_ref[CHIPS * MSG1 :, :] = other_ref[...]
     for i in range(BLD):
-        d, a = TURN[i // 2], i % 2
+        d, a = TURN3[i // 2], i % 2
         out_ref[d, a * 8 : a * 8 + 8, :] = tiles_ref[place_ref[i]].astype(f32)
         for e in range(2):
             at = 16 + (a * 2 + e) * 8
             s = pair_ref[i, e]
-            row = MSG1 * (s // 2 + CHIPS * lax.rem(s + core, 2))
+            chip = lax.div(s, 2)
+            at1 = jnp.where(lax.rem(chip, 8) == 7, chip - 7, chip + 1)
+            row = MSG1 * (at1 + CHIPS * lax.rem(s + core, 2))
             out_ref[d, at : at + 8, :] = rows_ref[pl.ds(row, 8), :]
     for c in range(NCH):
-        out_ref[TURN[c], 48:56, :] = seen_ref[c]
+        out_ref[TURN3[c], 48:56, :] = seen_ref[c]
 
 
 def blocks_swap(four):
@@ -250,7 +257,7 @@
     rows_lo_ref,
     out_ref,
 ):
-    planes = [[msg_ref[TURN[k], a * 8 : a * 8 + 8, :] for k in range(8)] for a in range(2)]
+    planes = [[msg_ref[TURN3[k], a * 8 : a * 8 + 8, :] for k in range(8)] for a in range(2)]
     grid_re = jnp.concatenate([to_rows(planes[a][:4]) for a in range(2)], axis=0)
     grid_im = jnp.concatenate([to_rows(planes[a][4:]) for a in range(2)], axis=0)
     grid = jnp.concatenate([grid_re, grid_im], axis=1)
@@ -275,7 +282,7 @@
 
         def jones(e):
             at = 16 + (a * 2 + e) * 8
-            return mat(lambda p: (msg_ref[TURN[p], at : at + 8, :], msg_ref[TURN[p + 4], at : at + 8, :]))
+            return mat(lambda p: (msg_ref[TURN3[p], at : at + 8, :], msg_ref[TURN3[p + 4], at : at + 8, :]))
 
         first, second = jones(0), jones(1)
         middle = prod(first, sky)
@@ -298,10 +305,10 @@
             vis_re.append(jnp.sum(cos_row * t_re + sin_row * t_im, axis=0, keepdims=True))
             vis_im.append(jnp.sum(cos_row * t_im - sin_row * t_re, axis=0, keepdims=True))
         vis = jnp.concatenate(vis_re + vis_im, axis=0)
-        seen = jnp.concatenate([msg_ref[c, 48:56, a * 32 : a * 32 + 32] for c in TURN], axis=1)
+        seen = jnp.concatenate([msg_ref[c, 48:56, a * 32 : a * 32 + 32] for c in TURN3], axis=1)
         resid = vis * (1.0 / SUB) - seen
         for k in range(8):
-            h, l = divmod(TURN[k], 2)
+            h, l = divmod(TURN5[k], 2)
             out_ref[h, l, 32:40, a * 32 : a * 32 + 32] = resid[:, k * 32 : k * 32 + 32]
         g = resid * (GRAD_SCALE / SUB)
         d_re, d_im = [], []
@@ -344,7 +351,7 @@
 def sum_terms(pair_ref, msg_ref, out_ref):
     out_ref[...] = jnp.zeros_like(out_ref)
     for i in range(BLD):
-        d, a = TURN[i // 2], i % 2
+        d, a = TURN5[i // 2], i % 2
         for e in range(2):
             s = pair_ref[i, e]
             at = (a * 2 + e) * 8
@@ -354,7 +361,8 @@
 def sum_chips(msg_ref, out_ref):
     total = jnp.sum(msg_ref[...], axis=0)
     for k in range(NCH):
-        out_ref[k] = total
+        out_ref[k, :8, :] = total[8:]
+        out_ref[k, 8:, :] = total[:8]
 
 
 def per_device(model_grid, screens, observed, uv_coords, station_pairs, tile_owner, tile_slot):
@@ -381,7 +389,8 @@
         compiler_params=params,
         name="send_requests",
     )(*[pltpu.with_memory_space_constraint(x, pltpu.HBM) for x in (owner, tile_slot, screens)])
-    got1 = lax.all_to_all(msg1.reshape(CHIPS, 1, MSG1 * 128), "xz", 0, 0, tiled=True)
+    msg1 = msg1.reshape(CHIPS, 1, MSG1 * 128)
+    got1 = lax.all_to_all(msg1, "xz", 0, 0, tiled=True, axis_index_groups=[CHIPS1])
     got1 = got1.reshape(CHIPS * MSG1, 128)
     other1 = from_other_core(got1)
 
@@ -417,7 +426,7 @@
         compiler_params=params,
         name="send_baselines",
     )(place, station_pairs, got2, got1, other1, seen)
-    got3 = lax.all_to_all(msg3, "ch", 0, 0, tiled=True, axis_index_groups=[RING])
+    got3 = lax.all_to_all(msg3, "ch", 0, 0, tiled=True, axis_index_groups=[RING3])
 
     msg5 = pl.pallas_call(
         calibrate,
@@ -428,7 +437,7 @@
         name="calibrate",
     )(got3, *waves, *dft)
     msg5 = msg5.reshape(NCH, MSG5, 128)
-    got5 = lax.all_to_all(msg5, "ch", 0, 0, tiled=True, axis_index_groups=[RING])
+    got5 = lax.all_to_all(msg5, "ch", 0, 0, tiled=True, axis_index_groups=[RING5])
 
     resid = got5[:, 32:40, :64].reshape(NCH // 2, 2, 8, 2, 2, TIMES)
     residual = resid.transpose(2, 5, 4, 1, 0, 3).reshape(8, TIMES, 2, BLD)
@@ -451,7 +460,8 @@
         compiler_params=params,
         name="sum_chips",
     )(got6)
-    got7 = lax.all_to_all(msg7.reshape(2 * NCH, 8, 128), ("ch", "core"), 0, 0, tiled=True)
+    msg7 = msg7.reshape(2 * NCH, 8, 128)
+    got7 = lax.all_to_all(msg7, ("ch", "core"), 0, 0, tiled=True, axis_index_groups=[RING7])
     got7 = got7.reshape(NCH, 2, 8, 128)
     screen_grad = (got7[:, 0] + got7[:, 1]).transpose(1, 0, 2).reshape(1, 8, PIX)
     return residual, screen_grad

time: 103 us -> 101 us (0.981)
  waiting for transfers between devices: 17.6 us -> 15 us
  starting transfers between devices: 34.1 us -> 36.3 us
  blocking collectives: 39.7 us -> 38.2 us
    all_to_all x2, waiting for transfers between devices: 11.7 us -> 10 us  [the longest x1 6.83 us: per_device(): lax.all_to_all(msg7, ('ch', 'core'), 0, 0, tiled=True, axis_index_groups=...]
    all_to_all x1, blocking collectives: 15.8 us -> 14.4 us  [per_device(): got6 = lax.all_to_all(msg6.reshape(CHIPS, 16, 128), 'xz', 0, 0, tiled=True)]
    ppermute x2, starting transfers between devices: 6.15 us -> 7.35 us  [from_other_core(): return lax.ppermute(x, 'core', [(0, 1), (1, 0)])]
  transfers between devices with their start and end apart: 5 -> 5, of which waited for: 4 -> 4; matrix products, arithmetic and copies ran while one was open for 1% -> 1% of each run, Pallas kernels for 1% -> 2%
where the time goes in v7:
time: 101 us
  blocking collectives  38.2 us (38%)
  starting transfers between devices  36.3 us (36%)
  waiting for transfers between devices  15 us (15%)
  Pallas kernels  8.45 us (8%)
  local copies, waits for them, and re-layouts  1.46 us (1%)
    all_to_all x1, blocking collectives, per_device(): got6 = lax.all_to_all(msg6.reshape(CHIPS, 16, 128), 'xz', 0, 0, tiled=True)  14.4 us
    all_to_all x1, starting transfers between devices, per_device(): lax.all_to_all(msg1, 'xz', 0, 0, tiled=True, axis_index_groups=[CHIPS1])  13.9 us
    all_to_all x1, blocking collectives, per_device(): lax.all_to_all(msg5, 'ch', 0, 0, tiled=True, axis_index_groups=[RING5])  12.2 us
    all_to_all x1, blocking collectives, per_device(): lax.all_to_all(msg3, 'ch', 0, 0, tiled=True, axis_index_groups=[RING3])  11.7 us
    all_to_all x1, starting transfers between devices, per_device(): lax.all_to_all(msg7, ('ch', 'core'), 0, 0, tiled=True, axis_index_groups=...  9.87 us
    ppermute x2, starting transfers between devices, from_other_core(): return lax.ppermute(x, 'core', [(0, 1), (1, 0)])  7.35 us
    all_to_all x1, waiting for transfers between devices, per_device(): lax.all_to_all(msg7, ('ch', 'core'), 0, 0, tiled=True, axis_index_groups=...  6.83 us
    all_to_all x1, starting transfers between devices, per_device(): lax.all_to_all(tiles, 'xz', 0, 0, tiled=True).reshape(2 * NBL, 8, 128)  5.17 us
  transfers between devices with their start and end apart: 5, of which 4 were waited for; matrix products, arithmetic and copies ran while one was open for 1% of the time, Pallas kernels for 2%

profile of v7, /device:TPU:1, one launch (start us, length us, event | category | flops | bytes accessed | tf_op | source)
XLA Modules:
  0.0 100.9 jit_solution(13728180904238911439)
XLA Ops:
  0.6 1.6 %send_requests.1 = f32[288,128]{1,0:T(8,128)} custom-call(s32[16]{0:T(128)} %bitcast.36, s32[16]{0:T(128)} %slot_hbm.1, f32[1,8,1024]{2,1,0:T(8,128)} %screen_hbm.1), custom_call_target="tpu_custom_call" | custom-call | tf_op jit(solution)/shard_map/send_requests/pallas_call | solution.py:378
  2.3 13.9 %all-to-all-start = ((f32[32,1,1152]{2,1,0:T(1,128)}), f32[32,1,1152]{2,1,0:T(1,128)S(1)}, u32[]{:S(2)}, u32[]{:S(2)}) async-start(f32[32,1,1152]{2,1,0:T(1,128)} %bitcast.1), calls=%async_computation | async-start | bytes 294912 | tf_op jit(solution)/shard_map/all_to_all | solution.py:393
  16.2 3.1 %collective-permute-start = (bf16[1,128,1024]{2,1,0:T(8,128)(2,1)S(1)}, bf16[1,128,1024]{2,1,0:T(8,128)(2,1)S(1)}, u32[]{:S(2)}, u32[]{:S(2)}) collective-permute-start(bf16[1,128,1024]{2,1,0:T(8,128)(2,1)S(1)} %copy-done), channel_id=1, source_target_pairs={{0,8},{8,0},{1,9},{9,1},{2,10},{10,2},{3,11},{11,3},{4,12},{12,4},... | collective-permute-start | bytes 786440 | tf_op jit(solution)/shard_map/ppermute | solution.py:374
  19.4 1.5 %phases.1 = (bf16[128,256]{1,0:T(8,128)(2,1)S(1)}, bf16[128,256]{1,0:T(8,128)(2,1)S(1)}, f32[2,32,256]{2,1,0:T(8,128)S(1)}, f32[2,32,256]{2,1,0:T(8,128)S(1)}, s32[16]{0:T(128)S(1)}) custom-call(s32[16]{0:T(128)S(1)} %bitcast.37, f32[2,16,16]{2,1,0:T(8,128)S(1)} %copy-done.4, f32[2,32,128]{2,1,0:T(8,128)S(1)} %copy-done.3, f32[8,256]{1,0:T(8,128)S(1)} %copy-done.7), custom_call_target="tpu_custom_call" | custom-call | tf_op jit(solution)/shard_map/phases/pallas_call | solution.py:399
  20.9 3.2 %all-to-all-done = f32[32,1,1152]{2,1,0:T(1,128)S(1)} async-done(((f32[32,1,1152]{2,1,0:T(1,128)}), f32[32,1,1152]{2,1,0:T(1,128)S(1)}, u32[]{:S(2)}, u32[]{:S(2)}) %all-to-all-start) | async-done | bytes 147488 | tf_op jit(solution)/shard_map/all_to_all | solution.py:393
  24.1 1.2 %reply_tiles.1 = bf16[32,32,128]{2,1,0:T(8,128)(2,1)} custom-call(f32[288,128]{1,0:T(8,128)S(1)} %bitcast.30, bf16[1,128,1024]{2,1,0:T(8,128)(2,1)S(1)} %copy-done, bf16[1,128,1024]{2,1,0:T(8,128)(2,1)S(1)} %collective-permute-done.other_ref, bf16[128,256]{1,0:T(8,128)(2,1)S(1)} %get-tuple-element.8._.wave_hi_ref), custom_call_target="tpu_custom_call" | custom-call | tf_op jit(solution)/shard_map/reply_tiles/pallas_call | solution.py:408
  25.3 5.2 %all-to-all-start.1 = ((bf16[32,32,128]{2,1,0:T(8,128)(2,1)}), bf16[32,32,128]{2,1,0:T(8,128)(2,1)S(1)}, u32[]{:S(2)}, u32[]{:S(2)}) async-start(bf16[32,32,128]{2,1,0:T(8,128)(2,1)} %reply_tiles.1), calls=%async_computation.1 | async-start | bytes 524288 | tf_op jit(solution)/shard_map/all_to_all | solution.py:417
  30.5 4.2 %collective-permute-start.1 = (f32[288,128]{1,0:T(8,128)S(1)}, f32[288,128]{1,0:T(8,128)S(1)}, u32[]{:S(2)}, u32[]{:S(2)}) collective-permute-start(f32[288,128]{1,0:T(8,128)S(1)} %bitcast.31), channel_id=1, source_target_pairs={{0,8},{8,0},{1,9},{9,1},{2,10},{10,2},{3,11},{11,3},{4,12},{12,4},... | collective-permute-start | bytes 442376 | tf_op jit(solution)/shard_map/ppermute | solution.py:374
  34.8 0.1 copy.30
  35.0 0.2 reshape.49
  35.2 0.5 collective-permute-done.1.other_ref
  35.7 4.5 %all-to-all-done.1 = bf16[32,32,128]{2,1,0:T(8,128)(2,1)S(1)} async-done(((bf16[32,32,128]{2,1,0:T(8,128)(2,1)}), bf16[32,32,128]{2,1,0:T(8,128)(2,1)S(1)}, u32[]{:S(2)}, u32[]{:S(2)}) %all-to-all-start.1) | async-done | bytes 262176 | tf_op jit(solution)/shard_map/all_to_all | solution.py:417
  40.2 0.9 send_baselines.1
  41.1 11.7 %all_to_all.30.msg_ref = f32[8,56,128]{2,1,0:T(8,128)S(1)} all-to-all(f32[8,56,128]{2,1,0:T(8,128)S(1)} %send_baselines.1), channel_id=1, replica_groups={{4,0,5,1,6,2,7,3},{12,8,13,9,14,10,15,11},{20,16,21,17,22,18,23,19},{28..., dimensions={0} | all-to-all | bytes 458752 | tf_op jit(solution)/shard_map/all_to_all | solution.py:429
  52.8 1.8 %calibrate.1 = f32[4,2,40,128]{3,2,1,0:T(8,128)S(1)} custom-call(f32[8,56,128]{2,1,0:T(8,128)S(1)} %all_to_all.30.msg_ref, bf16[128,256]{1,0:T(8,128)(2,1)S(1)} %get-tuple-element.8._.wave_hi_ref, bf16[128,256]{1,0:T(8,128)(2,1)S(1)} %get-tuple-element.9.wave_lo_ref, f32[2,32,256]{2,1,0:T(8,128)S(1)} %get-tuple-element.10.cos_ref, ...), custom_call_target="tpu_custom_call" | custom-call | tf_op jit(solution)/shard_map/calibrate/pallas_call | solution.py:431
  54.6 12.2 %all_to_all.31.msg_ref = f32[8,40,128]{2,1,0:T(8,128)S(1)} all-to-all(f32[8,40,128]{2,1,0:T(8,128)S(1)} %bitcast.35), channel_id=1, replica_groups={{0,4,1,5,2,6,3,7},{8,12,9,13,10,14,11,15},{16,20,17,21,18,22,19,23},{24..., dimensions={0} | all-to-all | bytes 327680 | tf_op jit(solution)/shard_map/all_to_all | solution.py:440
  66.8 0.8 sum_terms.1
  67.5 14.4 %all_to_all.32.msg_ref = f32[32,16,128]{2,1,0:T(8,128)S(1)} all-to-all(f32[32,16,128]{2,1,0:T(8,128)S(1)} %bitcast.33), channel_id=1, replica_groups=mesh['xz'=32,'core'=2,'ch'=8] {'xz'}, dimensions={0} | all-to-all | bytes 524288 | tf_op jit(solution)/shard_map/all_to_all | solution.py:453
  81.9 0.7 sum_chips.1
  82.6 9.9 %all-to-all-start.5 = ((f32[16,8,128]{2,1,0:T(8,128)}), f32[16,8,128]{2,1,0:T(8,128)S(1)}, u32[]{:S(2)}, u32[]{:S(2)}) async-start(f32[16,8,128]{2,1,0:T(8,128)} %bitcast.10), calls=%async_computation.5 | async-start | bytes 131072 | tf_op jit(solution)/shard_map/all_to_all | solution.py:464
  92.5 0.1 reshape.51
  92.7 0.8 copy.37
  93.4 6.8 %all-to-all-done.5 = f32[16,8,128]{2,1,0:T(8,128)S(1)} async-done(((f32[16,8,128]{2,1,0:T(8,128)}), f32[16,8,128]{2,1,0:T(8,128)S(1)}, u32[]{:S(2)}, u32[]{:S(2)}) %all-to-all-start.5) | async-done | bytes 65568 | tf_op jit(solution)/shard_map/all_to_all | solution.py:464
  100.3 0.6 fusion.1
  (28 shorter events, 0.3 us)
Async XLA Ops:
  0.6 15.5 %copy-start = (bf16[1,128,1024]{2,1,0:T(8,128)(2,1)S(1)}, bf16[1,128,1024]{2,1,0:T(8,128)(2,1)}, u32[]{:S(2)}) copy-start(bf16[1,128,1024]{2,1,0:T(8,128)(2,1)} %grid_ref.1) | copy-start | bytes 786436
  2.2 17.1 %copy-start.3 = (f32[2,32,128]{2,1,0:T(8,128)S(1)}, f32[2,32,128]{2,1,0:T(8,128)}, u32[]{:S(2)}) copy-start(f32[2,32,128]{2,1,0:T(8,128)} %constant.15.clone.places_ref) | copy-start | bytes 98308
  2.2 17.1 %copy-start.4 = (f32[2,16,16]{2,1,0:T(8,128)S(1)}, f32[2,16,16]{2,1,0:T(8,128)}, u32[]{:S(2)}) copy-start(f32[2,16,16]{2,1,0:T(8,128)} %uv_ref.1) | copy-start | bytes 6148
  2.2 17.1 %copy-start.7 = (f32[8,256]{1,0:T(8,128)S(1)}, f32[8,256]{1,0:T(8,128)}, u32[]{:S(2)}) copy-start(f32[8,256]{1,0:T(8,128)} %constant.16.clone.factor_ref) | copy-start | bytes 24580
  2.2 17.1 %copy-start.8 = (s32[16,1]{0,1:T(1,128)S(1)}, s32[16,1]{0,1:T(1,128)}, u32[]{:S(2)}) copy-start(s32[16,1]{0,1:T(1,128)} %param.18) | copy-start | bytes 196
  2.3 21.8 %all-to-all-start = ((f32[32,1,1152]{2,1,0:T(1,128)}), f32[32,1,1152]{2,1,0:T(1,128)S(1)}, u32[]{:S(2)}, u32[]{:S(2)}) async-start(f32[32,1,1152]{2,1,0:T(1,128)} %bitcast.1), calls=%async_computation | async-start | bytes 294912 | tf_op jit(solution)/shard_map/all_to_all | solution.py:393
  16.2 4.7 %collective-permute-start = (bf16[1,128,1024]{2,1,0:T(8,128)(2,1)S(1)}, bf16[1,128,1024]{2,1,0:T(8,128)(2,1)S(1)}, u32[]{:S(2)}, u32[]{:S(2)}) collective-permute-start(bf16[1,128,1024]{2,1,0:T(8,128)(2,1)S(1)} %copy-done), channel_id=1, source_target_pairs={{0,8},{8,0},{1,9},{9,1},{2,10},{10,2},{3,11},{11,3},{4,12},{12,4},... | collective-permute-start | bytes 786440 | tf_op jit(solution)/shard_map/ppermute | solution.py:374
  25.3 9.4 %copy-start.10 = (s32[16,2]{0,1:T(2,128)S(1)}, s32[16,2]{0,1:T(2,128)}, u32[]{:S(2)}) copy-start(s32[16,2]{0,1:T(2,128)} %param.17) | copy-start | bytes 388
  25.3 9.5 %copy-start.9 = (f32[8,16,2,16]{3,2,1,0:T(2,128)S(1)}, f32[8,16,2,16]{3,2,1,0:T(2,128)}, u32[]{:S(2)}) copy-start(f32[8,16,2,16]{3,2,1,0:T(2,128)} %param.15) | copy-start | bytes 49156
  25.3 14.8 %all-to-all-start.1 = ((bf16[32,32,128]{2,1,0:T(8,128)(2,1)}), bf16[32,32,128]{2,1,0:T(8,128)(2,1)S(1)}, u32[]{:S(2)}, u32[]{:S(2)}) async-start(bf16[32,32,128]{2,1,0:T(8,128)(2,1)} %reply_tiles.1), calls=%async_computation.1 | async-start | bytes 524288 | tf_op jit(solution)/shard_map/all_to_all | solution.py:417
  30.5 5.2 %collective-permute-start.1 = (f32[288,128]{1,0:T(8,128)S(1)}, f32[288,128]{1,0:T(8,128)S(1)}, u32[]{:S(2)}, u32[]{:S(2)}) collective-permute-start(f32[288,128]{1,0:T(8,128)S(1)} %bitcast.31), channel_id=1, source_target_pairs={{0,8},{8,0},{1,9},{9,1},{2,10},{10,2},{3,11},{11,3},{4,12},{12,4},... | collective-permute-start | bytes 442376 | tf_op jit(solution)/shard_map/ppermute | solution.py:374
  41.1 11.7 %copy-start.1 = (bf16[256,256]{1,0:T(8,128)(2,1)S(1)}, bf16[256,256]{1,0:T(8,128)(2,1)}, u32[]{:S(2)}) copy-start(bf16[256,256]{1,0:T(8,128)(2,1)} %constant.17.clone.cols_hi_ref) | copy-start | bytes 393220
  41.1 11.7 %copy-start.2 = (bf16[256,256]{1,0:T(8,128)(2,1)S(1)}, bf16[256,256]{1,0:T(8,128)(2,1)}, u32[]{:S(2)}) copy-start(bf16[256,256]{1,0:T(8,128)(2,1)} %constant.18.clone.cols_lo_ref) | copy-start | bytes 393220
  41.1 11.7 %copy-start.5 = (bf16[64,64]{1,0:T(8,128)(2,1)S(1)}, bf16[64,64]{1,0:T(8,128)(2,1)}, u32[]{:S(2)}) copy-start(bf16[64,64]{1,0:T(8,128)(2,1)} %constant.19.clone.rows_hi_ref) | copy-start | bytes 24580
  41.1 11.7 %copy-start.6 = (bf16[64,64]{1,0:T(8,128)(2,1)S(1)}, bf16[64,64]{1,0:T(8,128)(2,1)}, u32[]{:S(2)}) copy-start(bf16[64,64]{1,0:T(8,128)(2,1)} %constant.20.clone.rows_lo_ref) | copy-start | bytes 24580
  82.6 17.7 %all-to-all-start.5 = ((f32[16,8,128]{2,1,0:T(8,128)}), f32[16,8,128]{2,1,0:T(8,128)S(1)}, u32[]{:S(2)}, u32[]{:S(2)}) async-start(f32[16,8,128]{2,1,0:T(8,128)} %bitcast.10), calls=%async_computation.5 | async-start | bytes 131072 | tf_op jit(solution)/shard_map/all_to_all | solution.py:464

commit v8 on v7

--- a/solution.py
+++ b/solution.py
@@ -24,7 +24,7 @@
 RING5 = (0, 4, 1, 5, 2, 6, 3, 7)
 TURN5 = (0, 2, 4, 6, 1, 3, 5, 7)
 CHIPS1 = tuple(x * 8 + (z + 7) % 8 for x in range(4) for z in range(8))
-RING7 = tuple(2 * c + 1 - k for c in range(NCH) for k in range(2))
+RING7 = tuple(2 * ((c + 4) % NCH) + 1 - k for c in range(NCH) for k in range(2))
 MSG1 = 9
 MSG3 = 56
 MSG5 = 40
@@ -343,8 +343,8 @@
             for p in range(4):
                 re, im = grads[e][p // 2][p % 2]
                 for l in range(2):
-                    out_ref[:, l, at + p, :] = re[4 * l : 4 * l + 4]
-                    out_ref[:, l, at + p + 4, :] = im[4 * l : 4 * l + 4]
+                    out_ref[:, l, at + p, :] = re[4 - 4 * l : 8 - 4 * l]
+                    out_ref[:, l, at + p + 4, :] = im[4 - 4 * l : 8 - 4 * l]
     out_ref[:, :, 32:40, 64:] = jnp.zeros((4, 2, 8, 64), f32)
 
 

time: 101 us -> 101 us (level)
  waiting for transfers between devices: 15 us -> 10.3 us
  starting transfers between devices: 36.3 us -> 40.2 us
    all_to_all x1, waiting for transfers between devices: 6.83 us -> 2.12 us  [per_device(): lax.all_to_all(msg7, ('ch', 'core'), 0, 0, tiled=True, axis_index_groups=...]
    all_to_all x1, starting transfers between devices: 9.87 us -> 13.7 us  [per_device(): lax.all_to_all(msg7, ('ch', 'core'), 0, 0, tiled=True, axis_index_groups=...]
where the time goes in v8:
time: 101 us; the launch traced here: 100 us
  starting transfers between devices  40.2 us (40%)
  blocking collectives  38.2 us (38%)
  waiting for transfers between devices  10.3 us (10%)
  Pallas kernels  8.46 us (8%)
  local copies, waits for them, and re-layouts  1.46 us (1%)
    all_to_all x1, blocking collectives, per_device(): got6 = lax.all_to_all(msg6.reshape(CHIPS, 16, 128), 'xz', 0, 0, tiled=True)  14.4 us
    all_to_all x1, starting transfers between devices, per_device(): lax.all_to_all(msg1, 'xz', 0, 0, tiled=True, axis_index_groups=[CHIPS1])  13.9 us
    all_to_all x1, starting transfers between devices, per_device(): lax.all_to_all(msg7, ('ch', 'core'), 0, 0, tiled=True, axis_index_groups=...  13.7 us
    all_to_all x1, blocking collectives, per_device(): lax.all_to_all(msg5, 'ch', 0, 0, tiled=True, axis_index_groups=[RING5])  12.2 us
    all_to_all x1, blocking collectives, per_device(): lax.all_to_all(msg3, 'ch', 0, 0, tiled=True, axis_index_groups=[RING3])  11.7 us
    ppermute x2, starting transfers between devices, from_other_core(): return lax.ppermute(x, 'core', [(0, 1), (1, 0)])  7.35 us
    all_to_all x1, starting transfers between devices, per_device(): lax.all_to_all(tiles, 'xz', 0, 0, tiled=True).reshape(2 * NBL, 8, 128)  5.17 us
    all_to_all x1, waiting for transfers between devices, per_device(): lax.all_to_all(tiles, 'xz', 0, 0, tiled=True).reshape(2 * NBL, 8, 128)  4.47 us
  transfers between devices with their start and end apart: 5, of which 4 were waited for; matrix products, arithmetic and copies ran while one was open for 1% of the time, Pallas kernels for 2%

profile of v8, /device:TPU:1, one launch (start us, length us, event | category | flops | bytes accessed | tf_op | source)
XLA Modules:
  0.0 100.0 jit_solution(12580309210808874919)
XLA Ops:
  0.6 1.6 %send_requests.1 = f32[288,128]{1,0:T(8,128)} custom-call(s32[16]{0:T(128)} %bitcast.36, s32[16]{0:T(128)} %slot_hbm.1, f32[1,8,1024]{2,1,0:T(8,128)} %screen_hbm.1), custom_call_target="tpu_custom_call" | custom-call | tf_op jit(solution)/shard_map/send_requests/pallas_call | solution.py:378
  2.3 13.9 %all-to-all-start = ((f32[32,1,1152]{2,1,0:T(1,128)}), f32[32,1,1152]{2,1,0:T(1,128)S(1)}, u32[]{:S(2)}, u32[]{:S(2)}) async-start(f32[32,1,1152]{2,1,0:T(1,128)} %bitcast.1), calls=%async_computation | async-start | bytes 294912 | tf_op jit(solution)/shard_map/all_to_all | solution.py:393
  16.2 3.1 %collective-permute-start = (bf16[1,128,1024]{2,1,0:T(8,128)(2,1)S(1)}, bf16[1,128,1024]{2,1,0:T(8,128)(2,1)S(1)}, u32[]{:S(2)}, u32[]{:S(2)}) collective-permute-start(bf16[1,128,1024]{2,1,0:T(8,128)(2,1)S(1)} %copy-done), channel_id=1, source_target_pairs={{0,8},{8,0},{1,9},{9,1},{2,10},{10,2},{3,11},{11,3},{4,12},{12,4},... | collective-permute-start | bytes 786440 | tf_op jit(solution)/shard_map/ppermute | solution.py:374
  19.4 1.5 %phases.1 = (bf16[128,256]{1,0:T(8,128)(2,1)S(1)}, bf16[128,256]{1,0:T(8,128)(2,1)S(1)}, f32[2,32,256]{2,1,0:T(8,128)S(1)}, f32[2,32,256]{2,1,0:T(8,128)S(1)}, s32[16]{0:T(128)S(1)}) custom-call(s32[16]{0:T(128)S(1)} %bitcast.37, f32[2,16,16]{2,1,0:T(8,128)S(1)} %copy-done.4, f32[2,32,128]{2,1,0:T(8,128)S(1)} %copy-done.3, f32[8,256]{1,0:T(8,128)S(1)} %copy-done.7), custom_call_target="tpu_custom_call" | custom-call | tf_op jit(solution)/shard_map/phases/pallas_call | solution.py:399
  20.9 3.2 %all-to-all-done = f32[32,1,1152]{2,1,0:T(1,128)S(1)} async-done(((f32[32,1,1152]{2,1,0:T(1,128)}), f32[32,1,1152]{2,1,0:T(1,128)S(1)}, u32[]{:S(2)}, u32[]{:S(2)}) %all-to-all-start) | async-done | bytes 147488 | tf_op jit(solution)/shard_map/all_to_all | solution.py:393
  24.1 1.2 %reply_tiles.1 = bf16[32,32,128]{2,1,0:T(8,128)(2,1)} custom-call(f32[288,128]{1,0:T(8,128)S(1)} %bitcast.30, bf16[1,128,1024]{2,1,0:T(8,128)(2,1)S(1)} %copy-done, bf16[1,128,1024]{2,1,0:T(8,128)(2,1)S(1)} %collective-permute-done.other_ref, bf16[128,256]{1,0:T(8,128)(2,1)S(1)} %get-tuple-element.8._.wave_hi_ref), custom_call_target="tpu_custom_call" | custom-call | tf_op jit(solution)/shard_map/reply_tiles/pallas_call | solution.py:408
  25.3 5.2 %all-to-all-start.1 = ((bf16[32,32,128]{2,1,0:T(8,128)(2,1)}), bf16[32,32,128]{2,1,0:T(8,128)(2,1)S(1)}, u32[]{:S(2)}, u32[]{:S(2)}) async-start(bf16[32,32,128]{2,1,0:T(8,128)(2,1)} %reply_tiles.1), calls=%async_computation.1 | async-start | bytes 524288 | tf_op jit(solution)/shard_map/all_to_all | solution.py:417
  30.5 4.2 %collective-permute-start.1 = (f32[288,128]{1,0:T(8,128)S(1)}, f32[288,128]{1,0:T(8,128)S(1)}, u32[]{:S(2)}, u32[]{:S(2)}) collective-permute-start(f32[288,128]{1,0:T(8,128)S(1)} %bitcast.31), channel_id=1, source_target_pairs={{0,8},{8,0},{1,9},{9,1},{2,10},{10,2},{3,11},{11,3},{4,12},{12,4},... | collective-permute-start | bytes 442376 | tf_op jit(solution)/shard_map/ppermute | solution.py:374
  34.8 0.1 copy.30
  35.0 0.2 reshape.49
  35.2 0.5 collective-permute-done.1.other_ref
  35.7 4.5 %all-to-all-done.1 = bf16[32,32,128]{2,1,0:T(8,128)(2,1)S(1)} async-done(((bf16[32,32,128]{2,1,0:T(8,128)(2,1)}), bf16[32,32,128]{2,1,0:T(8,128)(2,1)S(1)}, u32[]{:S(2)}, u32[]{:S(2)}) %all-to-all-start.1) | async-done | bytes 262176 | tf_op jit(solution)/shard_map/all_to_all | solution.py:417
  40.2 0.9 send_baselines.1
  41.1 11.7 %all_to_all.30.msg_ref = f32[8,56,128]{2,1,0:T(8,128)S(1)} all-to-all(f32[8,56,128]{2,1,0:T(8,128)S(1)} %send_baselines.1), channel_id=1, replica_groups={{4,0,5,1,6,2,7,3},{12,8,13,9,14,10,15,11},{20,16,21,17,22,18,23,19},{28..., dimensions={0} | all-to-all | bytes 458752 | tf_op jit(solution)/shard_map/all_to_all | solution.py:429
  52.8 1.8 %calibrate.1 = f32[4,2,40,128]{3,2,1,0:T(8,128)S(1)} custom-call(f32[8,56,128]{2,1,0:T(8,128)S(1)} %all_to_all.30.msg_ref, bf16[128,256]{1,0:T(8,128)(2,1)S(1)} %get-tuple-element.8._.wave_hi_ref, bf16[128,256]{1,0:T(8,128)(2,1)S(1)} %get-tuple-element.9.wave_lo_ref, f32[2,32,256]{2,1,0:T(8,128)S(1)} %get-tuple-element.10.cos_ref, ...), custom_call_target="tpu_custom_call" | custom-call | tf_op jit(solution)/shard_map/calibrate/pallas_call | solution.py:431
  54.6 12.2 %all_to_all.31.msg_ref = f32[8,40,128]{2,1,0:T(8,128)S(1)} all-to-all(f32[8,40,128]{2,1,0:T(8,128)S(1)} %bitcast.35), channel_id=1, replica_groups={{0,4,1,5,2,6,3,7},{8,12,9,13,10,14,11,15},{16,20,17,21,18,22,19,23},{24..., dimensions={0} | all-to-all | bytes 327680 | tf_op jit(solution)/shard_map/all_to_all | solution.py:440
  66.8 0.8 sum_terms.1
  67.5 14.4 %all_to_all.32.msg_ref = f32[32,16,128]{2,1,0:T(8,128)S(1)} all-to-all(f32[32,16,128]{2,1,0:T(8,128)S(1)} %bitcast.33), channel_id=1, replica_groups=mesh['xz'=32,'core'=2,'ch'=8] {'xz'}, dimensions={0} | all-to-all | bytes 524288 | tf_op jit(solution)/shard_map/all_to_all | solution.py:453
  81.9 0.7 sum_chips.1
  82.6 13.7 %all-to-all-start.5 = ((f32[16,8,128]{2,1,0:T(8,128)}), f32[16,8,128]{2,1,0:T(8,128)S(1)}, u32[]{:S(2)}, u32[]{:S(2)}) async-start(f32[16,8,128]{2,1,0:T(8,128)} %bitcast.10), calls=%async_computation.5 | async-start | bytes 131072 | tf_op jit(solution)/shard_map/all_to_all | solution.py:464
  96.4 0.1 reshape.51
  96.5 0.8 copy.37
  97.3 2.1 %all-to-all-done.5 = f32[16,8,128]{2,1,0:T(8,128)S(1)} async-done(((f32[16,8,128]{2,1,0:T(8,128)}), f32[16,8,128]{2,1,0:T(8,128)S(1)}, u32[]{:S(2)}, u32[]{:S(2)}) %all-to-all-start.5) | async-done | bytes 65568 | tf_op jit(solution)/shard_map/all_to_all | solution.py:464
  99.4 0.6 fusion.1
  (28 shorter events, 0.3 us)
Async XLA Ops:
  0.6 15.5 %copy-start = (bf16[1,128,1024]{2,1,0:T(8,128)(2,1)S(1)}, bf16[1,128,1024]{2,1,0:T(8,128)(2,1)}, u32[]{:S(2)}) copy-start(bf16[1,128,1024]{2,1,0:T(8,128)(2,1)} %grid_ref.1) | copy-start | bytes 786436
  2.2 17.1 %copy-start.3 = (f32[2,32,128]{2,1,0:T(8,128)S(1)}, f32[2,32,128]{2,1,0:T(8,128)}, u32[]{:S(2)}) copy-start(f32[2,32,128]{2,1,0:T(8,128)} %constant.15.clone.places_ref) | copy-start | bytes 98308
  2.2 17.1 %copy-start.4 = (f32[2,16,16]{2,1,0:T(8,128)S(1)}, f32[2,16,16]{2,1,0:T(8,128)}, u32[]{:S(2)}) copy-start(f32[2,16,16]{2,1,0:T(8,128)} %uv_ref.1) | copy-start | bytes 6148
  2.2 17.1 %copy-start.7 = (f32[8,256]{1,0:T(8,128)S(1)}, f32[8,256]{1,0:T(8,128)}, u32[]{:S(2)}) copy-start(f32[8,256]{1,0:T(8,128)} %constant.16.clone.factor_ref) | copy-start | bytes 24580
  2.2 17.1 %copy-start.8 = (s32[16,1]{0,1:T(1,128)S(1)}, s32[16,1]{0,1:T(1,128)}, u32[]{:S(2)}) copy-start(s32[16,1]{0,1:T(1,128)} %param.18) | copy-start | bytes 196
  2.3 21.8 %all-to-all-start = ((f32[32,1,1152]{2,1,0:T(1,128)}), f32[32,1,1152]{2,1,0:T(1,128)S(1)}, u32[]{:S(2)}, u32[]{:S(2)}) async-start(f32[32,1,1152]{2,1,0:T(1,128)} %bitcast.1), calls=%async_computation | async-start | bytes 294912 | tf_op jit(solution)/shard_map/all_to_all | solution.py:393
  16.2 4.7 %collective-permute-start = (bf16[1,128,1024]{2,1,0:T(8,128)(2,1)S(1)}, bf16[1,128,1024]{2,1,0:T(8,128)(2,1)S(1)}, u32[]{:S(2)}, u32[]{:S(2)}) collective-permute-start(bf16[1,128,1024]{2,1,0:T(8,128)(2,1)S(1)} %copy-done), channel_id=1, source_target_pairs={{0,8},{8,0},{1,9},{9,1},{2,10},{10,2},{3,11},{11,3},{4,12},{12,4},... | collective-permute-start | bytes 786440 | tf_op jit(solution)/shard_map/ppermute | solution.py:374
  25.3 9.4 %copy-start.10 = (s32[16,2]{0,1:T(2,128)S(1)}, s32[16,2]{0,1:T(2,128)}, u32[]{:S(2)}) copy-start(s32[16,2]{0,1:T(2,128)} %param.17) | copy-start | bytes 388
  25.3 9.5 %copy-start.9 = (f32[8,16,2,16]{3,2,1,0:T(2,128)S(1)}, f32[8,16,2,16]{3,2,1,0:T(2,128)}, u32[]{:S(2)}) copy-start(f32[8,16,2,16]{3,2,1,0:T(2,128)} %param.15) | copy-start | bytes 49156
  25.3 14.8 %all-to-all-start.1 = ((bf16[32,32,128]{2,1,0:T(8,128)(2,1)}), bf16[32,32,128]{2,1,0:T(8,128)(2,1)S(1)}, u32[]{:S(2)}, u32[]{:S(2)}) async-start(bf16[32,32,128]{2,1,0:T(8,128)(2,1)} %reply_tiles.1), calls=%async_computation.1 | async-start | bytes 524288 | tf_op jit(solution)/shard_map/all_to_all | solution.py:417
  30.5 5.2 %collective-permute-start.1 = (f32[288,128]{1,0:T(8,128)S(1)}, f32[288,128]{1,0:T(8,128)S(1)}, u32[]{:S(2)}, u32[]{:S(2)}) collective-permute-start(f32[288,128]{1,0:T(8,128)S(1)} %bitcast.31), channel_id=1, source_target_pairs={{0,8},{8,0},{1,9},{9,1},{2,10},{10,2},{3,11},{11,3},{4,12},{12,4},... | collective-permute-start | bytes 442376 | tf_op jit(solution)/shard_map/ppermute | solution.py:374
  41.1 11.7 %copy-start.1 = (bf16[256,256]{1,0:T(8,128)(2,1)S(1)}, bf16[256,256]{1,0:T(8,128)(2,1)}, u32[]{:S(2)}) copy-start(bf16[256,256]{1,0:T(8,128)(2,1)} %constant.17.clone.cols_hi_ref) | copy-start | bytes 393220
  41.1 11.7 %copy-start.2 = (bf16[256,256]{1,0:T(8,128)(2,1)S(1)}, bf16[256,256]{1,0:T(8,128)(2,1)}, u32[]{:S(2)}) copy-start(bf16[256,256]{1,0:T(8,128)(2,1)} %constant.18.clone.cols_lo_ref) | copy-start | bytes 393220
  41.1 11.7 %copy-start.5 = (bf16[64,64]{1,0:T(8,128)(2,1)S(1)}, bf16[64,64]{1,0:T(8,128)(2,1)}, u32[]{:S(2)}) copy-start(bf16[64,64]{1,0:T(8,128)(2,1)} %constant.19.clone.rows_hi_ref) | copy-start | bytes 24580
  41.1 11.7 %copy-start.6 = (bf16[64,64]{1,0:T(8,128)(2,1)S(1)}, bf16[64,64]{1,0:T(8,128)(2,1)}, u32[]{:S(2)}) copy-start(bf16[64,64]{1,0:T(8,128)(2,1)} %constant.20.clone.rows_lo_ref) | copy-start | bytes 24580
  82.6 16.8 %all-to-all-start.5 = ((f32[16,8,128]{2,1,0:T(8,128)}), f32[16,8,128]{2,1,0:T(8,128)S(1)}, u32[]{:S(2)}, u32[]{:S(2)}) async-start(f32[16,8,128]{2,1,0:T(8,128)} %bitcast.10), calls=%async_computation.5 | async-start | bytes 131072 | tf_op jit(solution)/shard_map/all_to_all | solution.py:464

commit v9 on v8

--- a/solution.py
+++ b/solution.py
@@ -19,11 +19,12 @@
 BLD = 16
 TILES = 128
 SAMPLES = TIMES * CHANS
-RING3 = (4, 0, 5, 1, 6, 2, 7, 3)
-TURN3 = (1, 3, 5, 7, 0, 2, 4, 6)
+RING3 = (4, 0, 6, 2, 5, 1, 7, 3)
+TURN3 = (1, 5, 3, 7, 0, 4, 2, 6)
 RING5 = (0, 4, 1, 5, 2, 6, 3, 7)
 TURN5 = (0, 2, 4, 6, 1, 3, 5, 7)
 CHIPS1 = tuple(x * 8 + (z + 7) % 8 for x in range(4) for z in range(8))
+CHIPS6 = tuple(x * 8 + (8 - z) % 8 for x in range(4) for z in range(8))
 RING7 = tuple(2 * ((c + 4) % NCH) + 1 - k for c in range(NCH) for k in range(2))
 MSG1 = 9
 MSG3 = 56
@@ -354,6 +355,8 @@
         d, a = TURN5[i // 2], i % 2
         for e in range(2):
             s = pair_ref[i, e]
+            z = lax.rem(lax.div(s, 2), 8)
+            s = s - 2 * z + 2 * lax.rem(8 - z, 8)
             at = (a * 2 + e) * 8
             out_ref[s] = out_ref[s] + msg_ref[d, at : at + 8, :]
 
@@ -450,7 +453,7 @@
         compiler_params=params,
         name="sum_terms",
     )(station_pairs, got5)
-    got6 = lax.all_to_all(msg6.reshape(CHIPS, 16, 128), "xz", 0, 0, tiled=True)
+    got6 = lax.all_to_all(msg6.reshape(CHIPS, 16, 128), "xz", 0, 0, tiled=True, axis_index_groups=[CHIPS6])
 
     msg7 = pl.pallas_call(
         sum_chips,

time: 101 us -> 100 us (0.990)
  no operation moved by 1% of the time
where the time goes in v9:
time: 100 us; the launch traced here: 99.5 us
  starting transfers between devices  40 us (40%)
  blocking collectives  37.7 us (38%)
  waiting for transfers between devices  10.3 us (10%)
  Pallas kernels  8.56 us (9%)
  local copies, waits for them, and re-layouts  1.46 us (1%)
    all_to_all x1, blocking collectives, per_device(): lax.all_to_all(msg6.reshape(CHIPS, 16, 128), 'xz', 0, 0, tiled=True, axis...  14.6 us
    all_to_all x1, starting transfers between devices, per_device(): lax.all_to_all(msg1, 'xz', 0, 0, tiled=True, axis_index_groups=[CHIPS1])  13.9 us
    all_to_all x1, starting transfers between devices, per_device(): lax.all_to_all(msg7, ('ch', 'core'), 0, 0, tiled=True, axis_index_groups=...  13.6 us
    all_to_all x1, blocking collectives, per_device(): lax.all_to_all(msg3, 'ch', 0, 0, tiled=True, axis_index_groups=[RING3])  12 us
    all_to_all x1, blocking collectives, per_device(): lax.all_to_all(msg5, 'ch', 0, 0, tiled=True, axis_index_groups=[RING5])  11.2 us
    ppermute x2, starting transfers between devices, from_other_core(): return lax.ppermute(x, 'core', [(0, 1), (1, 0)])  7.35 us
    all_to_all x1, starting transfers between devices, per_device(): lax.all_to_all(tiles, 'xz', 0, 0, tiled=True).reshape(2 * NBL, 8, 128)  5.17 us
    all_to_all x1, waiting for transfers between devices, per_device(): lax.all_to_all(tiles, 'xz', 0, 0, tiled=True).reshape(2 * NBL, 8, 128)  4.47 us
  transfers between devices with their start and end apart: 5, of which 4 were waited for; matrix products, arithmetic and copies ran while one was open for 1% of the time, Pallas kernels for 2%

profile of v9, /device:TPU:1, one launch (start us, length us, event | category | flops | bytes accessed | tf_op | source)
XLA Modules:
  0.0 99.5 jit_solution(4622254009309535076)
XLA Ops:
  0.6 1.6 %send_requests.1 = f32[288,128]{1,0:T(8,128)} custom-call(s32[16]{0:T(128)} %bitcast.36, s32[16]{0:T(128)} %slot_hbm.1, f32[1,8,1024]{2,1,0:T(8,128)} %screen_hbm.1), custom_call_target="tpu_custom_call" | custom-call | tf_op jit(solution)/shard_map/send_requests/pallas_call | solution.py:381
  2.3 13.9 %all-to-all-start = ((f32[32,1,1152]{2,1,0:T(1,128)}), f32[32,1,1152]{2,1,0:T(1,128)S(1)}, u32[]{:S(2)}, u32[]{:S(2)}) async-start(f32[32,1,1152]{2,1,0:T(1,128)} %bitcast.1), calls=%async_computation | async-start | bytes 294912 | tf_op jit(solution)/shard_map/all_to_all | solution.py:396
  16.2 3.1 %collective-permute-start = (bf16[1,128,1024]{2,1,0:T(8,128)(2,1)S(1)}, bf16[1,128,1024]{2,1,0:T(8,128)(2,1)S(1)}, u32[]{:S(2)}, u32[]{:S(2)}) collective-permute-start(bf16[1,128,1024]{2,1,0:T(8,128)(2,1)S(1)} %copy-done), channel_id=1, source_target_pairs={{0,8},{8,0},{1,9},{9,1},{2,10},{10,2},{3,11},{11,3},{4,12},{12,4},... | collective-permute-start | bytes 786440 | tf_op jit(solution)/shard_map/ppermute | solution.py:377
  19.4 1.5 %phases.1 = (bf16[128,256]{1,0:T(8,128)(2,1)S(1)}, bf16[128,256]{1,0:T(8,128)(2,1)S(1)}, f32[2,32,256]{2,1,0:T(8,128)S(1)}, f32[2,32,256]{2,1,0:T(8,128)S(1)}, s32[16]{0:T(128)S(1)}) custom-call(s32[16]{0:T(128)S(1)} %bitcast.37, f32[2,16,16]{2,1,0:T(8,128)S(1)} %copy-done.4, f32[2,32,128]{2,1,0:T(8,128)S(1)} %copy-done.3, f32[8,256]{1,0:T(8,128)S(1)} %copy-done.7), custom_call_target="tpu_custom_call" | custom-call | tf_op jit(solution)/shard_map/phases/pallas_call | solution.py:402
  20.9 3.2 %all-to-all-done = f32[32,1,1152]{2,1,0:T(1,128)S(1)} async-done(((f32[32,1,1152]{2,1,0:T(1,128)}), f32[32,1,1152]{2,1,0:T(1,128)S(1)}, u32[]{:S(2)}, u32[]{:S(2)}) %all-to-all-start) | async-done | bytes 147488 | tf_op jit(solution)/shard_map/all_to_all | solution.py:396
  24.1 1.2 %reply_tiles.1 = bf16[32,32,128]{2,1,0:T(8,128)(2,1)} custom-call(f32[288,128]{1,0:T(8,128)S(1)} %bitcast.30, bf16[1,128,1024]{2,1,0:T(8,128)(2,1)S(1)} %copy-done, bf16[1,128,1024]{2,1,0:T(8,128)(2,1)S(1)} %collective-permute-done.other_ref, bf16[128,256]{1,0:T(8,128)(2,1)S(1)} %get-tuple-element.8._.wave_hi_ref), custom_call_target="tpu_custom_call" | custom-call | tf_op jit(solution)/shard_map/reply_tiles/pallas_call | solution.py:411
  25.3 5.2 %all-to-all-start.1 = ((bf16[32,32,128]{2,1,0:T(8,128)(2,1)}), bf16[32,32,128]{2,1,0:T(8,128)(2,1)S(1)}, u32[]{:S(2)}, u32[]{:S(2)}) async-start(bf16[32,32,128]{2,1,0:T(8,128)(2,1)} %reply_tiles.1), calls=%async_computation.1 | async-start | bytes 524288 | tf_op jit(solution)/shard_map/all_to_all | solution.py:420
  30.5 4.2 %collective-permute-start.1 = (f32[288,128]{1,0:T(8,128)S(1)}, f32[288,128]{1,0:T(8,128)S(1)}, u32[]{:S(2)}, u32[]{:S(2)}) collective-permute-start(f32[288,128]{1,0:T(8,128)S(1)} %bitcast.31), channel_id=1, source_target_pairs={{0,8},{8,0},{1,9},{9,1},{2,10},{10,2},{3,11},{11,3},{4,12},{12,4},... | collective-permute-start | bytes 442376 | tf_op jit(solution)/shard_map/ppermute | solution.py:377
  34.8 0.1 copy.30
  35.0 0.2 reshape.49
  35.2 0.5 collective-permute-done.1.other_ref
  35.7 4.5 %all-to-all-done.1 = bf16[32,32,128]{2,1,0:T(8,128)(2,1)S(1)} async-done(((bf16[32,32,128]{2,1,0:T(8,128)(2,1)}), bf16[32,32,128]{2,1,0:T(8,128)(2,1)S(1)}, u32[]{:S(2)}, u32[]{:S(2)}) %all-to-all-start.1) | async-done | bytes 262176 | tf_op jit(solution)/shard_map/all_to_all | solution.py:420
  40.2 0.9 send_baselines.1
  41.1 12.0 %all_to_all.30.msg_ref = f32[8,56,128]{2,1,0:T(8,128)S(1)} all-to-all(f32[8,56,128]{2,1,0:T(8,128)S(1)} %send_baselines.1), channel_id=1, replica_groups={{4,0,6,2,5,1,7,3},{12,8,14,10,13,9,15,11},{20,16,22,18,21,17,23,19},{28..., dimensions={0} | all-to-all | bytes 458752 | tf_op jit(solution)/shard_map/all_to_all | solution.py:432
  53.1 1.8 %calibrate.1 = f32[4,2,40,128]{3,2,1,0:T(8,128)S(1)} custom-call(f32[8,56,128]{2,1,0:T(8,128)S(1)} %all_to_all.30.msg_ref, bf16[128,256]{1,0:T(8,128)(2,1)S(1)} %get-tuple-element.8._.wave_hi_ref, bf16[128,256]{1,0:T(8,128)(2,1)S(1)} %get-tuple-element.9.wave_lo_ref, f32[2,32,256]{2,1,0:T(8,128)S(1)} %get-tuple-element.10.cos_ref, ...), custom_call_target="tpu_custom_call" | custom-call | tf_op jit(solution)/shard_map/calibrate/pallas_call | solution.py:434
  54.9 11.2 %all_to_all.31.msg_ref = f32[8,40,128]{2,1,0:T(8,128)S(1)} all-to-all(f32[8,40,128]{2,1,0:T(8,128)S(1)} %bitcast.35), channel_id=1, replica_groups={{0,4,1,5,2,6,3,7},{8,12,9,13,10,14,11,15},{16,20,17,21,18,22,19,23},{24..., dimensions={0} | all-to-all | bytes 327680 | tf_op jit(solution)/shard_map/all_to_all | solution.py:443
  66.1 0.9 sum_terms.1
  67.0 14.6 %all_to_all.32.msg_ref = f32[32,16,128]{2,1,0:T(8,128)S(1)} all-to-all(f32[32,16,128]{2,1,0:T(8,128)S(1)} %bitcast.33), channel_id=1, replica_groups={{0,112,96,80,64,48,32,16,128,240,224,208,192,176,160,144,256,368,352,33..., dimensions={0} | all-to-all | bytes 524288 | tf_op jit(solution)/shard_map/all_to_all | solution.py:456
  81.6 0.7 sum_chips.1
  82.2 13.6 %all-to-all-start.5 = ((f32[16,8,128]{2,1,0:T(8,128)}), f32[16,8,128]{2,1,0:T(8,128)S(1)}, u32[]{:S(2)}, u32[]{:S(2)}) async-start(f32[16,8,128]{2,1,0:T(8,128)} %bitcast.10), calls=%async_computation.5 | async-start | bytes 131072 | tf_op jit(solution)/shard_map/all_to_all | solution.py:467
  95.8 0.1 reshape.51
  96.0 0.8 copy.37
  96.7 2.1 %all-to-all-done.5 = f32[16,8,128]{2,1,0:T(8,128)S(1)} async-done(((f32[16,8,128]{2,1,0:T(8,128)}), f32[16,8,128]{2,1,0:T(8,128)S(1)}, u32[]{:S(2)}, u32[]{:S(2)}) %all-to-all-start.5) | async-done | bytes 65568 | tf_op jit(solution)/shard_map/all_to_all | solution.py:467
  98.9 0.6 fusion.1
  (28 shorter events, 0.3 us)
Async XLA Ops:
  0.6 15.5 %copy-start = (bf16[1,128,1024]{2,1,0:T(8,128)(2,1)S(1)}, bf16[1,128,1024]{2,1,0:T(8,128)(2,1)}, u32[]{:S(2)}) copy-start(bf16[1,128,1024]{2,1,0:T(8,128)(2,1)} %grid_ref.1) | copy-start | bytes 786436
  2.2 17.1 %copy-start.3 = (f32[2,32,128]{2,1,0:T(8,128)S(1)}, f32[2,32,128]{2,1,0:T(8,128)}, u32[]{:S(2)}) copy-start(f32[2,32,128]{2,1,0:T(8,128)} %constant.15.clone.places_ref) | copy-start | bytes 98308
  2.2 17.1 %copy-start.4 = (f32[2,16,16]{2,1,0:T(8,128)S(1)}, f32[2,16,16]{2,1,0:T(8,128)}, u32[]{:S(2)}) copy-start(f32[2,16,16]{2,1,0:T(8,128)} %uv_ref.1) | copy-start | bytes 6148
  2.2 17.1 %copy-start.7 = (f32[8,256]{1,0:T(8,128)S(1)}, f32[8,256]{1,0:T(8,128)}, u32[]{:S(2)}) copy-start(f32[8,256]{1,0:T(8,128)} %constant.16.clone.factor_ref) | copy-start | bytes 24580
  2.2 17.1 %copy-start.8 = (s32[16,1]{0,1:T(1,128)S(1)}, s32[16,1]{0,1:T(1,128)}, u32[]{:S(2)}) copy-start(s32[16,1]{0,1:T(1,128)} %param.18) | copy-start | bytes 196
  2.3 21.8 %all-to-all-start = ((f32[32,1,1152]{2,1,0:T(1,128)}), f32[32,1,1152]{2,1,0:T(1,128)S(1)}, u32[]{:S(2)}, u32[]{:S(2)}) async-start(f32[32,1,1152]{2,1,0:T(1,128)} %bitcast.1), calls=%async_computation | async-start | bytes 294912 | tf_op jit(solution)/shard_map/all_to_all | solution.py:396
  16.2 4.7 %collective-permute-start = (bf16[1,128,1024]{2,1,0:T(8,128)(2,1)S(1)}, bf16[1,128,1024]{2,1,0:T(8,128)(2,1)S(1)}, u32[]{:S(2)}, u32[]{:S(2)}) collective-permute-start(bf16[1,128,1024]{2,1,0:T(8,128)(2,1)S(1)} %copy-done), channel_id=1, source_target_pairs={{0,8},{8,0},{1,9},{9,1},{2,10},{10,2},{3,11},{11,3},{4,12},{12,4},... | collective-permute-start | bytes 786440 | tf_op jit(solution)/shard_map/ppermute | solution.py:377
  25.3 9.4 %copy-start.10 = (s32[16,2]{0,1:T(2,128)S(1)}, s32[16,2]{0,1:T(2,128)}, u32[]{:S(2)}) copy-start(s32[16,2]{0,1:T(2,128)} %param.17) | copy-start | bytes 388
  25.3 9.5 %copy-start.9 = (f32[8,16,2,16]{3,2,1,0:T(2,128)S(1)}, f32[8,16,2,16]{3,2,1,0:T(2,128)}, u32[]{:S(2)}) copy-start(f32[8,16,2,16]{3,2,1,0:T(2,128)} %param.15) | copy-start | bytes 49156
  25.3 14.8 %all-to-all-start.1 = ((bf16[32,32,128]{2,1,0:T(8,128)(2,1)}), bf16[32,32,128]{2,1,0:T(8,128)(2,1)S(1)}, u32[]{:S(2)}, u32[]{:S(2)}) async-start(bf16[32,32,128]{2,1,0:T(8,128)(2,1)} %reply_tiles.1), calls=%async_computation.1 | async-start | bytes 524288 | tf_op jit(solution)/shard_map/all_to_all | solution.py:420
  30.5 5.2 %collective-permute-start.1 = (f32[288,128]{1,0:T(8,128)S(1)}, f32[288,128]{1,0:T(8,128)S(1)}, u32[]{:S(2)}, u32[]{:S(2)}) collective-permute-start(f32[288,128]{1,0:T(8,128)S(1)} %bitcast.31), channel_id=1, source_target_pairs={{0,8},{8,0},{1,9},{9,1},{2,10},{10,2},{3,11},{11,3},{4,12},{12,4},... | collective-permute-start | bytes 442376 | tf_op jit(solution)/shard_map/ppermute | solution.py:377
  41.1 12.0 %copy-start.1 = (bf16[256,256]{1,0:T(8,128)(2,1)S(1)}, bf16[256,256]{1,0:T(8,128)(2,1)}, u32[]{:S(2)}) copy-start(bf16[256,256]{1,0:T(8,128)(2,1)} %constant.17.clone.cols_hi_ref) | copy-start | bytes 393220
  41.1 12.0 %copy-start.2 = (bf16[256,256]{1,0:T(8,128)(2,1)S(1)}, bf16[256,256]{1,0:T(8,128)(2,1)}, u32[]{:S(2)}) copy-start(bf16[256,256]{1,0:T(8,128)(2,1)} %constant.18.clone.cols_lo_ref) | copy-start | bytes 393220
  41.1 12.0 %copy-start.5 = (bf16[64,64]{1,0:T(8,128)(2,1)S(1)}, bf16[64,64]{1,0:T(8,128)(2,1)}, u32[]{:S(2)}) copy-start(bf16[64,64]{1,0:T(8,128)(2,1)} %constant.19.clone.rows_hi_ref) | copy-start | bytes 24580
  41.1 12.0 %copy-start.6 = (bf16[64,64]{1,0:T(8,128)(2,1)S(1)}, bf16[64,64]{1,0:T(8,128)(2,1)}, u32[]{:S(2)}) copy-start(bf16[64,64]{1,0:T(8,128)(2,1)} %constant.20.clone.rows_lo_ref) | copy-start | bytes 24580
  82.2 16.6 %all-to-all-start.5 = ((f32[16,8,128]{2,1,0:T(8,128)}), f32[16,8,128]{2,1,0:T(8,128)S(1)}, u32[]{:S(2)}, u32[]{:S(2)}) async-start(f32[16,8,128]{2,1,0:T(8,128)} %bitcast.10), calls=%async_computation.5 | async-start | bytes 131072 | tf_op jit(solution)/shard_map/all_to_all | solution.py:467

commit v10 on v9

--- a/solution.py
+++ b/solution.py
@@ -24,6 +24,7 @@
 RING5 = (0, 4, 1, 5, 2, 6, 3, 7)
 TURN5 = (0, 2, 4, 6, 1, 3, 5, 7)
 CHIPS1 = tuple(x * 8 + (z + 7) % 8 for x in range(4) for z in range(8))
+CHIPS2 = tuple(x * 8 + z for x in (0, 3, 2, 1) for z in range(8))
 CHIPS6 = tuple(x * 8 + (8 - z) % 8 for x in range(4) for z in range(8))
 RING7 = tuple(2 * ((c + 4) % NCH) + 1 - k for c in range(NCH) for k in range(2))
 MSG1 = 9
@@ -130,7 +131,7 @@
 def reply_tiles(msg_ref, grid_ref, other_ref, _, out_ref, scr_ref):
     core = lax.axis_index("core")
     req = msg_ref[pl.ds(8, CHIPS, stride=MSG1), :].astype(jnp.int32)
-    req = jnp.concatenate([pltpu.roll(req[x : x + 8], 7, 0) for x in range(0, CHIPS, 8)], axis=0)
+    req = jnp.concatenate([pltpu.roll(req[x : x + 8], 7, 0) for x in (0, 24, 16, 8)], axis=0)
     lanes = lax.broadcasted_iota(jnp.int32, (CHIPS, 2 * TILES), 1) + 1
     picks = []
     for k in range(4):
@@ -220,7 +221,8 @@
         rank = jnp.int32(0)
         for e in range(i):
             rank = jnp.where(owners[e] == owners[i], 1, rank)
-        at_ref[i] = owners[i] * 2 + rank
+        x = lax.div(owners[i], 16)
+        at_ref[i] = (owners[i] - 16 * x + 16 * lax.rem(4 - x, 4)) * 2 + rank
 
     mine = lax.axis_index("ch") * 2
     sub = lax.broadcasted_iota(jnp.int32, (BLD, TIMES), 0)
@@ -417,7 +419,7 @@
         compiler_params=params,
         name="reply_tiles",
     )(got1, model_grid, other_grid, waves[0])
-    got2 = lax.all_to_all(tiles, "xz", 0, 0, tiled=True).reshape(2 * NBL, 8, 128)
+    got2 = lax.all_to_all(tiles, "xz", 0, 0, tiled=True, axis_index_groups=[CHIPS2]).reshape(2 * NBL, 8, 128)
     seen = observed.reshape(8, TIMES, 2, NCH, 2).transpose(3, 0, 4, 2, 1).reshape(NCH, 8, 64)
     seen = jnp.pad(seen, ((0, 0), (0, 0), (0, 64)))
     msg3 = pl.pallas_call(

time: 100 us -> 99.8 us (level)
  no operation moved by 1% of the time
where the time goes in v10:
time: 99.8 us; the launch traced here: 99.3 us
  starting transfers between devices  39.8 us (40%)
  blocking collectives  37.6 us (38%)
  waiting for transfers between devices  10.3 us (10%)
  Pallas kernels  8.64 us (9%)
  local copies, waits for them, and re-layouts  1.46 us (1%)
    all_to_all x1, blocking collectives, per_device(): lax.all_to_all(msg6.reshape(CHIPS, 16, 128), 'xz', 0, 0, tiled=True, axis...  14.5 us
    all_to_all x1, starting transfers between devices, per_device(): lax.all_to_all(msg1, 'xz', 0, 0, tiled=True, axis_index_groups=[CHIPS1])  13.9 us
    all_to_all x1, starting transfers between devices, per_device(): lax.all_to_all(msg7, ('ch', 'core'), 0, 0, tiled=True, axis_index_groups=...  13.3 us
    all_to_all x1, blocking collectives, per_device(): lax.all_to_all(msg3, 'ch', 0, 0, tiled=True, axis_index_groups=[RING3])  12 us
    all_to_all x1, blocking collectives, per_device(): lax.all_to_all(msg5, 'ch', 0, 0, tiled=True, axis_index_groups=[RING5])  11.2 us
    ppermute x2, starting transfers between devices, from_other_core(): return lax.ppermute(x, 'core', [(0, 1), (1, 0)])  7.35 us
    all_to_all x1, starting transfers between devices, per_device(): lax.all_to_all(tiles, 'xz', 0, 0, tiled=True, axis_index_groups=[CHIPS2])  5.17 us
    all_to_all x1, waiting for transfers between devices, per_device(): lax.all_to_all(tiles, 'xz', 0, 0, tiled=True, axis_index_groups=[CHIPS2])  4.55 us
  transfers between devices with their start and end apart: 5, of which 4 were waited for; matrix products, arithmetic and copies ran while one was open for 1% of the time, Pallas kernels for 2%

profile of v10, /device:TPU:1, one launch (start us, length us, event | category | flops | bytes accessed | tf_op | source)
XLA Modules:
  0.0 99.3 jit_solution(8181887885944441165)
XLA Ops:
  0.6 1.6 %send_requests.1 = f32[288,128]{1,0:T(8,128)} custom-call(s32[16]{0:T(128)} %bitcast.36, s32[16]{0:T(128)} %slot_hbm.1, f32[1,8,1024]{2,1,0:T(8,128)} %screen_hbm.1), custom_call_target="tpu_custom_call" | custom-call | tf_op jit(solution)/shard_map/send_requests/pallas_call | solution.py:383
  2.3 13.9 %all-to-all-start = ((f32[32,1,1152]{2,1,0:T(1,128)}), f32[32,1,1152]{2,1,0:T(1,128)S(1)}, u32[]{:S(2)}, u32[]{:S(2)}) async-start(f32[32,1,1152]{2,1,0:T(1,128)} %bitcast.1), calls=%async_computation | async-start | bytes 294912 | tf_op jit(solution)/shard_map/all_to_all | solution.py:398
  16.2 3.1 %collective-permute-start = (bf16[1,128,1024]{2,1,0:T(8,128)(2,1)S(1)}, bf16[1,128,1024]{2,1,0:T(8,128)(2,1)S(1)}, u32[]{:S(2)}, u32[]{:S(2)}) collective-permute-start(bf16[1,128,1024]{2,1,0:T(8,128)(2,1)S(1)} %copy-done), channel_id=1, source_target_pairs={{0,8},{8,0},{1,9},{9,1},{2,10},{10,2},{3,11},{11,3},{4,12},{12,4},... | collective-permute-start | bytes 786440 | tf_op jit(solution)/shard_map/ppermute | solution.py:379
  19.4 1.6 %phases.1 = (bf16[128,256]{1,0:T(8,128)(2,1)S(1)}, bf16[128,256]{1,0:T(8,128)(2,1)S(1)}, f32[2,32,256]{2,1,0:T(8,128)S(1)}, f32[2,32,256]{2,1,0:T(8,128)S(1)}, s32[16]{0:T(128)S(1)}) custom-call(s32[16]{0:T(128)S(1)} %bitcast.37, f32[2,16,16]{2,1,0:T(8,128)S(1)} %copy-done.4, f32[2,32,128]{2,1,0:T(8,128)S(1)} %copy-done.3, f32[8,256]{1,0:T(8,128)S(1)} %copy-done.7), custom_call_target="tpu_custom_call" | custom-call | tf_op jit(solution)/shard_map/phases/pallas_call | solution.py:404
  21.0 3.1 %all-to-all-done = f32[32,1,1152]{2,1,0:T(1,128)S(1)} async-done(((f32[32,1,1152]{2,1,0:T(1,128)}), f32[32,1,1152]{2,1,0:T(1,128)S(1)}, u32[]{:S(2)}, u32[]{:S(2)}) %all-to-all-start) | async-done | bytes 147488 | tf_op jit(solution)/shard_map/all_to_all | solution.py:398
  24.1 1.2 %reply_tiles.1 = bf16[32,32,128]{2,1,0:T(8,128)(2,1)} custom-call(f32[288,128]{1,0:T(8,128)S(1)} %bitcast.30, bf16[1,128,1024]{2,1,0:T(8,128)(2,1)S(1)} %copy-done, bf16[1,128,1024]{2,1,0:T(8,128)(2,1)S(1)} %collective-permute-done.other_ref, bf16[128,256]{1,0:T(8,128)(2,1)S(1)} %get-tuple-element.8._.wave_hi_ref), custom_call_target="tpu_custom_call" | custom-call | tf_op jit(solution)/shard_map/reply_tiles/pallas_call | solution.py:413
  25.3 5.2 %all-to-all-start.1 = ((bf16[32,32,128]{2,1,0:T(8,128)(2,1)}), bf16[32,32,128]{2,1,0:T(8,128)(2,1)S(1)}, u32[]{:S(2)}, u32[]{:S(2)}) async-start(bf16[32,32,128]{2,1,0:T(8,128)(2,1)} %reply_tiles.1), calls=%async_computation.1 | async-start | bytes 524288 | tf_op jit(solution)/shard_map/all_to_all | solution.py:422
  30.5 4.2 %collective-permute-start.1 = (f32[288,128]{1,0:T(8,128)S(1)}, f32[288,128]{1,0:T(8,128)S(1)}, u32[]{:S(2)}, u32[]{:S(2)}) collective-permute-start(f32[288,128]{1,0:T(8,128)S(1)} %bitcast.31), channel_id=1, source_target_pairs={{0,8},{8,0},{1,9},{9,1},{2,10},{10,2},{3,11},{11,3},{4,12},{12,4},... | collective-permute-start | bytes 442376 | tf_op jit(solution)/shard_map/ppermute | solution.py:379
  34.8 0.1 copy.30
  35.0 0.2 reshape.49
  35.2 0.5 collective-permute-done.1.other_ref
  35.7 4.5 %all-to-all-done.1 = bf16[32,32,128]{2,1,0:T(8,128)(2,1)S(1)} async-done(((bf16[32,32,128]{2,1,0:T(8,128)(2,1)}), bf16[32,32,128]{2,1,0:T(8,128)(2,1)S(1)}, u32[]{:S(2)}, u32[]{:S(2)}) %all-to-all-start.1) | async-done | bytes 262176 | tf_op jit(solution)/shard_map/all_to_all | solution.py:422
  40.2 0.9 send_baselines.1
  41.2 12.0 %all_to_all.30.msg_ref = f32[8,56,128]{2,1,0:T(8,128)S(1)} all-to-all(f32[8,56,128]{2,1,0:T(8,128)S(1)} %send_baselines.1), channel_id=1, replica_groups={{4,0,6,2,5,1,7,3},{12,8,14,10,13,9,15,11},{20,16,22,18,21,17,23,19},{28..., dimensions={0} | all-to-all | bytes 458752 | tf_op jit(solution)/shard_map/all_to_all | solution.py:434
  53.2 1.8 %calibrate.1 = f32[4,2,40,128]{3,2,1,0:T(8,128)S(1)} custom-call(f32[8,56,128]{2,1,0:T(8,128)S(1)} %all_to_all.30.msg_ref, bf16[128,256]{1,0:T(8,128)(2,1)S(1)} %get-tuple-element.8._.wave_hi_ref, bf16[128,256]{1,0:T(8,128)(2,1)S(1)} %get-tuple-element.9.wave_lo_ref, f32[2,32,256]{2,1,0:T(8,128)S(1)} %get-tuple-element.10.cos_ref, ...), custom_call_target="tpu_custom_call" | custom-call | tf_op jit(solution)/shard_map/calibrate/pallas_call | solution.py:436
  55.0 11.2 %all_to_all.31.msg_ref = f32[8,40,128]{2,1,0:T(8,128)S(1)} all-to-all(f32[8,40,128]{2,1,0:T(8,128)S(1)} %bitcast.35), channel_id=1, replica_groups={{0,4,1,5,2,6,3,7},{8,12,9,13,10,14,11,15},{16,20,17,21,18,22,19,23},{24..., dimensions={0} | all-to-all | bytes 327680 | tf_op jit(solution)/shard_map/all_to_all | solution.py:445
  66.2 0.9 sum_terms.1
  67.0 14.5 %all_to_all.32.msg_ref = f32[32,16,128]{2,1,0:T(8,128)S(1)} all-to-all(f32[32,16,128]{2,1,0:T(8,128)S(1)} %bitcast.33), channel_id=1, replica_groups={{0,112,96,80,64,48,32,16,128,240,224,208,192,176,160,144,256,368,352,33..., dimensions={0} | all-to-all | bytes 524288 | tf_op jit(solution)/shard_map/all_to_all | solution.py:458
  81.6 0.7 sum_chips.1
  82.2 13.3 %all-to-all-start.5 = ((f32[16,8,128]{2,1,0:T(8,128)}), f32[16,8,128]{2,1,0:T(8,128)S(1)}, u32[]{:S(2)}, u32[]{:S(2)}) async-start(f32[16,8,128]{2,1,0:T(8,128)} %bitcast.10), calls=%async_computation.5 | async-start | bytes 131072 | tf_op jit(solution)/shard_map/all_to_all | solution.py:469
  95.6 0.1 reshape.51
  95.8 0.8 copy.37
  96.5 2.1 %all-to-all-done.5 = f32[16,8,128]{2,1,0:T(8,128)S(1)} async-done(((f32[16,8,128]{2,1,0:T(8,128)}), f32[16,8,128]{2,1,0:T(8,128)S(1)}, u32[]{:S(2)}, u32[]{:S(2)}) %all-to-all-start.5) | async-done | bytes 65568 | tf_op jit(solution)/shard_map/all_to_all | solution.py:469
  98.6 0.6 fusion.1
  (28 shorter events, 0.3 us)
Async XLA Ops:
  0.6 15.5 %copy-start = (bf16[1,128,1024]{2,1,0:T(8,128)(2,1)S(1)}, bf16[1,128,1024]{2,1,0:T(8,128)(2,1)}, u32[]{:S(2)}) copy-start(bf16[1,128,1024]{2,1,0:T(8,128)(2,1)} %grid_ref.1) | copy-start | bytes 786436
  2.2 17.1 %copy-start.3 = (f32[2,32,128]{2,1,0:T(8,128)S(1)}, f32[2,32,128]{2,1,0:T(8,128)}, u32[]{:S(2)}) copy-start(f32[2,32,128]{2,1,0:T(8,128)} %constant.15.clone.places_ref) | copy-start | bytes 98308
  2.2 17.1 %copy-start.4 = (f32[2,16,16]{2,1,0:T(8,128)S(1)}, f32[2,16,16]{2,1,0:T(8,128)}, u32[]{:S(2)}) copy-start(f32[2,16,16]{2,1,0:T(8,128)} %uv_ref.1) | copy-start | bytes 6148
  2.2 17.1 %copy-start.7 = (f32[8,256]{1,0:T(8,128)S(1)}, f32[8,256]{1,0:T(8,128)}, u32[]{:S(2)}) copy-start(f32[8,256]{1,0:T(8,128)} %constant.16.clone.factor_ref) | copy-start | bytes 24580
  2.2 17.1 %copy-start.8 = (s32[16,1]{0,1:T(1,128)S(1)}, s32[16,1]{0,1:T(1,128)}, u32[]{:S(2)}) copy-start(s32[16,1]{0,1:T(1,128)} %param.18) | copy-start | bytes 196
  2.3 21.8 %all-to-all-start = ((f32[32,1,1152]{2,1,0:T(1,128)}), f32[32,1,1152]{2,1,0:T(1,128)S(1)}, u32[]{:S(2)}, u32[]{:S(2)}) async-start(f32[32,1,1152]{2,1,0:T(1,128)} %bitcast.1), calls=%async_computation | async-start | bytes 294912 | tf_op jit(solution)/shard_map/all_to_all | solution.py:398
  16.2 4.8 %collective-permute-start = (bf16[1,128,1024]{2,1,0:T(8,128)(2,1)S(1)}, bf16[1,128,1024]{2,1,0:T(8,128)(2,1)S(1)}, u32[]{:S(2)}, u32[]{:S(2)}) collective-permute-start(bf16[1,128,1024]{2,1,0:T(8,128)(2,1)S(1)} %copy-done), channel_id=1, source_target_pairs={{0,8},{8,0},{1,9},{9,1},{2,10},{10,2},{3,11},{11,3},{4,12},{12,4},... | collective-permute-start | bytes 786440 | tf_op jit(solution)/shard_map/ppermute | solution.py:379
  25.3 9.4 %copy-start.10 = (s32[16,2]{0,1:T(2,128)S(1)}, s32[16,2]{0,1:T(2,128)}, u32[]{:S(2)}) copy-start(s32[16,2]{0,1:T(2,128)} %param.17) | copy-start | bytes 388
  25.3 9.5 %copy-start.9 = (f32[8,16,2,16]{3,2,1,0:T(2,128)S(1)}, f32[8,16,2,16]{3,2,1,0:T(2,128)}, u32[]{:S(2)}) copy-start(f32[8,16,2,16]{3,2,1,0:T(2,128)} %param.15) | copy-start | bytes 49156
  25.3 14.9 %all-to-all-start.1 = ((bf16[32,32,128]{2,1,0:T(8,128)(2,1)}), bf16[32,32,128]{2,1,0:T(8,128)(2,1)S(1)}, u32[]{:S(2)}, u32[]{:S(2)}) async-start(bf16[32,32,128]{2,1,0:T(8,128)(2,1)} %reply_tiles.1), calls=%async_computation.1 | async-start | bytes 524288 | tf_op jit(solution)/shard_map/all_to_all | solution.py:422
  30.5 5.2 %collective-permute-start.1 = (f32[288,128]{1,0:T(8,128)S(1)}, f32[288,128]{1,0:T(8,128)S(1)}, u32[]{:S(2)}, u32[]{:S(2)}) collective-permute-start(f32[288,128]{1,0:T(8,128)S(1)} %bitcast.31), channel_id=1, source_target_pairs={{0,8},{8,0},{1,9},{9,1},{2,10},{10,2},{3,11},{11,3},{4,12},{12,4},... | collective-permute-start | bytes 442376 | tf_op jit(solution)/shard_map/ppermute | solution.py:379
  41.2 12.0 %copy-start.1 = (bf16[256,256]{1,0:T(8,128)(2,1)S(1)}, bf16[256,256]{1,0:T(8,128)(2,1)}, u32[]{:S(2)}) copy-start(bf16[256,256]{1,0:T(8,128)(2,1)} %constant.17.clone.cols_hi_ref) | copy-start | bytes 393220
  41.2 12.0 %copy-start.2 = (bf16[256,256]{1,0:T(8,128)(2,1)S(1)}, bf16[256,256]{1,0:T(8,128)(2,1)}, u32[]{:S(2)}) copy-start(bf16[256,256]{1,0:T(8,128)(2,1)} %constant.18.clone.cols_lo_ref) | copy-start | bytes 393220
  41.2 12.0 %copy-start.5 = (bf16[64,64]{1,0:T(8,128)(2,1)S(1)}, bf16[64,64]{1,0:T(8,128)(2,1)}, u32[]{:S(2)}) copy-start(bf16[64,64]{1,0:T(8,128)(2,1)} %constant.19.clone.rows_hi_ref) | copy-start | bytes 24580
  41.2 12.0 %copy-start.6 = (bf16[64,64]{1,0:T(8,128)(2,1)S(1)}, bf16[64,64]{1,0:T(8,128)(2,1)}, u32[]{:S(2)}) copy-start(bf16[64,64]{1,0:T(8,128)(2,1)} %constant.20.clone.rows_lo_ref) | copy-start | bytes 24580
  82.2 16.4 %all-to-all-start.5 = ((f32[16,8,128]{2,1,0:T(8,128)}), f32[16,8,128]{2,1,0:T(8,128)S(1)}, u32[]{:S(2)}, u32[]{:S(2)}) async-start(f32[16,8,128]{2,1,0:T(8,128)} %bitcast.10), calls=%async_computation.5 | async-start | bytes 131072 | tf_op jit(solution)/shard_map/all_to_all | solution.py:469
